TPU v7x, 32 devices: a whole 2x2x4 slice. The times are simulated.
32 devices in a mesh: batch: 16 (over z, y, core), seq: 2 (over x).
Axes of the slice: x: 2, y: 2, z: 4, core: 2. Of those that a mesh axis runs over, the one named last changes fastest.
Arguments:
- block_in: bfloat16 [16, 1024, 1024], P('batch', 'seq'), may hold values from -2.5 to 2.5
- conditioning: bfloat16 [16, 1024], P('batch'), may hold values from -2.5 to 2.5
- cotangent: bfloat16 [16, 1024, 1024], P('batch', 'seq'), may hold values from -2.5 to 2.5
- ada_weight: bfloat16 [1024, 6144], P(('batch', 'seq')), may hold values from -0.25 to 0.25
- ada_bias: bfloat16 [6144], P(('batch', 'seq')), may hold values from -1.25 to 1.25
- qkv_weight: bfloat16 [1024, 3072], P(('batch', 'seq')), may hold values from -0.1875 to 0.1875
- qv_bias: bfloat16 [2048], P(('batch', 'seq')), may hold values from -1.25 to 1.25
- out_weight: bfloat16 [1024, 1024], P(('batch', 'seq')), may hold values from -1.5 to 1.5
- out_bias: bfloat16 [1024], P(('batch', 'seq')), may hold values from -1.25 to 1.25
- up_weight: bfloat16 [1024, 4096], P(('batch', 'seq')), may hold values from -0.1875 to 0.1875
- up_bias: bfloat16 [4096], P(('batch', 'seq')), may hold values from -1.25 to 1.25
- down_weight: bfloat16 [4096, 1024], P(('batch', 'seq')), may hold values from -0.09375 to 0.09375
- down_bias: bfloat16 [1024], P(('batch', 'seq')), may hold values from -1.25 to 1.25
Outputs:
- block_out: bfloat16 [16, 1024, 1024], P('batch', 'seq')
- input_grad: bfloat16 [16, 1024, 1024], P('batch', 'seq')
- cond_grad: bfloat16 [16, 1024], P('batch')
- ada_weight_grad: float32 [1024, 6144], P(('batch', 'seq'))
- ada_bias_grad: float32 [6144], P(('batch', 'seq'))
- qkv_weight_grad: float32 [1024, 3072], P(('batch', 'seq'))
- qv_bias_grad: float32 [2048], P(('batch', 'seq'))
- out_weight_grad: float32 [1024, 1024], P(('batch', 'seq'))
- out_bias_grad: float32 [1024], P(('batch', 'seq'))
- up_weight_grad: float32 [1024, 4096], P(('batch', 'seq'))
- up_bias_grad: float32 [4096], P(('batch', 'seq'))
- down_weight_grad: float32 [4096, 1024], P(('batch', 'seq'))
- down_bias_grad: float32 [1024], P(('batch', 'seq'))
All inputs are finite; a program needn't handle non-finite values.
Results may differ from a plain program's by a relative error of at most 0.015.
The roundings to bfloat16 on the way count: a program that leaves them out, or rounds other values in their place, can miss the bound.
Values may be sent and summed in bfloat16 or wider, within the bound.
No kernel may reach another device: no remote copies, remote signals or barrier semaphores. Data moves between devices by JAX's collectives and lax.ppermute only.
A program may use at most 256 MiB of HBM per device.

v0:
```python
from functools import partial

import jax
import jax.numpy as jnp
from jax import lax
from jax.sharding import PartitionSpec as P

HEAD_DIM = 64


HIGHEST = lax.Precision.HIGHEST
EPSILON = 1e-06


def modulate(values, shifts, scales):
    average = jnp.mean(values, axis=-1, keepdims=True)
    centered = values - average
    variance = jnp.mean(centered * centered, axis=-1, keepdims=True)
    return centered * lax.rsqrt(variance + EPSILON) * (1.0 + scales) + shifts


def outer_sum(left, right):
    return lax.dot_general(
        left, right, (((0,), (0,)), ((), ())), preferred_element_type=jnp.float32
    )


def back_dot(grads, weight):
    return lax.dot_general(
        grads, weight, (((1,), (1,)), ((), ())), preferred_element_type=jnp.float32
    )


def split_heads(values):
    return values.reshape(values.shape[0], -1, HEAD_DIM)


def attend(items):
    queries, key_part, value_part = items
    query_heads = split_heads(queries)
    scores = jnp.einsum(
        "qhd,khd->hqk", query_heads, split_heads(key_part), preferred_element_type=jnp.float32
    ) * HEAD_DIM ** (-0.5)
    row_max = jnp.max(scores, axis=-1, keepdims=True)
    exp_scores = jnp.exp(scores - row_max)
    row_total = jnp.sum(exp_scores, axis=-1, keepdims=True)
    probs = exp_scores / row_total
    logsum = (row_max + jnp.log(row_total))[..., 0]
    attended = jnp.einsum(
        "hqk,khd->qhd",
        probs.astype(jnp.bfloat16),
        split_heads(value_part),
        preferred_element_type=jnp.float32,
    )
    return (attended.reshape(queries.shape[0], -1).astype(jnp.bfloat16), logsum)


def attend_back(items):
    queries, key_part, value_part, logsum, attended_grad = items
    query_heads = split_heads(queries)
    key_heads = split_heads(key_part)
    grad_heads = split_heads(attended_grad)
    scores = jnp.einsum(
        "qhd,khd->hqk", query_heads, key_heads, preferred_element_type=jnp.float32
    ) * HEAD_DIM ** (-0.5)
    probs = jnp.exp(scores - logsum[..., None])
    prob_grad = jnp.einsum(
        "qhd,khd->hqk", grad_heads, split_heads(value_part), preferred_element_type=jnp.float32
    )
    inner = jnp.sum(probs * prob_grad, axis=-1, keepdims=True)
    score_grad = (probs * (prob_grad - inner)).astype(jnp.bfloat16)
    factor = HEAD_DIM ** (-0.5)
    query_grad = (
        jnp.einsum("hqk,khd->qhd", score_grad, key_heads, preferred_element_type=jnp.float32)
        * factor
    )
    key_grad = (
        jnp.einsum("hqk,qhd->khd", score_grad, query_heads, preferred_element_type=jnp.float32)
        * factor
    )
    value_grad = jnp.einsum(
        "hqk,qhd->khd", probs.astype(jnp.bfloat16), grad_heads, preferred_element_type=jnp.float32
    )
    return (
        query_grad.reshape(queries.shape[0], -1),
        key_grad.reshape(key_part.shape[0], -1),
        value_grad.reshape(key_part.shape[0], -1),
    )


def local(
    block_in,
    conditioning,
    cotangent,
    ada_weight,
    ada_bias,
    qkv_weight,
    qv_bias,
    out_weight,
    out_bias,
    up_weight,
    up_bias,
    down_weight,
    down_bias,
):
    w_ada, b_ada, w_qkv, b_qv, w_out, b_out, w_up, b_up, w_down, b_down = (
        lax.all_gather(ada_weight, ("batch", "seq"), axis=0, tiled=True),
        lax.all_gather(ada_bias, ("batch", "seq"), axis=0, tiled=True),
        lax.all_gather(qkv_weight, ("batch", "seq"), axis=0, tiled=True),
        lax.all_gather(qv_bias, ("batch", "seq"), axis=0, tiled=True),
        lax.all_gather(out_weight, ("batch", "seq"), axis=0, tiled=True),
        lax.all_gather(out_bias, ("batch", "seq"), axis=0, tiled=True),
        lax.all_gather(up_weight, ("batch", "seq"), axis=0, tiled=True),
        lax.all_gather(up_bias, ("batch", "seq"), axis=0, tiled=True),
        lax.all_gather(down_weight, ("batch", "seq"), axis=0, tiled=True),
        lax.all_gather(down_bias, ("batch", "seq"), axis=0, tiled=True),
    )
    latents, local_rows, model_width = block_in.shape
    tok_rows = latents * local_rows
    inputs = block_in.astype(jnp.float32)
    cond_act = jax.nn.silu(conditioning.astype(jnp.float32)).astype(jnp.bfloat16)
    modulation = jnp.dot(cond_act, w_ada, preferred_element_type=jnp.float32) + b_ada.astype(
        jnp.float32
    )
    pieces = modulation.reshape(latents, 6, 1, model_width)
    shift_attn, scale_attn, gate_attn, shift_mlp, scale_mlp, gate_mlp = [
        pieces[:, index] for index in range(6)
    ]
    modded_attn = (
        modulate(inputs, shift_attn, scale_attn).astype(jnp.bfloat16).reshape(tok_rows, model_width)
    )
    qkv_bias = jnp.concatenate(
        [b_qv[:model_width], jnp.zeros((model_width,), jnp.bfloat16), b_qv[model_width:]]
    ).astype(jnp.float32)
    qkv_proj = (jnp.dot(modded_attn, w_qkv, preferred_element_type=jnp.float32) + qkv_bias).astype(
        jnp.bfloat16
    )
    qkv_proj = qkv_proj.reshape(latents, local_rows, 3 * model_width)
    queries = qkv_proj[..., :model_width]
    key_part = qkv_proj[..., model_width : 2 * model_width]
    value_part = qkv_proj[..., 2 * model_width :]
    all_keys, all_values = (
        lax.all_gather(key_part, "seq", axis=1, tiled=True),
        lax.all_gather(value_part, "seq", axis=1, tiled=True),
    )
    attended, logsum = lax.map(attend, (queries, all_keys, all_values))
    attended_flat = attended.reshape(tok_rows, model_width)
    attn_proj = (
        jnp.dot(attended_flat, w_out, preferred_element_type=jnp.float32)
        + b_out.astype(jnp.float32)
    ).reshape(latents, local_rows, model_width)
    middle = inputs + gate_attn * attn_proj
    modded_mlp = (
        modulate(middle, shift_mlp, scale_mlp).astype(jnp.bfloat16).reshape(tok_rows, model_width)
    )
    pre_act = jnp.dot(modded_mlp, w_up, preferred_element_type=jnp.float32) + b_up.astype(
        jnp.float32
    )
    gelu_tanh = partial(jax.nn.gelu, approximate=True)
    activated = gelu_tanh(pre_act).astype(jnp.bfloat16)
    mlp_proj = (
        jnp.dot(activated, w_down, preferred_element_type=jnp.float32) + b_down.astype(jnp.float32)
    ).reshape(latents, local_rows, model_width)
    block_out = (middle + gate_mlp * mlp_proj).astype(jnp.bfloat16)
    w_ada, b_ada, w_qkv, b_qv, w_out, b_out, w_up, b_up, w_down, b_down = (
        lax.all_gather(ada_weight, ("batch", "seq"), axis=0, tiled=True),
        lax.all_gather(ada_bias, ("batch", "seq"), axis=0, tiled=True),
        lax.all_gather(qkv_weight, ("batch", "seq"), axis=0, tiled=True),
        lax.all_gather(qv_bias, ("batch", "seq"), axis=0, tiled=True),
        lax.all_gather(out_weight, ("batch", "seq"), axis=0, tiled=True),
        lax.all_gather(out_bias, ("batch", "seq"), axis=0, tiled=True),
        lax.all_gather(up_weight, ("batch", "seq"), axis=0, tiled=True),
        lax.all_gather(up_bias, ("batch", "seq"), axis=0, tiled=True),
        lax.all_gather(down_weight, ("batch", "seq"), axis=0, tiled=True),
        lax.all_gather(down_bias, ("batch", "seq"), axis=0, tiled=True),
    )
    out_cot = cotangent.astype(jnp.float32)
    mlp_grad = (gate_mlp * out_cot).astype(jnp.bfloat16).reshape(tok_rows, model_width)
    down_bias_grad = jnp.sum(mlp_grad.astype(jnp.float32), axis=0)
    down_weight_grad = outer_sum(activated, mlp_grad)
    act_grad = back_dot(mlp_grad, w_down)
    gelu_out, gelu_back = jax.vjp(gelu_tanh, pre_act)
    pre_grad = gelu_back(act_grad)[0].astype(jnp.bfloat16)
    up_bias_grad = jnp.sum(pre_grad.astype(jnp.float32), axis=0)
    up_weight_grad = outer_sum(modded_mlp, pre_grad)
    mlp_mod_grad = back_dot(pre_grad, w_up).reshape(latents, local_rows, model_width)
    mlp_mod_out, mlp_mod_back = jax.vjp(modulate, middle, shift_mlp, scale_mlp)
    middle_part, shift_mlp_grad, scale_mlp_grad = mlp_mod_back(mlp_mod_grad)
    middle_grad = out_cot + middle_part
    gate_mlp_grad = jnp.sum(out_cot * mlp_proj, axis=1, keepdims=True)
    attn_grad = (gate_attn * middle_grad).astype(jnp.bfloat16).reshape(tok_rows, model_width)
    gate_attn_grad = jnp.sum(middle_grad * attn_proj, axis=1, keepdims=True)
    out_bias_grad = jnp.sum(attn_grad.astype(jnp.float32), axis=0)
    out_weight_grad = outer_sum(attended_flat, attn_grad)
    attended_grad = (
        back_dot(attn_grad, w_out).astype(jnp.bfloat16).reshape(latents, local_rows, model_width)
    )
    query_grad, key_terms, value_terms = lax.map(
        attend_back, (queries, all_keys, all_values, logsum, attended_grad)
    )
    key_grad, value_grad = (
        lax.psum_scatter(
            key_terms.astype(jnp.bfloat16), "seq", scatter_dimension=1, tiled=True
        ).astype(jnp.float32),
        lax.psum_scatter(
            value_terms.astype(jnp.bfloat16), "seq", scatter_dimension=1, tiled=True
        ).astype(jnp.float32),
    )
    qkv_grad = (
        jnp.concatenate([query_grad, key_grad, value_grad], axis=-1)
        .astype(jnp.bfloat16)
        .reshape(tok_rows, 3 * model_width)
    )
    qkv_weight_grad = outer_sum(modded_attn, qkv_grad)
    column_sums = jnp.sum(qkv_grad.astype(jnp.float32), axis=0)
    qv_bias_grad = jnp.concatenate([column_sums[:model_width], column_sums[2 * model_width :]])
    attn_mod_grad = back_dot(qkv_grad, w_qkv).reshape(latents, local_rows, model_width)
    attn_mod_out, attn_mod_back = jax.vjp(modulate, inputs, shift_attn, scale_attn)
    input_part, shift_attn_grad, scale_attn_grad = attn_mod_back(attn_mod_grad)
    input_grad = (middle_grad + input_part).astype(jnp.bfloat16)
    modulation_grad = jnp.concatenate(
        [
            shift_attn_grad,
            scale_attn_grad,
            gate_attn_grad,
            shift_mlp_grad,
            scale_mlp_grad,
            gate_mlp_grad,
        ],
        axis=1,
    ).reshape(latents, 6 * model_width)
    ada_bias_grad = jnp.sum(modulation_grad, axis=0)
    ada_weight_grad = lax.dot_general(
        cond_act.astype(jnp.float32), modulation_grad, (((0,), (0,)), ((), ())), precision=HIGHEST
    )
    cond_terms = lax.dot_general(
        modulation_grad, w_ada.astype(jnp.float32), (((1,), (1,)), ((), ())), precision=HIGHEST
    )
    cond_total = lax.psum(cond_terms, "seq")
    silu_out, silu_back = jax.vjp(jax.nn.silu, conditioning.astype(jnp.float32))
    cond_grad = silu_back(cond_total)[0].astype(jnp.bfloat16)
    grad_shards = (
        lax.psum_scatter(ada_weight_grad, ("batch", "seq"), scatter_dimension=0, tiled=True),
        lax.psum_scatter(ada_bias_grad, ("batch", "seq"), scatter_dimension=0, tiled=True),
        lax.psum_scatter(qkv_weight_grad, ("batch", "seq"), scatter_dimension=0, tiled=True),
        lax.psum_scatter(qv_bias_grad, ("batch", "seq"), scatter_dimension=0, tiled=True),
        lax.psum_scatter(out_weight_grad, ("batch", "seq"), scatter_dimension=0, tiled=True),
        lax.psum_scatter(out_bias_grad, ("batch", "seq"), scatter_dimension=0, tiled=True),
        lax.psum_scatter(up_weight_grad, ("batch", "seq"), scatter_dimension=0, tiled=True),
        lax.psum_scatter(up_bias_grad, ("batch", "seq"), scatter_dimension=0, tiled=True),
        lax.psum_scatter(down_weight_grad, ("batch", "seq"), scatter_dimension=0, tiled=True),
        lax.psum_scatter(down_bias_grad, ("batch", "seq"), scatter_dimension=0, tiled=True),
    )
    return (block_out, input_grad, cond_grad) + tuple(grad_shards)


def solution(mesh):
    in_specs = (
        P("batch", "seq", None),
        P("batch", None),
        P("batch", "seq", None),
        P(("batch", "seq"), None),
        P(("batch", "seq")),
        P(("batch", "seq"), None),
        P(("batch", "seq")),
        P(("batch", "seq"), None),
        P(("batch", "seq")),
        P(("batch", "seq"), None),
        P(("batch", "seq")),
        P(("batch", "seq"), None),
        P(("batch", "seq")),
    )
    out_specs = (
        P("batch", "seq", None),
        P("batch", "seq", None),
        P("batch", None),
        P(("batch", "seq"), None),
        P(("batch", "seq")),
        P(("batch", "seq"), None),
        P(("batch", "seq")),
        P(("batch", "seq"), None),
        P(("batch", "seq")),
        P(("batch", "seq"), None),
        P(("batch", "seq")),
        P(("batch", "seq"), None),
        P(("batch", "seq")),
    )
    return jax.shard_map(local, mesh=mesh, in_specs=in_specs, out_specs=out_specs, check_vma=False)
```

profile of v0, /device:TPU:0, one launch (start us, length us, event | category | flops | bytes accessed | tf_op | source)
XLA Modules:
  0.0 1900.1 jit_solution(8685022622630463927)
XLA Ops:
  12.1 43.3 %all-reduce.10 = (bf16[2048]{0:T(1024)(128)(2,1)S(1)}, bf16[6144]{0:T(1024)(128)(2,1)S(1)}, bf16[1024]{0:T(1024)(128)(2,1)S(1)}, bf16[1024]{0:T(1024)(128)(2,1)}) all-reduce(bf16[2048]{0:T(1024)(128)(2,1)S(1)} %dynamic-update-slice.1, bf16[6144]{0:T(1024)(128)(2,1)S(1)} %dynamic-update-slice, ...), channel_id=1, replica_groups=mesh['batch'=16,'seq'=2] {'batch','seq'}, use_global_device_ids=true, to_apply=%add.1 | all-reduce | flops 10240 | bytes 40960
  60.4 50.2 %all-gather.9.cloned.1.call-done = bf16[1024,6144]{1,0:T(8,128)(2,1)} async-done(((bf16[32,6144]{1,0:T(8,128)(2,1)}), bf16[1024,6144]{1,0:T(8,128)(2,1)}) %all-gather.9.cloned.1.call-update) | async-done | bytes 12582928 | tf_op jit(solution)/shard_map/all_gather | solution.py:107
  117.0 64.2 %all-gather.11.cloned.1.call-done = bf16[1024,3072]{1,0:T(8,128)(2,1)} async-done(((bf16[32,3072]{1,0:T(8,128)(2,1)}), bf16[1024,3072]{1,0:T(8,128)(2,1)}) %all-gather.11.cloned.1.call-update) | async-done | bytes 6291472 | tf_op jit(solution)/shard_map/all_gather | solution.py:109
  192.2 65.8 %all-gather = bf16[32,1,128]{2,1,0:T(2,128)(2,1)S(1)} all-gather(bf16[1,1,128]{2,1,0:T(2,128)(2,1)S(1)} %bitcast.176), channel_id=1, replica_groups=mesh['batch'=16,'seq'=2] {'batch','seq'}, dimensions={0}, use_global_device_ids=true | all-gather | bytes 8448 | tf_op jit(solution)/shard_map/all_gather | solution.py:114
  266.5 13.2 multiply_reduce_fusion.1
  279.7 14.3 fusion
  294.1 14.5 fusion.35
  322.4 72.7 %all-gather.19.cloned.1.call-done = bf16[1024,4096]{1,0:T(8,128)(2,1)} async-done(((bf16[32,4096]{1,0:T(8,128)(2,1)}), bf16[1024,4096]{1,0:T(8,128)(2,1)}) %all-gather.19.cloned.1.call-update) | async-done | bytes 8388624 | tf_op jit(solution)/shard_map/all_gather | solution.py:113
  395.1 12.1 fusion.63
  407.2 66.8 %all-gather.21.cloned.1.call-done = bf16[4096,1024]{1,0:T(8,128)(2,1)} async-done(((bf16[128,1024]{1,0:T(8,128)(2,1)}), bf16[4096,1024]{1,0:T(8,128)(2,1)}) %all-gather.21.cloned.1.call-update) | async-done | bytes 8388624 | tf_op jit(solution)/shard_map/all_gather | solution.py:115
  474.0 16.8 convert_reduce_fusion
  506.3 14.8 fusion.32
  521.1 22.8 %multiply_reduce_fusion = (f32[16,512]{1,0:T(8,128)S(1)}, f32[16,512,1024]{2,1,0:T(8,128)}) fusion(f32[16,512,1024]{2,1,0:T(8,128)} %get-tuple-element.98, f32[16,512]{1,0:T(8,128)S(1)} %log_add_fusion, bf16[512,16,64]{0,2,1:T(8,128)(2,1)S(1)} %bitcast.132, bf16[1024,16,64]{0,2,1:T(8,128)(2,1)S(1)} %bitcast.130), kind=kOutput, calls=%fused_computation.1 | convolution fusion | flops 1107288064 | bytes 70320128 | tf_op jit(solution)/shard_map/while/body/eval_jaxpr/qhd,khd->hqk/dot_general | solution.py:67
  544.0 28.6 %multiply_convert_fusion = bf16[16,512,1024]{2,1,0:T(8,128)(2,1)} fusion(f32[16,512,1024]{2,1,0:T(8,128)} %get-tuple-element.102, f32[16,512,1024]{2,1,0:T(8,128)} %get-tuple-element.98, f32[16,512]{1,0:T(8,128)S(1)} %get-tuple-element.101, f32[16,512]{1,0:T(8,128)S(1)} %log_add_fusion), kind=kLoop, calls=%fused_computation | loop fusion | flops 41943040 | bytes 83951616 | tf_op jit(solution)/shard_map/while/body/eval_jaxpr/convert_element_type | solution.py:71
  587.9 12.2 multiply_convert_fusion.3
  600.1 13.6 reduce-scatter.8.cloned.1.call-done
  636.6 16.1 fusion.40
  668.7 13.7 fusion.27
  696.9 41.1 %all-reduce.9 = (f32[6144]{0:T(1024)S(1)}, f32[2048]{0:T(1024)S(1)}, f32[1024]{0:T(1024)S(1)}, f32[4096]{0:T(1024)S(1)}, f32[1024]{0:T(1024)S(1)}) all-reduce(f32[6144]{0:T(1024)S(1)} %reshape.387, f32[2048]{0:T(1024)S(1)} %pad_maximum_fusion.1, f32[1024]{0:T(1024)S(1)} %copy-done.33, ...), channel_id=5, replica_groups=mesh['batch'=16,'seq'=2] {'batch','seq'}, use_global_device_ids=true, to_apply=%region_21.22.clone | all-reduce | flops 14336 | bytes 114688
  741.0 12.8 fusion.73
  759.5 158.2 %reduce-scatter.14.cloned.1.call-done = f32[32,3072]{1,0:T(8,128)} async-done(((f32[1024,3072]{1,0:T(8,128)}), f32[32,3072]{1,0:T(8,128)}) %reduce-scatter.14.cloned.1.call-update) | async-done | bytes 393232 | tf_op jit(solution)/shard_map/reduce_scatter | solution.py:245
  917.7 359.3 %reduce-scatter.18.cloned.1.call-done = f32[32,4096]{1,0:T(8,128)} async-done(((f32[1024,4096]{1,0:T(8,128)}), f32[32,4096]{1,0:T(8,128)}) %reduce-scatter.18.cloned.1.call-update) | async-done | bytes 524304 | tf_op jit(solution)/shard_map/reduce_scatter | solution.py:249
  1277.1 361.6 %reduce-scatter.20.cloned.1.call-done = f32[128,1024]{1,0:T(8,128)} async-done(((f32[4096,1024]{1,0:T(8,128)}), f32[128,1024]{1,0:T(8,128)}) %reduce-scatter.20.cloned.1.call-update) | async-done | bytes 524304 | tf_op jit(solution)/shard_map/reduce_scatter | solution.py:251
  1638.7 254.7 %reduce-scatter.12.cloned.1.call-done = f32[32,6144]{1,0:T(8,128)} async-done(((f32[1024,6144]{1,0:T(8,128)}), f32[32,6144]{1,0:T(8,128)}) %reduce-scatter.12.cloned.1.call-update) | async-done | bytes 786448 | tf_op jit(solution)/shard_map/reduce_scatter | solution.py:243
  (189 shorter events, 141.9 us)
Async XLA Ops:
  7.2 103.4 %all-gather.9.cloned.1.call-start = ((), (), s32[]{:S(2)}) async-start(), calls=%async_computation.7 | async-start | bytes 12976128 | tf_op jit(solution)/shard_map/all_gather | solution.py:107
  7.9 173.3 %all-gather.11.cloned.1.call-start = ((), (), s32[]{:S(2)}) async-start(), calls=%async_computation.8 | async-start | bytes 6488064 | tf_op jit(solution)/shard_map/all_gather | solution.py:109
  8.7 250.0 %all-gather.15.cloned.1.call-start = ((), (), s32[]{:S(2)}) async-start(), calls=%async_computation.10 | async-start | bytes 3145728 | tf_op jit(solution)/shard_map/all_gather | solution.py:143
  56.8 124.4 %copy-start.28 = (f32[512]{0:T(512)}, f32[512]{0:T(512)S(1)}, u32[]{:S(2)}) copy-start(f32[512]{0:T(512)S(1)} %broadcast_multiply_fusion.2) | copy-start | bytes 6148
  59.1 122.1 %copy-start.24 = (f32[512]{0:T(512)}, f32[512]{0:T(512)S(1)}, u32[]{:S(2)}) copy-start(f32[512]{0:T(512)S(1)} %fusion.52) | copy-start | bytes 6148
  60.4 56.6 %copy-start.22 = (f32[1,1024]{1,0:T(1,128)}, f32[1,1024]{1,0:T(1,128)S(1)}, u32[]{:S(2)}) copy-start(f32[1,1024]{1,0:T(1,128)S(1)} %get-tuple-element.76) | copy-start | bytes 12292
  110.5 70.7 %copy-start.5 = (bf16[1,512,1024]{2,1,0:T(8,128)(2,1)S(1)}, bf16[1,512,1024]{2,1,0:T(8,128)(2,1)}, u32[]{:S(2)}) copy-start(bf16[1,512,1024]{2,1,0:T(8,128)(2,1)} %param.13) | copy-start | bytes 3145732
  117.0 70.9 %copy-start.30 = (f32[1,1,1,1024]{3,2,1,0:T(1,128)}, f32[1,1,1,1024]{3,2,1,0:T(1,128)S(1)}, u32[]{:S(2)}) copy-start(f32[1,1,1,1024]{3,2,1,0:T(1,128)S(1)} %get-tuple-element.91) | copy-start | bytes 12292
  117.0 70.9 %copy-start.37 = (f32[1,1,1,1024]{3,2,1,0:T(1,128)}, f32[1,1,1,1024]{3,2,1,0:T(1,128)S(1)}, u32[]{:S(2)}) copy-start(f32[1,1,1,1024]{3,2,1,0:T(1,128)S(1)} %get-tuple-element.90) | copy-start | bytes 12292
  189.6 72.3 %all-gather.13.cloned.1.call-start = ((), (), s32[]{:S(2)}) async-start(), calls=%async_computation.9 | async-start | bytes 3145728 | tf_op jit(solution)/shard_map/all_gather | solution.py:144
  190.2 125.9 %all-gather.17.cloned.1.call-start = ((), (), s32[]{:S(2)}) async-start(), calls=%async_computation.11 | async-start | bytes 2162688 | tf_op jit(solution)/shard_map/all_gather | solution.py:111
  190.8 204.3 %all-gather.19.cloned.1.call-start = ((), (), s32[]{:S(2)}) async-start(), calls=%async_computation.12 | async-start | bytes 8650752 | tf_op jit(solution)/shard_map/all_gather | solution.py:113
  191.4 282.6 %all-gather.21.cloned.1.call-start = ((), (), s32[]{:S(2)}) async-start(), calls=%async_computation.13 | async-start | bytes 8650752 | tf_op jit(solution)/shard_map/all_gather | solution.py:115
  192.1 408.0 %reduce-scatter.10.cloned.1.call-start = ((), (), s32[]{:S(2)}) async-start(), calls=%async_computation.15 | async-start | bytes 3145728 | tf_op jit(solution)/shard_map/reduce_scatter | solution.py:205
  192.2 123.9 %copy-start.39 = (f32[1024]{0:T(1024)}, f32[1024]{0:T(1024)S(1)}, u32[]{:S(2)}) copy-start(f32[1024]{0:T(1024)S(1)} %convert_element_type.154) | copy-start | bytes 12292
  395.1 78.9 %copy-start.17 = (bf16[1,512,1024]{2,1,0:T(8,128)(2,1)S(1)}, bf16[1,512,1024]{2,1,0:T(8,128)(2,1)}, u32[]{:S(2)}) copy-start(bf16[1,512,1024]{2,1,0:T(8,128)(2,1)} %param.15) | copy-start | bytes 3145732
  544.0 69.8 %reduce-scatter.8.cloned.1.call-start = ((), (), s32[]{:S(2)}) async-start(), calls=%async_computation.14 | async-start | bytes 3145728 | tf_op jit(solution)/shard_map/reduce_scatter | solution.py:202
  544.0 28.6 %copy-start.3 = (bf16[1,512,1024]{1,2,0:T(8,128)(2,1)S(1)}, bf16[1,512,1024]{1,2,0:T(8,128)(2,1)}, u32[]{:S(2)}) copy-start(bf16[1,512,1024]{1,2,0:T(8,128)(2,1)} %copy-done.2) | copy-start | bytes 3145732
  583.0 176.5 %reduce-scatter.16.cloned.1.call-start = ((), (), s32[]{:S(2)}) async-start(), calls=%async_computation.18 | async-start | bytes 4325376 | tf_op jit(solution)/shard_map/reduce_scatter | solution.py:247
  586.3 27.4 %copy-start.7 = (bf16[1,512,1024]{2,1,0:T(8,128)(2,1)S(1)}, bf16[1,512,1024]{2,1,0:T(8,128)(2,1)}, u32[]{:S(2)}) copy-start(bf16[1,512,1024]{2,1,0:T(8,128)(2,1)} %param.13) | copy-start | bytes 3145732
  586.4 331.4 %reduce-scatter.14.cloned.1.call-start = ((), (), s32[]{:S(2)}) async-start(), calls=%async_computation.17 | async-start | bytes 12976128 | tf_op jit(solution)/shard_map/reduce_scatter | solution.py:245
  624.0 653.1 %reduce-scatter.18.cloned.1.call-start = ((), (), s32[]{:S(2)}) async-start(), calls=%async_computation.19 | async-start | bytes 17301504 | tf_op jit(solution)/shard_map/reduce_scatter | solution.py:249
  636.2 1002.5 %reduce-scatter.20.cloned.1.call-start = ((), (), s32[]{:S(2)}) async-start(), calls=%async_computation.20 | async-start | bytes 17301504 | tf_op jit(solution)/shard_map/reduce_scatter | solution.py:251
  652.8 1240.6 %reduce-scatter.12.cloned.1.call-start = ((), (), s32[]{:S(2)}) async-start(), calls=%async_computation.16 | async-start | bytes 25952256 | tf_op jit(solution)/shard_map/reduce_scatter | solution.py:243
  (36 other events, 326.9 us)
Sparse Core Ops, SparseCore 0:
  10.9 99.5 all-gather.8
  113.4 67.7 all-gather.10
  189.7 31.7 all-gather.14
  223.5 33.2 all-gather.12
  259.6 56.4 all-gather.16
  319.0 76.1 all-gather.18
  398.1 75.8 all-gather.20
  544.1 30.4 reduce-scatter.9
  583.1 30.5 reduce-scatter.7
  616.5 142.0 reduce-scatter.15
  765.2 152.5 reduce-scatter.13
  920.6 356.4 reduce-scatter.17
  1280.0 358.5 reduce-scatter.19
  1646.7 246.7 reduce-scatter.11
where the time goes:
time: 1910 us; the launch traced here: 1900 us
  waiting for transfers between devices  1410 us (74%)
  matrix products  220 us (12%)
  blocking collectives  155 us (8%)
  other arithmetic  69 us (4%)
  local copies, waits for them, and re-layouts  27.3 us (1%)
    reduce_scatter x1, waiting for transfers between devices, local(): lax.psum_scatter(down_weight_grad, ('batch', 'seq'), scatter_dimension=0,...  362 us
    reduce_scatter x1, waiting for transfers between devices, local(): lax.psum_scatter(up_weight_grad, ('batch', 'seq'), scatter_dimension=0, t...  359 us
    reduce_scatter x1, waiting for transfers between devices, local(): lax.psum_scatter(ada_weight_grad, ('batch', 'seq'), scatter_dimension=0,...  255 us
    reduce_scatter x1, waiting for transfers between devices, local(): lax.psum_scatter(qkv_weight_grad, ('batch', 'seq'), scatter_dimension=0,...  158 us
    unnamed x2, blocking collectives  84.4 us
    all_gather x1, waiting for transfers between devices, local(): lax.all_gather(up_weight, ('batch', 'seq'), axis=0, tiled=True)  72.7 us
    all_gather x1, waiting for transfers between devices, local(): lax.all_gather(down_weight, ('batch', 'seq'), axis=0, tiled=True)  66.8 us
    all_gather x1, blocking collectives, local(): lax.all_gather(up_bias, ('batch', 'seq'), axis=0, tiled=True)  65.8 us
  transfers between devices with their start and end apart: 14, of which 10 were waited for; matrix products, arithmetic and copies ran while one was open for 12% of the time, Pallas kernels for 0%

commit v1 on v0

v1 whole, which is shorter than its diff:
```python
from functools import partial

import jax
import jax.numpy as jnp
import numpy as np
from jax import lax
from jax.experimental import pallas as pl
from jax.experimental.pallas import tpu as pltpu
from jax.sharding import PartitionSpec as P

HEAD_DIM = 64
SCALE = HEAD_DIM**-0.5
EPSILON = 1e-06
HIGHEST = lax.Precision.HIGHEST
F32, BF16 = jnp.float32, jnp.bfloat16
AXES = ("batch", "seq")
VMEM_LIMIT = 56 * 1024 * 1024
TILE = 256


def dot(left, right, dims, kind=F32):
    out = lax.dot_general(left, right, ((dims[:1], dims[1:]), ((), ())), preferred_element_type=F32)
    return out.astype(kind)


def modulate(values, shifts, scales):
    average = jnp.mean(values, axis=-1, keepdims=True)
    centered = values - average
    variance = jnp.mean(centered * centered, axis=-1, keepdims=True)
    return centered * lax.rsqrt(variance + EPSILON) * (1.0 + scales) + shifts


class Grid:
    def __init__(self, mesh):
        batch, seq = mesh.shape["batch"], mesh.shape["seq"]
        self.size = {"z": batch // 4, "y": 2, "c": 2, "s": seq}
        self.shape = tuple(self.size.values())
        self.count = batch * seq

    def locate(self):
        batch, seq = lax.axis_index("batch"), lax.axis_index("seq")
        self.at = {"z": batch // 4, "y": (batch // 2) % 2, "c": batch % 2, "s": seq}
        self.me = batch * self.size["s"] + seq

    def send(self, value, **steps):
        moves = [steps.get(name, 0) for name in self.size]
        pairs = []
        for place in np.ndindex(*self.shape):
            target = tuple((p + m) % n for p, m, n in zip(place, moves, self.shape))
            pairs.append(
                (int(np.ravel_multi_index(place, self.shape)), int(np.ravel_multi_index(target, self.shape)))
            )
        return lax.ppermute(value, AXES, pairs)

    def arrivals(self, value, name):
        return [value] + [self.send(value, **{name: d}) for d in range(1, self.size[name])]

    def gather(self, value, name):
        return jnp.concatenate([part[None] for part in self.arrivals(value, name)])

    def gather_rows(self, value, order):
        for name in order[:-1]:
            value = jnp.concatenate([part[None] for part in self.arrivals(value, name)])
        parts = self.arrivals(value, order[-1])
        names = tuple(reversed(order))
        steps = [dict(zip(names, at)) for at in np.ndindex(*[self.size[name] for name in names])]
        lead = len(order) - 1
        return [part.reshape((-1,) + part.shape[lead:]) for part in parts], steps

    def reduce(self, terms, axis, name, kind):
        n, me = self.size[name], self.at[name]
        total = lax.dynamic_index_in_dim(terms, me, axis, keepdims=False).astype(F32)
        for d in range(1, n):
            part = lax.dynamic_index_in_dim(terms, (me + d) % n, axis, keepdims=False)
            total = total + self.send(part, **{name: d}).astype(F32)
        return total.astype(kind)

    def shard_of(self, back):
        index = 0
        for name, n in self.size.items():
            index = index * n + (self.at[name] - back.get(name, 0)) % n
        return index

    def to_latents(self, terms):
        for axis, name in ((2, "c"), (1, "y"), (0, "z")):
            terms = self.reduce(terms, axis, name, F32)
        return sum(self.arrivals(terms, "s"))


def place_kernel(jobs, flat, table, *refs):
    pieces, out, sems = refs[:-2], refs[-2], refs[-1]
    copies = []
    for at, (piece, block, unit, part) in enumerate(jobs):
        source = pieces[piece].at[block, unit]
        rows, columns = source.shape
        if flat:
            target = out.at[
                pl.ds(pl.multiple_of(table[at] * rows, rows), rows), pl.ds(part * columns, columns)
            ]
        else:
            target = out.at[table[at], part]
        copies.append(pltpu.make_async_copy(source, target, sems.at[at]))
        copies[-1].start()
    for copy in copies:
        copy.wait()


def place(pieces, jobs, table):
    rows, columns = pieces[0].shape[2:]
    parts = 1 + max(job[3] for job in jobs)
    count = len(jobs) // parts
    flat = rows % 16 == 0
    out = pl.pallas_call(
        partial(place_kernel, jobs, flat),
        out_shape=jax.ShapeDtypeStruct(
            (count * rows, parts * columns) if flat else (count, parts, rows, columns), pieces[0].dtype
        ),
        grid_spec=pltpu.PrefetchScalarGridSpec(
            num_scalar_prefetch=1,
            in_specs=[pl.BlockSpec(memory_space=pl.ANY)] * len(pieces),
            out_specs=pl.BlockSpec(memory_space=pltpu.VMEM if flat else pl.ANY),
            scratch_shapes=[pltpu.SemaphoreType.DMA((len(jobs),))],
        ),
        compiler_params=pltpu.CompilerParams(vmem_limit_bytes=VMEM_LIMIT),
        cost_estimate=pl.CostEstimate(
            flops=0, bytes_accessed=4 * len(jobs) * rows * columns, transcendentals=0
        ),
    )(jnp.stack(table).astype(jnp.int32), *pieces)
    if not flat:
        out = out.transpose(0, 2, 1, 3).reshape(count * rows, parts * columns)
    return out


def head_mask(width, head):
    lanes = lax.broadcasted_iota(jnp.int32, (1, width), 1)
    return (lanes >= head * HEAD_DIM) & (lanes < (head + 1) * HEAD_DIM)


def attend_kernel(width, qkv, out, logsum):
    tokens = qkv.shape[1]
    step = min(128, width)
    tile = min(TILE, tokens)
    for start in range(0, width, step):
        keys = qkv[0, :, width + start : width + start + step]
        values = qkv[0, :, 2 * width + start : 2 * width + start + step]
        for row in range(0, tokens, tile):
            queries = qkv[0, row : row + tile, start : start + step] * jnp.asarray(SCALE, BF16)
            total, sums = None, None
            for head in range(step // HEAD_DIM):
                mask = head_mask(step, head)
                scores = dot(jnp.where(mask, queries, jnp.zeros_like(queries)), keys, (1, 1))
                top = jnp.max(scores, axis=1, keepdims=True)
                powers = jnp.exp(scores - top)
                weight = jnp.sum(powers, axis=1, keepdims=True)
                part = dot(powers.astype(BF16), values, (1, 0)) / weight
                level = jnp.broadcast_to(top + jnp.log(weight), part.shape)
                total = part if total is None else jnp.where(mask, part, total)
                sums = level if sums is None else jnp.where(mask, level, sums)
            out[0, row : row + tile, start : start + step] = total.astype(BF16)
            logsum[0, row : row + tile, start : start + step] = sums


def attend(qkv, width):
    latents, tokens, _ = qkv.shape
    spec = lambda columns: pl.BlockSpec((1, tokens, columns), lambda l: (l, 0, 0))
    return pl.pallas_call(
        partial(attend_kernel, width),
        grid=(latents,),
        in_specs=[spec(3 * width)],
        out_specs=[spec(width), spec(width)],
        out_shape=[
            jax.ShapeDtypeStruct((latents, tokens, width), BF16),
            jax.ShapeDtypeStruct((latents, tokens, width), F32),
        ],
        compiler_params=pltpu.CompilerParams(vmem_limit_bytes=VMEM_LIMIT),
        cost_estimate=pl.CostEstimate(
            flops=16 * latents * tokens * tokens * width,
            bytes_accessed=12 * latents * tokens * width,
            transcendentals=latents * tokens * tokens * width // HEAD_DIM,
        ),
    )(qkv)


def attend_back_kernel(width, qkv, grads, logsum, out, key_sum, value_sum):
    tokens = qkv.shape[1]
    step = min(128, width)
    tile = min(TILE, tokens)
    for start in range(0, width, step):
        keys = qkv[0, :, width + start : width + start + step]
        values = qkv[0, :, 2 * width + start : 2 * width + start + step]
        key_sum[...] = jnp.zeros_like(key_sum)
        value_sum[...] = jnp.zeros_like(value_sum)
        for row in range(0, tokens, tile):
            queries = qkv[0, row : row + tile, start : start + step] * jnp.asarray(SCALE, BF16)
            grad = grads[0, row : row + tile, start : start + step]
            query_grad = None
            for head in range(step // HEAD_DIM):
                mask = head_mask(step, head)
                own_queries = jnp.where(mask, queries, jnp.zeros_like(queries))
                own_grad = jnp.where(mask, grad, jnp.zeros_like(grad))
                lane = start + head * HEAD_DIM
                level = logsum[0, row : row + tile, lane : lane + 1]
                probs = jnp.exp(dot(own_queries, keys, (1, 1)) - level)
                prob_grad = dot(own_grad, values, (1, 1))
                inner = jnp.sum(probs * prob_grad, axis=1, keepdims=True)
                score_grad = (probs * (prob_grad - inner)).astype(BF16)
                part = dot(score_grad, keys, (1, 0))
                query_grad = part if query_grad is None else jnp.where(mask, part, query_grad)
                key_sum[...] += dot(score_grad, own_queries, (0, 0))
                value_sum[...] += dot(probs.astype(BF16), own_grad, (0, 0))
            out[0, row : row + tile, start : start + step] = (query_grad * SCALE).astype(BF16)
        out[0, :, width + start : width + start + step] = key_sum[...].astype(BF16)
        out[0, :, 2 * width + start : 2 * width + start + step] = value_sum[...].astype(BF16)


def attend_back(qkv, grads, logsum, width):
    latents, tokens, _ = qkv.shape
    step = min(128, width)
    spec = lambda columns: pl.BlockSpec((1, tokens, columns), lambda l: (l, 0, 0))
    return pl.pallas_call(
        partial(attend_back_kernel, width),
        grid=(latents,),
        in_specs=[spec(3 * width), spec(width), spec(width)],
        out_specs=spec(3 * width),
        out_shape=jax.ShapeDtypeStruct((latents, tokens, 3 * width), BF16),
        scratch_shapes=[pltpu.VMEM((tokens, step), F32), pltpu.VMEM((tokens, step), F32)],
        compiler_params=pltpu.CompilerParams(vmem_limit_bytes=VMEM_LIMIT),
        cost_estimate=pl.CostEstimate(
            flops=40 * latents * tokens * tokens * width,
            bytes_accessed=18 * latents * tokens * width,
            transcendentals=latents * tokens * tokens * width // HEAD_DIM,
        ),
    )(qkv, grads, logsum)


def local(
    grid,
    block_in,
    conditioning,
    cotangent,
    ada_weight,
    ada_bias,
    qkv_weight,
    qv_bias,
    out_weight,
    out_bias,
    up_weight,
    up_bias,
    down_weight,
    down_bias,
):
    grid.locate()
    size, at = grid.size, grid.at
    z_n, y_n, c_n, s_n = grid.shape
    _, rows, width = block_in.shape
    hidden = up_weight.shape[1]
    count = grid.count
    groups = c_n * s_n
    head_cols = width // groups
    short = width // count
    long = hidden // count
    block_cols = s_n * long
    half = hidden // 2
    own_group = at["c"] * s_n + at["s"]
    send = grid.send

    cond_own = conditioning[0].astype(F32)
    cond_act = jax.nn.silu(cond_own).astype(BF16)
    shares = jnp.concatenate([qv_bias, out_bias, up_bias, down_bias, cond_act])
    all_shares = lax.dynamic_update_slice(
        jnp.zeros((count, shares.shape[0]), BF16), shares[None], (grid.me, 0)
    )
    for name in ("c", "z", "y", "s"):
        all_shares = sum(grid.arrivals(all_shares, name))
    cuts = np.cumsum([qv_bias.shape[0], out_bias.shape[0], up_bias.shape[0]])
    bias_cols = shares.shape[0] - width
    b_qv, b_out, b_up, b_down = [
        part.reshape(-1).astype(F32) for part in jnp.split(all_shares[:, :bias_cols], cuts, axis=1)
    ]

    x_own = block_in[0]
    x_all = grid.gather(x_own, "s")
    cond_all = all_shares[:, bias_cols:].reshape(count // s_n, s_n, width)[:, 0]
    cond_flat = lax.dynamic_slice_in_dim(cond_all, grid.me * short, short, axis=1)
    bias_row = lax.dynamic_update_slice(
        jnp.zeros((6 * width,), F32), ada_bias.astype(F32), (grid.me * ada_bias.shape[0],)
    )
    terms = (dot(cond_flat, ada_weight, (1, 0)) + bias_row).reshape(z_n, y_n, c_n, 6 * width)
    modulation = grid.to_latents(terms)
    shift_attn, scale_attn, gate_attn, shift_mlp, scale_mlp, gate_mlp = jnp.split(modulation, 6)

    cols = qkv_weight.reshape(short, 3, groups, head_cols)
    blocks = []
    for c_d in range(c_n):
        for s_d in range(s_n):
            target = (at["c"] + c_d) % c_n * s_n + (at["s"] + s_d) % s_n
            part = lax.dynamic_index_in_dim(cols, target, 2, keepdims=False).reshape(short, 3 * head_cols)
            blocks.append(send(part, c=c_d, s=s_d) if c_d + s_d else part)
    value = jnp.concatenate([block[None] for block in blocks])
    parts, steps = grid.gather_rows(value, ("z", "y"))
    jobs, table = [], []
    for i, back in enumerate(steps):
        piece, block = divmod(i, z_n)
        for group, (c_d, s_d) in enumerate(np.ndindex(c_n, s_n)):
            jobs.append((piece, block * groups + group, 0, 0))
            table.append(grid.shard_of({**back, "c": c_d, "s": s_d}))
    w_qkv = place([part.reshape(-1, 1, short, 3 * head_cols) for part in parts], jobs, table)

    wide = half // width
    up_cols = up_weight.reshape(short, z_n * y_n, c_n, block_cols)
    up_own = lax.dynamic_index_in_dim(up_cols, at["c"], 2, keepdims=False).reshape(short, wide, width)
    up_other = lax.dynamic_index_in_dim(up_cols, 1 - at["c"], 2, keepdims=False).reshape(short, wide, width)
    up_other = send(up_other, c=1)
    units = [out_weight] + [rows_of[:, i] for rows_of in (up_own, up_other) for i in range(wide)]
    units = jnp.concatenate([unit[None] for unit in units])
    parts, steps = grid.gather_rows(units, ("z", "s", "y"))
    each = len(steps) // len(parts)
    jobs, table, out_jobs, out_table = [], [], [], []
    for i, back in enumerate(steps):
        piece, block = divmod(i, each)
        for c_d in range(c_n):
            shard = grid.shard_of({**back, "c": c_d})
            out_jobs.append((c_d, i, 0, 0))
            out_table.append(shard)
            for part in range(wide):
                jobs.append((piece, block, 1 + c_d * wide + part, part))
                table.append(shard)
    w_up = place(parts, jobs, table)
    out_own = jnp.concatenate([part[:, :1] for part in parts])
    w_out = place([out_own, send(out_own, c=1)], out_jobs, out_table)

    parts, steps = grid.gather_rows(down_weight[None], ("z", "y", "s"))
    jobs, table = [], []
    for i, back in enumerate(steps):
        shard = grid.shard_of(back)
        jobs.append(divmod(i, each) + (0, 0))
        table.append(shard // (c_n * s_n) * s_n + shard % s_n)
    w_down = place(parts, jobs, table)

    inputs = x_own.astype(F32)
    modded_all = modulate(x_all.astype(F32), shift_attn, scale_attn).astype(BF16)
    modded_all = modded_all.reshape(s_n * rows, width)
    modded_all = jnp.concatenate([modded_all, send(modded_all, c=1)])
    q_bias = lax.dynamic_index_in_dim(b_qv[:width].reshape(groups, head_cols), own_group, 0, keepdims=False)
    v_bias = lax.dynamic_index_in_dim(b_qv[width:].reshape(groups, head_cols), own_group, 0, keepdims=False)
    qkv_bias = jnp.concatenate([q_bias, jnp.zeros_like(q_bias), v_bias])
    qkv = (dot(modded_all, w_qkv, (1, 0)) + qkv_bias).astype(BF16).reshape(c_n, s_n * rows, 3 * head_cols)
    attended_all, logsum = attend(qkv, head_cols)

    parts = attended_all.reshape(c_n, s_n, rows, head_cols)
    arrived = []
    for c_d in range(c_n):
        for s_d in range(s_n):
            part = parts[c_d, s_d]
            arrived.append(send(part, c=-c_d, s=-s_d) if c_d + s_d else part)
    arrived = jnp.stack(arrived)
    ordered = []
    for c in range(c_n):
        for s in range(s_n):
            index = (c - at["c"]) % c_n * s_n + (s - at["s"]) % s_n
            ordered.append(lax.dynamic_index_in_dim(arrived, index, 0, keepdims=False))
    attended = jnp.concatenate(ordered, axis=1)
    attn_proj = dot(attended, w_out, (1, 0)) + b_out
    middle = inputs + gate_attn * attn_proj
    modded_mlp = modulate(middle, shift_mlp, scale_mlp).astype(BF16)
    mlp_all = jnp.concatenate([modded_mlp, send(modded_mlp, c=1)])
    up_half = lax.dynamic_index_in_dim(b_up.reshape(-1, c_n, block_cols), at["c"], 1, keepdims=False).reshape(half)
    pre_act = dot(mlp_all, w_up, (1, 0)) + up_half
    gelu_tanh = partial(jax.nn.gelu, approximate=True)
    activated = gelu_tanh(pre_act).astype(BF16)
    proj_terms = dot(activated, w_down, (1, 0))
    mlp_proj = proj_terms[:rows] + send(proj_terms[rows:], c=1) + b_down
    block_out = (middle + gate_mlp * mlp_proj).astype(BF16)

    out_cot = cotangent[0].astype(F32)
    mlp_grad = (gate_mlp * out_cot).astype(BF16)
    mlp_grad_all = jnp.concatenate([mlp_grad, send(mlp_grad, c=1)])
    down_bias_grad = jnp.sum(mlp_grad.astype(F32), axis=0)
    down_terms = dot(activated, mlp_grad_all, (0, 0), BF16).reshape(z_n, y_n, s_n, long, width)
    act_grad = dot(mlp_grad_all, w_down, (1, 1))
    _, gelu_back = jax.vjp(gelu_tanh, pre_act)
    pre_grad = gelu_back(act_grad)[0].astype(BF16)
    up_bias_grad = jnp.sum(pre_grad.astype(F32), axis=0)
    up_terms = dot(mlp_all, pre_grad, (0, 0), BF16).reshape(z_n, y_n, c_n, s_n, short, half)
    mod_terms = dot(pre_grad, w_up, (1, 1))
    mlp_mod_grad = mod_terms[:rows] + send(mod_terms[rows:].astype(BF16), c=1).astype(F32)
    _, mlp_mod_back = jax.vjp(modulate, middle, shift_mlp, scale_mlp)
    middle_part, shift_mlp_grad, scale_mlp_grad = mlp_mod_back(mlp_mod_grad)
    middle_grad = out_cot + middle_part
    gate_mlp_grad = jnp.sum(out_cot * mlp_proj, axis=0)
    attn_grad = (gate_attn * middle_grad).astype(BF16)
    gate_attn_grad = jnp.sum(middle_grad * attn_proj, axis=0)
    out_bias_grad = jnp.sum(attn_grad.astype(F32), axis=0)
    out_terms = dot(attended, attn_grad, (0, 0), BF16).reshape(z_n, y_n, c_n, s_n, short, width)
    attended_grad = dot(attn_grad, w_out, (1, 1), BF16).reshape(rows, groups, head_cols)
    arrived = []
    for c_d in range(c_n):
        for s_d in range(s_n):
            target = (at["c"] + c_d) % c_n * s_n + (at["s"] + s_d) % s_n
            part = lax.dynamic_index_in_dim(attended_grad, target, 1, keepdims=False)
            arrived.append(send(part, c=c_d, s=s_d) if c_d + s_d else part)
    grads_all = jnp.concatenate(arrived).reshape(c_n, s_n * rows, head_cols)
    qkv_grad = attend_back(qkv, grads_all, logsum, head_cols).reshape(c_n * s_n * rows, 3 * head_cols)
    qkv_terms = dot(modded_all, qkv_grad, (0, 0), BF16).reshape(z_n, y_n, c_n, s_n, short, 3 * head_cols)
    column_sums = jnp.sum(qkv_grad.astype(F32), axis=0)
    mod_terms = dot(qkv_grad, w_qkv, (1, 1)).reshape(c_n, s_n, rows, width)
    mod_sum = (mod_terms[0] + send(mod_terms[1].astype(BF16), c=1).astype(F32))
    attn_mod_grad = mod_sum[0]
    for d in range(1, s_n):
        attn_mod_grad = attn_mod_grad + send(mod_sum[d].astype(BF16), s=-d).astype(F32)
    _, attn_mod_back = jax.vjp(modulate, inputs, shift_attn, scale_attn)
    input_part, shift_attn_grad, scale_attn_grad = attn_mod_back(attn_mod_grad)
    input_grad = (middle_grad + input_part).astype(BF16)

    modulation_grad = jnp.concatenate(
        [shift_attn_grad, scale_attn_grad, gate_attn_grad, shift_mlp_grad, scale_mlp_grad, gate_mlp_grad]
    )
    def spread(value, index, n, axis):
        shape = value.shape[:axis] + (n,) + value.shape[axis:]
        start = tuple(index if i == axis else 0 for i in range(len(shape)))
        return lax.dynamic_update_slice(jnp.zeros(shape, F32), jnp.expand_dims(value, axis), start)

    q_sums = spread(column_sums[:head_cols], own_group, groups, 0).reshape(-1)
    v_sums = spread(column_sums[2 * head_cols :], own_group, groups, 0).reshape(-1)
    up_sums = spread(up_bias_grad.reshape(-1, block_cols), at["c"], c_n, 1).reshape(-1)
    total = jnp.concatenate([modulation_grad, q_sums, v_sums, out_bias_grad, up_sums, down_bias_grad])
    total = sum(grid.arrivals(total, "s"))
    for name in ("z", "y", "c"):
        total = grid.gather(total, name)
    z, y, c = (
        (at[name] - jnp.arange(size[name])) % size[name] for name in ("z", "y", "c")
    )
    latent = ((z[None, None] * y_n + y[None, :, None]) * c_n + c[:, None, None]).reshape(-1)
    cond_back = jnp.dot(jax.nn.one_hot(latent, count // s_n, dtype=BF16), cond_flat, preferred_element_type=F32)
    mod_grads = total.reshape(-1, total.shape[-1])[:, : 6 * width]
    bias_sums = jnp.sum(total.reshape(-1, total.shape[-1]), axis=0)

    def own_share(start, kept):
        return lax.dynamic_slice_in_dim(bias_sums[start : start + kept * count], grid.me * kept, kept)

    ada_bias_grad = own_share(0, ada_bias.shape[0])
    start = 6 * width
    bias_grads = []
    for bias in (qv_bias, out_bias, up_bias, down_bias):
        bias_grads.append(own_share(start, bias.shape[0]))
        start += bias.shape[0] * count
    qv_bias_grad, out_bias_grad, up_bias_grad, down_bias_grad = bias_grads
    ada_weight_grad = lax.dot_general(
        cond_back, mod_grads, (((0,), (0,)), ((), ())), precision=HIGHEST
    )
    cond_terms = lax.dot_general(
        mod_grads, ada_weight.astype(F32), (((1,), (1,)), ((), ())), precision=HIGHEST
    )
    cond_terms = lax.dynamic_update_slice(
        jnp.zeros((cond_terms.shape[0], width), F32), cond_terms, (0, grid.me * short)
    )
    cond_terms = cond_terms.reshape(c_n, y_n, z_n, width)
    for name in ("c", "y", "z"):
        moved = [cond_terms[0]] + [send(cond_terms[d], **{name: -d}) for d in range(1, size[name])]
        cond_terms = sum(moved)
    cond_total = sum(grid.arrivals(cond_terms, "s"))
    _, silu_back = jax.vjp(jax.nn.silu, cond_own)
    cond_grad = silu_back(cond_total)[0].astype(BF16)[None]

    for axis, name in ((1, "y"), (1, "s"), (0, "z")):
        down_terms = grid.reduce(down_terms, axis, name, F32 if name == "z" else BF16)
    down_weight_grad = down_terms
    out_terms = grid.reduce(out_terms, 2, "c", BF16)
    up_first = lax.dynamic_index_in_dim(up_terms, at["c"], 2, keepdims=False)
    up_second = lax.dynamic_index_in_dim(up_terms, 1 - at["c"], 2, keepdims=False)
    units = [out_terms] + [
        rows_of[..., i * width : (i + 1) * width] for rows_of in (up_first, up_second) for i in range(wide)
    ]
    units = jnp.concatenate(units, axis=3)
    for axis, name in ((2, "s"), (1, "y"), (0, "z")):
        units = grid.reduce(units, axis, name, F32 if name == "z" else BF16)
    units = units.reshape(1 + c_n * wide, short, width)
    out_weight_grad = units[0]
    up_first, up_second = [
        jnp.concatenate([units[first + i] for i in range(wide)], axis=1).reshape(short, -1, 1, block_cols)
        for first in (1, 1 + wide)
    ]
    up_second = send(up_second, c=1)
    even = at["c"] == 0
    up_weight_grad = jnp.concatenate(
        [jnp.where(even, up_first, up_second), jnp.where(even, up_second, up_first)], axis=2
    ).reshape(short, hidden)
    qkv_terms = grid.reduce(grid.reduce(qkv_terms, 1, "y", BF16), 0, "z", F32)
    qkv_terms = qkv_terms.reshape(groups, short, 3 * head_cols)
    arrived = []
    for c_d in range(c_n):
        for s_d in range(s_n):
            target = (at["c"] + c_d) % c_n * s_n + (at["s"] + s_d) % s_n
            part = lax.dynamic_index_in_dim(qkv_terms, target, 0, keepdims=False)
            arrived.append(send(part, c=c_d, s=s_d) if c_d + s_d else part)
    arrived = jnp.stack(arrived)
    ordered = []
    for c in range(c_n):
        for s in range(s_n):
            index = (at["c"] - c) % c_n * s_n + (at["s"] - s) % s_n
            ordered.append(lax.dynamic_index_in_dim(arrived, index, 0, keepdims=False).reshape(short, 3, head_cols))
    qkv_weight_grad = jnp.stack(ordered, axis=2).reshape(short, 3 * width)

    return (
        block_out[None],
        input_grad[None],
        cond_grad,
        ada_weight_grad,
        ada_bias_grad,
        qkv_weight_grad,
        qv_bias_grad,
        out_weight_grad,
        out_bias_grad,
        up_weight_grad,
        up_bias_grad,
        down_weight_grad,
        down_bias_grad,
    )


def solution(mesh):
    tokens = P("batch", "seq", None)
    vector = P("batch", None)
    matrix, line = P(AXES, None), P(AXES)
    in_specs = (tokens, vector, tokens) + (matrix, line) * 5
    out_specs = (tokens, tokens, vector) + (matrix, line) * 5
    return jax.shard_map(
        partial(local, Grid(mesh)), mesh=mesh, in_specs=in_specs, out_specs=out_specs, check_vma=False
    )
```

time: 1910 us -> 716 us (0.37)
  waiting for transfers between devices: 1410 us -> 313 us
  blocking collectives: 155 us -> 0 us
  matrix products: 220 us -> 83.9 us
  starting transfers between devices: 1.18 us -> 96.5 us
  Pallas kernels: 0 us -> 70.8 us
  local copies, waits for them, and re-layouts: 27.3 us -> 81.3 us
    reduce_scatter x7 -> x0, waiting for transfers between devices: 1150 us -> none  [the longest x1 362 us: local(): lax.psum_scatter(down_weight_grad, ('batch', 'seq'), scatter_dimension=0,...]
    ppermute x0 -> x76, waiting for transfers between devices: none -> 313 us  [send(): return lax.ppermute(value, AXES, pairs)]
    all_gather x7 -> x0, waiting for transfers between devices: 261 us -> none  [the longest x1 72.7 us: local(): lax.all_gather(up_weight, ('batch', 'seq'), axis=0, tiled=True)]
    dot_general x20 -> x16, matrix products: 220 us -> 83.9 us  [the longest x13 80.3 us: dot(): lax.dot_general(left, right, ((dims[:1], dims[1:]), ((), ())), preferred_...]
    ppermute x0 -> x76, starting transfers between devices: none -> 96.5 us  [send(): return lax.ppermute(value, AXES, pairs)]
    unnamed x2 -> x0, blocking collectives: 84.4 us -> none
    pallas_call x0 -> x6, Pallas kernels: none -> 70.8 us  [the longest x1 33.8 us: attend_back(): pl.pallas_call(partial(attend_back_kernel, width), grid=(latents,), in_sp...]
    all_gather x1 -> x0, blocking collectives: 65.8 us -> none  [local(): lax.all_gather(up_bias, ('batch', 'seq'), axis=0, tiled=True)]
  transfers between devices with their start and end apart: 14 -> 76, of which waited for: 10 -> 33; matrix products, arithmetic and copies ran while one was open for 12% -> 22% of each run, Pallas kernels for 0% -> 10%
where the time goes in v1:
time: 716 us; the launch traced here: 706 us
  waiting for transfers between devices  313 us (44%)
  starting transfers between devices  96.5 us (13%)
  matrix products  83.9 us (12%)
  local copies, waits for them, and re-layouts  81.3 us (11%)
  Pallas kernels  70.8 us (10%)
  other arithmetic  57.8 us (8%)
    ppermute x76, waiting for transfers between devices, send(): return lax.ppermute(value, AXES, pairs)  313 us
    ppermute x76, starting transfers between devices, send(): return lax.ppermute(value, AXES, pairs)  96.5 us
    dot_general x13, matrix products, dot(): lax.dot_general(left, right, ((dims[:1], dims[1:]), ((), ())), preferred_...  80.3 us
    pallas_call x1, Pallas kernels, attend_back(): pl.pallas_call(partial(attend_back_kernel, width), grid=(latents,), in_sp...  33.8 us
    pallas_call x1, Pallas kernels, attend(): pl.pallas_call(partial(attend_kernel, width), grid=(latents,), in_specs=[...  19.2 us
    pallas_call x4, Pallas kernels, place(): pl.pallas_call(partial(place_kernel, jobs, flat), out_shape=jax.ShapeDtyp...  17.8 us
    unnamed x204, local copies, waits for them, and re-layouts  16.6 us
  transfers between devices with their start and end apart: 76, of which 33 were waited for; matrix products, arithmetic and copies ran while one was open for 22% of the time, Pallas kernels for 10%

profile of v1, /device:TPU:0, one launch (start us, length us, event | category | flops | bytes accessed | tf_op | source)
XLA Modules:
  0.0 706.4 jit_solution(2646292738448408516)
XLA Ops:
  27.9 8.2 %collective-permute-done.5 = bf16[32,1280]{1,0:T(8,128)(2,1)S(1)} collective-permute-done((bf16[32,1280]{1,0:T(8,128)(2,1)S(1)}, bf16[32,1280]{1,0:T(8,128)(2,1)S(1)}, u32[]{:S(2)}, u32[]{:S(2)}) %collective-permute-start.5) | collective-permute-done | bytes 81952 | tf_op jit(solution)/shard_map/ppermute | solution.py:53
  53.2 17.9 %collective-permute-done.8 = f32[6144]{0:T(1024)S(1)} collective-permute-done((f32[6144]{0:T(1024)S(1)}, f32[6144]{0:T(1024)S(1)}, u32[]{:S(2)}, u32[]{:S(2)}) %collective-permute-start.8) | collective-permute-done | bytes 24608 | tf_op jit(solution)/shard_map/ppermute | solution.py:53
  71.8 9.5 %collective-permute-start.9 = (f32[6144]{0:T(1024)S(1)}, f32[6144]{0:T(1024)S(1)}, u32[]{:S(2)}, u32[]{:S(2)}) collective-permute-start(f32[6144]{0:T(1024)S(1)} %bitcast.416), channel_id=1, source_target_pairs={{0,16},{1,17},{2,18},{3,19},{4,20},{5,21},{6,22},{7,23},{8,24},{9,... | collective-permute-start | bytes 73736 | tf_op jit(solution)/shard_map/ppermute | solution.py:53
  95.4 25.1 %collective-permute-done.28 = bf16[4,5,32,1024]{3,2,1,0:T(8,128)(2,1)S(1)} collective-permute-done((bf16[4,5,32,1024]{3,2,1,0:T(8,128)(2,1)S(1)}, bf16[4,5,32,1024]{3,2,1,0:T(8,128)(2,1)S(1)}, u32[]{:S(2)}, u32[]{:S(2)}) %collective-permute-start.28) | collective-permute-done | bytes 1310752 | tf_op jit(solution)/shard_map/ppermute | solution.py:53
  126.8 15.8 %collective-permute-start.19 = (bf16[4,32,768]{2,1,0:T(8,128)(2,1)S(1)}, bf16[4,32,768]{2,1,0:T(8,128)(2,1)S(1)}, u32[]{:S(2)}, u32[]{:S(2)}) collective-permute-start(bf16[4,32,768]{2,1,0:T(8,128)(2,1)S(1)} %get-tuple-element.99), channel_id=1, source_target_pairs={{0,24},{1,25},{2,26},{3,27},{4,28},{5,29},{6,30},{7,31},{8,0},{9,1... | collective-permute-start | bytes 589832 | tf_op jit(solution)/shard_map/ppermute | solution.py:53
  154.0 14.0 %collective-permute-done.33 = bf16[1,128,1024]{2,1,0:T(8,128)(2,1)S(1)} collective-permute-done((bf16[1,128,1024]{2,1,0:T(8,128)(2,1)S(1)}, bf16[1,128,1024]{2,1,0:T(8,128)(2,1)S(1)}, u32[]{:S(2)}, u32[]{:S(2)}) %collective-permute-start.33) | collective-permute-done | bytes 262176 | tf_op jit(solution)/shard_map/ppermute | solution.py:53
  170.8 28.4 %collective-permute-done.20 = bf16[4,4,32,768]{3,2,1,0:T(8,128)(2,1)} collective-permute-done((bf16[4,4,32,768]{3,2,1,0:T(8,128)(2,1)S(1)}, bf16[4,4,32,768]{3,2,1,0:T(8,128)(2,1)}, u32[]{:S(2)}, u32[]{:S(2)}) %collective-permute-start.20) | collective-permute-done | bytes 786464 | tf_op jit(solution)/shard_map/ppermute | solution.py:53
  203.8 7.8 %add_convert_fusion = bf16[2048,768]{1,0:T(8,128)(2,1)} fusion(bf16[1024,768]{1,0:T(8,128)(2,1)} %shard_map.228, f32[768]{0:T(1024)S(1)} %pad_maximum_fusion.32, bf16[1024,1024]{1,0:T(8,128)(2,1)} %collective-permute-done.13, bf16[1024,1024]{1,0:T(8,128)(2,1)} %fusion.12), kind=kOutput, calls=%fused_computation.13 | convolution fusion | flops 3232759808 | bytes 8915968 | tf_op jit(solution)/shard_map/dot_general | solution.py:22
  212.8 19.2 %shard_map.229 = (bf16[2,1024,256]{2,1,0:T(8,128)(2,1)}, f32[2,1024,256]{2,1,0:T(8,128)}) custom-call(bf16[2,1024,768]{2,1,0:T(8,128)(2,1)} %bitcast.437), custom_call_target="tpu_custom_call" | custom-call | flops 8589934592 | bytes 6291456 | tf_op jit(solution)/shard_map/pallas_call | solution.py:166
  269.5 24.2 %collective-permute-done.36 = bf16[2,4,1,128,1024]{4,3,1,2,0:T(8,128)(2,1)} collective-permute-done((bf16[2,4,1,128,1024]{4,3,1,2,0:T(8,128)(2,1)}, bf16[2,4,1,128,1024]{4,3,1,2,0:T(8,128)(2,1)}, u32[]{:S(2)}, u32[]{:S(2)}) %collective-permute-start.36) | collective-permute-done | bytes 2097184 | tf_op jit(solution)/shard_map/ppermute | solution.py:53
  304.7 7.2 %fusion.32 = f32[1024,2048]{1,0:T(8,128)S(1)} fusion(bf16[1024,2048]{1,0:T(8,128)(2,1)} %shard_map.231, bf16[512,1024]{1,0:T(8,128)(2,1)} %collective-permute-done.31, bf16[512,1024]{1,0:T(8,128)(2,1)} %add_convert_fusion.3), kind=kOutput, calls=%fused_computation.87 | convolution fusion | flops 4299161600 | bytes 14680064 | tf_op jit(solution)/shard_map/dot_general | solution.py:22
  312.0 12.7 %convert_reduce_fusion = (f32[2048]{0:T(1024)}, bf16[1024,2048]{1,0:T(8,128)(2,1)}) fusion(f32[1024,2048]{1,0:T(8,128)S(1)} %fusion.32, f32[2048]{0:T(1024)S(1)} %bitcast.426, bf16[2048,1024]{1,0:T(8,128)(2,1)S(1)} %copy-done.22, bf16[512,1024]{1,0:T(8,128)(2,1)S(1)} %collective-permute-done.38, bf16[512,1024]{1,0:T(8,128)(2,1)S(1)} %get-tuple-element.32), kind=kOutput, calls=%fused_computation.9 | convolution fusion | flops 4347394048 | bytes 18890752 | tf_op jit(solution)/shard_map/dot_general | solution.py:22
  324.7 8.4 %fusion.96 = f32[1024,1024]{1,0:T(8,128)} fusion(bf16[1024,2048]{1,0:T(8,128)(2,1)} %get-tuple-element.130, bf16[1024,2048]{1,0:T(8,128)(2,1)S(1)} %copy-done.20), kind=kOutput, calls=%fused_computation.298 | convolution fusion | flops 4294967296 | bytes 12582912 | tf_op jit(solution)/shard_map/dot_general | solution.py:22
  333.1 6.8 convolution_convert_fusion.1
  346.5 10.5 %convolution_convert_fusion = bf16[2048,1024]{1,0:T(8,128)(2,1)S(1)} fusion(bf16[512,1024]{1,0:T(8,128)(2,1)} %copy-done.81, bf16[512,1024]{1,0:T(8,128)(2,1)} %copy-done.29, f32[1024,2048]{1,0:T(8,128)} %copy-done.82, f32[2048]{0:T(1024)} %bitcast.427), kind=kOutput, calls=%fused_computation.27 | convolution fusion | flops 4322230272 | bytes 14688256 | tf_op jit(solution)/shard_map/dot_general | solution.py:22
  365.5 8.2 %fusion.84 = f32[1024,1024]{1,0:T(8,128)S(1)} fusion(bf16[2048,1024]{1,0:T(8,128)(2,1)S(1)} %copy-done.23, f32[1024,2048]{1,0:T(8,128)} %copy-done.82, f32[2048]{0:T(1024)S(1)} %bitcast.428), kind=kOutput, calls=%fused_computation.287 | convolution fusion | flops 4315938816 | bytes 16785408 | tf_op jit(solution)/shard_map/dot_general | solution.py:22
  404.7 33.8 %shard_map.233 = bf16[2,1024,768]{2,1,0:T(8,128)(2,1)} custom-call(bf16[2,1024,768]{2,1,0:T(8,128)(2,1)} %bitcast.438, bf16[2,1024,256]{2,1,0:T(8,128)(2,1)} %bitcast.372, f32[2,1024,256]{2,1,0:T(8,128)} %get-tuple-element.16.logsum), custom_call_target="tpu_custom_call" | custom-call | flops 21474836480 | bytes 9437184 | tf_op jit(solution)/shard_map/pallas_call | solution.py:220
  464.8 12.1 %collective-permute-done.57 = bf16[4,2,2,32,768]{4,3,2,1,0:T(8,128)(2,1)S(1)} collective-permute-done((bf16[4,2,2,32,768]{4,3,2,1,0:T(8,128)(2,1)S(1)}, bf16[4,2,2,32,768]{4,3,2,1,0:T(8,128)(2,1)S(1)}, u32[]{:S(2)}, u32[]{:S(2)}) %collective-permute-start.57) | collective-permute-done | bytes 786464 | tf_op jit(solution)/shard_map/ppermute | solution.py:53
  488.5 9.6 %collective-permute-done.59 = bf16[2,2,32,768]{3,2,1,0:T(8,128)(2,1)S(1)} collective-permute-done((bf16[2,2,32,768]{3,2,1,0:T(8,128)(2,1)S(1)}, bf16[2,2,32,768]{3,2,1,0:T(8,128)(2,1)S(1)}, u32[]{:S(2)}, u32[]{:S(2)}) %collective-permute-start.59) | collective-permute-done | bytes 196640 | tf_op jit(solution)/shard_map/ppermute | solution.py:53
  501.6 8.0 %collective-permute-done.63 = f32[32,768]{1,0:T(8,128)S(1)} collective-permute-done((f32[32,768]{1,0:T(8,128)S(1)}, f32[32,768]{1,0:T(8,128)S(1)}, u32[]{:S(2)}, u32[]{:S(2)}) %collective-permute-start.63) | collective-permute-done | bytes 98336 | tf_op jit(solution)/shard_map/ppermute | solution.py:53
  534.8 57.1 %collective-permute-done.72 = bf16[4,128,1024]{2,1,0:T(8,128)(2,1)} collective-permute-done((bf16[4,128,1024]{2,1,0:T(8,128)(2,1)}, bf16[4,128,1024]{2,1,0:T(8,128)(2,1)}, u32[]{:S(2)}, u32[]{:S(2)}) %collective-permute-start.72) | collective-permute-done | bytes 1048608 | tf_op jit(solution)/shard_map/ppermute | solution.py:53
  613.5 11.2 %collective-permute-done.74 = bf16[128,1024]{1,0:T(8,128)(2,1)S(1)} collective-permute-done((bf16[128,1024]{1,0:T(8,128)(2,1)S(1)}, bf16[128,1024]{1,0:T(8,128)(2,1)S(1)}, u32[]{:S(2)}, u32[]{:S(2)}) %collective-permute-start.74) | collective-permute-done | bytes 262176 | tf_op jit(solution)/shard_map/ppermute | solution.py:53
  638.2 25.1 %collective-permute-done.52 = f32[4,1024]{1,0:T(4,128)S(1)} collective-permute-done((f32[4,1024]{1,0:T(4,128)S(1)}, f32[4,1024]{1,0:T(4,128)S(1)}, u32[]{:S(2)}, u32[]{:S(2)}) %collective-permute-start.52) | collective-permute-done | bytes 16416 | tf_op jit(solution)/shard_map/ppermute | solution.py:53
  686.7 14.7 %collective-permute-done.68 = bf16[160,1024]{1,0:T(8,128)(2,1)S(1)} collective-permute-done((bf16[160,1024]{1,0:T(8,128)(2,1)S(1)}, bf16[160,1024]{1,0:T(8,128)(2,1)S(1)}, u32[]{:S(2)}, u32[]{:S(2)}) %collective-permute-start.68) | collective-permute-done | bytes 327712 | tf_op jit(solution)/shard_map/ppermute | solution.py:53
  (538 shorter events, 308.1 us)
Async XLA Ops:
  7.6 33.3 %collective-permute-start.24 = (bf16[32,2,1024]{2,0,1:T(8,128)(2,1)S(1)}, bf16[32,2,1024]{2,0,1:T(8,128)(2,1)S(1)}, u32[]{:S(2)}, u32[]{:S(2)}) collective-permute-start(bf16[32,2,1024]{2,0,1:T(8,128)(2,1)S(1)} %copy.106), channel_id=1, source_target_pairs={{0,2},{1,3},{2,0},{3,1},{4,6},{5,7},{6,4},{7,5},{8,10},{9,11},{10,... | collective-permute-start | bytes 393224 | tf_op jit(solution)/shard_map/ppermute | solution.py:53
  7.7 84.2 %collective-permute-start.12 = (bf16[512,1024]{1,0:T(8,128)(2,1)}, bf16[512,1024]{1,0:T(8,128)(2,1)S(1)}, u32[]{:S(2)}, u32[]{:S(2)}) collective-permute-start(bf16[512,1024]{1,0:T(8,128)(2,1)} %bitcast.349), channel_id=1, source_target_pairs={{0,1},{1,0},{2,3},{3,2},{4,5},{5,4},{6,7},{7,6},{8,9},{9,8},{10,11... | collective-permute-start | bytes 3145736 | tf_op jit(solution)/shard_map/ppermute | solution.py:53
  48.6 36.3 %collective-permute-start.27 = (bf16[5,32,1024]{2,1,0:T(8,128)(2,1)S(1)}, bf16[5,32,1024]{2,1,0:T(8,128)(2,1)S(1)}, u32[]{:S(2)}, u32[]{:S(2)}) collective-permute-start(bf16[5,32,1024]{2,1,0:T(8,128)(2,1)S(1)} %fusion.49), channel_id=1, source_target_pairs={{0,24},{1,25},{2,26},{3,27},{4,28},{5,29},{6,30},{7,31},{8,0},{9,1... | collective-permute-start | bytes 983048 | tf_op jit(solution)/shard_map/ppermute | solution.py:53
  49.1 36.6 %collective-permute-start.26 = (bf16[5,32,1024]{2,1,0:T(8,128)(2,1)S(1)}, bf16[5,32,1024]{2,1,0:T(8,128)(2,1)}, u32[]{:S(2)}, u32[]{:S(2)}) collective-permute-start(bf16[5,32,1024]{2,1,0:T(8,128)(2,1)S(1)} %fusion.49), channel_id=1, source_target_pairs={{0,16},{1,17},{2,18},{3,19},{4,20},{5,21},{6,22},{7,23},{8,24},{9,... | collective-permute-start | bytes 983048 | tf_op jit(solution)/shard_map/ppermute | solution.py:53
  49.1 36.9 %collective-permute-start.25 = (bf16[5,32,1024]{2,1,0:T(8,128)(2,1)S(1)}, bf16[5,32,1024]{2,1,0:T(8,128)(2,1)}, u32[]{:S(2)}, u32[]{:S(2)}) collective-permute-start(bf16[5,32,1024]{2,1,0:T(8,128)(2,1)S(1)} %fusion.49), channel_id=1, source_target_pairs={{0,8},{1,9},{2,10},{3,11},{4,12},{5,13},{6,14},{7,15},{8,16},{9,17... | collective-permute-start | bytes 983048 | tf_op jit(solution)/shard_map/ppermute | solution.py:53
  83.2 40.8 %collective-permute-start.16 = (bf16[32,768]{1,0:T(8,128)(2,1)}, bf16[32,768]{1,0:T(8,128)(2,1)S(1)}, u32[]{:S(2)}, u32[]{:S(2)}) collective-permute-start(bf16[32,768]{1,0:T(8,128)(2,1)} %bitcast.194), channel_id=1, source_target_pairs={{0,3},{1,2},{2,1},{3,0},{4,7},{5,6},{6,5},{7,4},{8,11},{9,10},{10,... | collective-permute-start | bytes 147464 | tf_op jit(solution)/shard_map/ppermute | solution.py:53
  84.9 39.1 %collective-permute-start.14 = (bf16[32,768]{1,0:T(8,128)(2,1)S(1)}, bf16[32,768]{1,0:T(8,128)(2,1)}, u32[]{:S(2)}, u32[]{:S(2)}) collective-permute-start(bf16[32,768]{1,0:T(8,128)(2,1)S(1)} %bitcast.412), channel_id=1, source_target_pairs={{0,1},{1,0},{2,3},{3,2},{4,5},{5,4},{6,7},{7,6},{8,9},{9,8},{10,11... | collective-permute-start | bytes 147464 | tf_op jit(solution)/shard_map/ppermute | solution.py:53
  85.6 38.4 %collective-permute-start.15 = (bf16[32,768]{1,0:T(8,128)(2,1)S(1)}, bf16[32,768]{1,0:T(8,128)(2,1)}, u32[]{:S(2)}, u32[]{:S(2)}) collective-permute-start(bf16[32,768]{1,0:T(8,128)(2,1)S(1)} %bitcast.411), channel_id=1, source_target_pairs={{0,2},{1,3},{2,0},{3,1},{4,6},{5,7},{6,4},{7,5},{8,10},{9,11},{10,... | collective-permute-start | bytes 147464 | tf_op jit(solution)/shard_map/ppermute | solution.py:53
  95.4 108.4 %collective-permute-start.13 = (bf16[1024,1024]{1,0:T(8,128)(2,1)}, bf16[1024,1024]{1,0:T(8,128)(2,1)}, u32[]{:S(2)}, u32[]{:S(2)}) collective-permute-start(bf16[1024,1024]{1,0:T(8,128)(2,1)} %fusion.12), channel_id=1, source_target_pairs={{0,2},{1,3},{2,0},{3,1},{4,6},{5,7},{6,4},{7,5},{8,10},{9,11},{10,... | collective-permute-start | bytes 6291464 | tf_op jit(solution)/shard_map/ppermute | solution.py:53
  122.2 89.3 %collective-permute-start.29 = (bf16[2,4,5,32,1024]{4,3,2,1,0:T(8,128)(2,1)}, bf16[2,4,5,32,1024]{4,3,2,1,0:T(8,128)(2,1)}, u32[]{:S(2)}, u32[]{:S(2)}) collective-permute-start(bf16[2,4,5,32,1024]{4,3,2,1,0:T(8,128)(2,1)} %pad_maximum_fusion.3), channel_id=1, source_target_pairs={{0,4},{1,5},{2,6},{3,7},{4,0},{5,1},{6,2},{7,3},{8,12},{9,13},{10,... | collective-permute-start | bytes 7864328 | tf_op jit(solution)/shard_map/ppermute | solution.py:53
  153.5 45.7 %collective-permute-start.20 = (bf16[4,4,32,768]{3,2,1,0:T(8,128)(2,1)S(1)}, bf16[4,4,32,768]{3,2,1,0:T(8,128)(2,1)}, u32[]{:S(2)}, u32[]{:S(2)}) collective-permute-start(bf16[4,4,32,768]{3,2,1,0:T(8,128)(2,1)S(1)} %pad_maximum_fusion.22), channel_id=1, source_target_pairs={{0,4},{1,5},{2,6},{3,7},{4,0},{5,1},{6,2},{7,3},{8,12},{9,13},{10,... | collective-permute-start | bytes 2359304 | tf_op jit(solution)/shard_map/ppermute | solution.py:53
  170.1 69.0 %collective-permute-start.35 = (bf16[4,1,128,1024]{3,2,1,0:T(8,128)(2,1)}, bf16[4,1,128,1024]{3,2,1,0:T(8,128)(2,1)}, u32[]{:S(2)}, u32[]{:S(2)}) collective-permute-start(bf16[4,1,128,1024]{3,2,1,0:T(8,128)(2,1)} %get-tuple-element.63), channel_id=1, source_target_pairs={{0,4},{1,5},{2,6},{3,7},{4,0},{5,1},{6,2},{7,3},{8,12},{9,13},{10,... | collective-permute-start | bytes 3145736 | tf_op jit(solution)/shard_map/ppermute | solution.py:53
  212.8 37.6 %collective-permute-start.30 = (bf16[16,1,32,1024]{3,2,1,0:T(8,128)(2,1)S(1)}, bf16[16,1,32,1024]{3,2,1,0:T(8,128)(2,1)}, u32[]{:S(2)}, u32[]{:S(2)}) collective-permute-start(bf16[16,1,32,1024]{3,2,1,0:T(8,128)(2,1)S(1)} %pad_maximum_fusion.18.refs_0_), channel_id=1, source_target_pairs={{0,2},{1,3},{2,0},{3,1},{4,6},{5,7},{6,4},{7,5},{8,10},{9,11},{10,... | collective-permute-start | bytes 3145736 | tf_op jit(solution)/shard_map/ppermute | solution.py:53
  241.9 51.7 %collective-permute-start.36 = (bf16[2,4,1,128,1024]{4,3,1,2,0:T(8,128)(2,1)}, bf16[2,4,1,128,1024]{4,3,1,2,0:T(8,128)(2,1)}, u32[]{:S(2)}, u32[]{:S(2)}) collective-permute-start(bf16[2,4,1,128,1024]{4,3,1,2,0:T(8,128)(2,1)} %pad_maximum_fusion.5), channel_id=1, source_target_pairs={{0,1},{1,0},{2,3},{3,2},{4,5},{5,4},{6,7},{7,6},{8,9},{9,8},{10,11... | collective-permute-start | bytes 6291464 | tf_op jit(solution)/shard_map/ppermute | solution.py:53
  261.7 43.0 %collective-permute-start.31 = (bf16[512,1024]{1,0:T(8,128)(2,1)}, bf16[512,1024]{1,0:T(8,128)(2,1)}, u32[]{:S(2)}, u32[]{:S(2)}) collective-permute-start(bf16[512,1024]{1,0:T(8,128)(2,1)} %add_convert_fusion.3), channel_id=1, source_target_pairs={{0,2},{1,3},{2,0},{3,1},{4,6},{5,7},{6,4},{7,5},{8,10},{9,11},{10,... | collective-permute-start | bytes 3145736 | tf_op jit(solution)/shard_map/ppermute | solution.py:53
  268.9 43.0 %collective-permute-start.38 = (bf16[512,1024]{1,0:T(8,128)(2,1)S(1)}, bf16[512,1024]{1,0:T(8,128)(2,1)S(1)}, u32[]{:S(2)}, u32[]{:S(2)}) collective-permute-start(bf16[512,1024]{1,0:T(8,128)(2,1)S(1)} %get-tuple-element.32), channel_id=1, source_target_pairs={{0,2},{1,3},{2,0},{3,1},{4,6},{5,7},{6,4},{7,5},{8,10},{9,11},{10,... | collective-permute-start | bytes 3145736 | tf_op jit(solution)/shard_map/ppermute | solution.py:53
  375.5 153.4 %collective-permute-start.37 = (f32[512,1024]{1,0:T(8,128)}, f32[512,1024]{1,0:T(8,128)}, u32[]{:S(2)}, u32[]{:S(2)}) collective-permute-start(f32[512,1024]{1,0:T(8,128)} %slice.230), channel_id=1, source_target_pairs={{0,2},{1,3},{2,0},{3,1},{4,6},{5,7},{6,4},{7,5},{8,10},{9,11},{10,... | collective-permute-start | bytes 6291464 | tf_op jit(solution)/shard_map/ppermute | solution.py:53
  376.4 107.0 %collective-permute-start.71 = (bf16[4,2,128,1024]{3,2,0,1:T(8,128)(2,1)}, bf16[4,2,128,1024]{3,2,0,1:T(8,128)(2,1)}, u32[]{:S(2)}, u32[]{:S(2)}) collective-permute-start(bf16[4,2,128,1024]{3,2,0,1:T(8,128)(2,1)} %bitcast.334), channel_id=1, source_target_pairs={{0,4},{1,5},{2,6},{3,7},{4,0},{5,1},{6,2},{7,3},{8,12},{9,13},{10,... | collective-permute-start | bytes 6291464 | tf_op jit(solution)/shard_map/ppermute | solution.py:53
  397.7 59.7 %collective-permute-start.64 = (bf16[4,2,2,32,1024]{4,3,0,1,2:T(8,128)(2,1)}, bf16[4,2,2,32,1024]{4,3,0,1,2:T(8,128)(2,1)}, u32[]{:S(2)}, u32[]{:S(2)}) collective-permute-start(bf16[4,2,2,32,1024]{4,3,0,1,2:T(8,128)(2,1)} %bitcast.337), channel_id=1, source_target_pairs={{0,2},{1,3},{2,0},{3,1},{4,6},{5,7},{6,4},{7,5},{8,10},{9,11},{10,... | collective-permute-start | bytes 3145736 | tf_op jit(solution)/shard_map/ppermute | solution.py:53
  483.5 40.0 %collective-permute-start.44 = (bf16[512,1024]{1,0:T(8,128)(2,1)}, bf16[512,1024]{1,0:T(8,128)(2,1)}, u32[]{:S(2)}, u32[]{:S(2)}) collective-permute-start(bf16[512,1024]{1,0:T(8,128)(2,1)} %fusion.36), channel_id=1, source_target_pairs={{0,1},{1,0},{2,3},{3,2},{4,5},{5,4},{6,7},{7,6},{8,9},{9,8},{10,11... | collective-permute-start | bytes 3145736 | tf_op jit(solution)/shard_map/ppermute | solution.py:53
  509.6 116.3 %collective-permute-start.65 = (bf16[4,2,160,1024]{3,2,0,1:T(8,128)(2,1)}, bf16[4,2,160,1024]{3,2,0,1:T(8,128)(2,1)}, u32[]{:S(2)}, u32[]{:S(2)}) collective-permute-start(bf16[4,2,160,1024]{3,2,0,1:T(8,128)(2,1)} %dynamic-slice_bitcast_fusion), channel_id=1, source_target_pairs={{0,1},{1,0},{2,3},{3,2},{4,5},{5,4},{6,7},{7,6},{8,9},{9,8},{10,11... | collective-permute-start | bytes 7864328 | tf_op jit(solution)/shard_map/ppermute | solution.py:53
  510.5 81.4 %collective-permute-start.72 = (bf16[4,128,1024]{2,1,0:T(8,128)(2,1)}, bf16[4,128,1024]{2,1,0:T(8,128)(2,1)}, u32[]{:S(2)}, u32[]{:S(2)}) collective-permute-start(bf16[4,128,1024]{2,1,0:T(8,128)(2,1)} %dynamic-slice_bitcast_fusion.2), channel_id=1, source_target_pairs={{0,1},{1,0},{2,3},{3,2},{4,5},{5,4},{6,7},{7,6},{8,9},{9,8},{10,11... | collective-permute-start | bytes 3145736 | tf_op jit(solution)/shard_map/ppermute | solution.py:53
  533.7 59.9 %collective-permute-start.45 = (f32[14336]{0:T(1024)S(1)}, f32[14336]{0:T(1024)S(1)}, u32[]{:S(2)}, u32[]{:S(2)}) collective-permute-start(f32[14336]{0:T(1024)S(1)} %constant_dynamic-update-slice_fusion.3), channel_id=1, source_target_pairs={{0,1},{1,0},{2,3},{3,2},{4,5},{5,4},{6,7},{7,6},{8,9},{9,8},{10,11... | collective-permute-start | bytes 172040 | tf_op jit(solution)/shard_map/ppermute | solution.py:53
  631.6 35.6 %collective-permute-start.66 = (bf16[4,160,1024]{2,1,0:T(8,128)(2,1)}, bf16[4,160,1024]{2,1,0:T(8,128)(2,1)}, u32[]{:S(2)}, u32[]{:S(2)}) collective-permute-start(bf16[4,160,1024]{2,1,0:T(8,128)(2,1)} %dynamic-slice_bitcast_fusion.1), channel_id=1, source_target_pairs={{0,4},{1,5},{2,6},{3,7},{4,0},{5,1},{6,2},{7,3},{8,12},{9,13},{10,... | collective-permute-start | bytes 3932168 | tf_op jit(solution)/shard_map/ppermute | solution.py:53
  (138 other events, 2290.6 us)

commit v2 on v1

v2 whole, which is shorter than its diff:
```python
from functools import partial

import jax
import jax.numpy as jnp
import numpy as np
from jax import lax
from jax.experimental import pallas as pl
from jax.experimental.pallas import tpu as pltpu
from jax.sharding import PartitionSpec as P

HEAD_DIM = 64
SCALE = HEAD_DIM**-0.5
EPSILON = 1e-06
HIGHEST = lax.Precision.HIGHEST
F32, BF16 = jnp.float32, jnp.bfloat16
AXES = ("batch", "seq")
VMEM_LIMIT = 56 * 1024 * 1024
TILE = 256


def dot(left, right, dims, kind=F32):
    out = lax.dot_general(left, right, ((dims[:1], dims[1:]), ((), ())), preferred_element_type=F32)
    return out.astype(kind)


def after(value, *needed):
    return lax.optimization_barrier((value,) + needed)[0]


def settle(parts, kind, *needed):
    if needed:
        parts = lax.optimization_barrier(tuple(parts) + needed)[: len(parts)]
    return sum(part.astype(F32) for part in parts).astype(kind)


def normalize(values):
    average = jnp.mean(values, axis=-1, keepdims=True)
    centered = values - average
    variance = jnp.mean(centered * centered, axis=-1, keepdims=True)
    inverse = lax.rsqrt(variance + EPSILON)
    return centered * inverse, inverse


def normalize_back(grads, normed, inverse):
    average = jnp.mean(grads, axis=-1, keepdims=True)
    along = jnp.mean(grads * normed, axis=-1, keepdims=True)
    return inverse * (grads - average - normed * along)


class Grid:
    def __init__(self, mesh):
        batch, seq = mesh.shape["batch"], mesh.shape["seq"]
        self.size = {"z": batch // 4, "y": 2, "c": 2, "s": seq}
        self.shape = tuple(self.size.values())
        self.count = batch * seq

    def locate(self):
        batch, seq = lax.axis_index("batch"), lax.axis_index("seq")
        self.at = {"z": batch // 4, "y": (batch // 2) % 2, "c": batch % 2, "s": seq}
        self.me = batch * self.size["s"] + seq

    def send(self, value, **steps):
        moves = [steps.get(name, 0) for name in self.size]
        pairs = []
        for place in np.ndindex(*self.shape):
            target = tuple((p + m) % n for p, m, n in zip(place, moves, self.shape))
            pairs.append(
                (int(np.ravel_multi_index(place, self.shape)), int(np.ravel_multi_index(target, self.shape)))
            )
        return lax.ppermute(value, AXES, pairs)

    def steps(self, *names):
        return [dict(zip(names, at)) for at in np.ndindex(*[self.size[name] for name in names])]

    def arrivals(self, value, *names):
        return [self.send(value, **step) if any(step.values()) else value for step in self.steps(*names)]

    def gather(self, value, *names):
        return jnp.concatenate([part[None] for part in self.arrivals(value, *names)])

    def shed(self, terms, axis, name):
        n, me = self.size[name], self.at[name]
        parts = [lax.dynamic_index_in_dim(terms, (me + d) % n, axis, keepdims=False) for d in range(n)]
        self.sent = parts[1:]
        return [self.send(part, **{name: d}) if d else part for d, part in enumerate(parts)]

    def reduce(self, terms, axis, name, kind):
        return settle(self.shed(terms, axis, name), kind)

    def shard_of(self, back):
        index = 0
        for name, n in self.size.items():
            index = index * n + (self.at[name] - back.get(name, 0)) % n
        return index

    def sum_over(self, value, *names):
        return sum(self.arrivals(value, *names))


def place_kernel(jobs, flat, table, *refs):
    pieces, out, sems = refs[:-2], refs[-2], refs[-1]
    copies = []
    for at, (piece, block, unit, part) in enumerate(jobs):
        source = pieces[piece].at[block, unit]
        rows, columns = source.shape
        if flat:
            target = out.at[
                pl.ds(pl.multiple_of(table[at] * rows, rows), rows), pl.ds(part * columns, columns)
            ]
        else:
            target = out.at[table[at], part]
        copies.append(pltpu.make_async_copy(source, target, sems.at[at]))
        copies[-1].start()
    for copy in copies:
        copy.wait()


def place(pieces, jobs, table):
    rows, columns = pieces[0].shape[2:]
    parts = 1 + max(job[3] for job in jobs)
    count = len(jobs) // parts
    flat = rows % 16 == 0
    out = pl.pallas_call(
        partial(place_kernel, jobs, flat),
        out_shape=jax.ShapeDtypeStruct(
            (count * rows, parts * columns) if flat else (count, parts, rows, columns), pieces[0].dtype
        ),
        grid_spec=pltpu.PrefetchScalarGridSpec(
            num_scalar_prefetch=1,
            in_specs=[pl.BlockSpec(memory_space=pl.ANY)] * len(pieces),
            out_specs=pl.BlockSpec(memory_space=pltpu.VMEM if flat else pl.ANY),
            scratch_shapes=[pltpu.SemaphoreType.DMA((len(jobs),))],
        ),
        compiler_params=pltpu.CompilerParams(vmem_limit_bytes=VMEM_LIMIT),
        cost_estimate=pl.CostEstimate(
            flops=0, bytes_accessed=4 * len(jobs) * rows * columns, transcendentals=0
        ),
    )(jnp.stack(table).astype(jnp.int32), *pieces)
    if not flat:
        out = out.transpose(0, 2, 1, 3).reshape(count * rows, parts * columns)
    return out


def columns_kernel(width, table, *refs):
    pieces, out = refs[:-1], refs[-1]
    total = out.shape[1] // 3
    for at, piece in enumerate(pieces):
        for part in range(3):
            start = pl.multiple_of(part * total + table[at] * width, width)
            out[:, pl.ds(start, width)] = piece[:, part * width : (part + 1) * width]


def place_columns(pieces, table, width):
    rows, total = pieces[0].shape[0], len(pieces) * 3 * width
    if width % 128 != 0:
        out = jnp.zeros((rows, 3, total // 3), F32)
        for piece, group in zip(pieces, table):
            out = lax.dynamic_update_slice(out, piece.reshape(rows, 3, width), (0, 0, group * width))
        return out.reshape(rows, total)
    return pl.pallas_call(
        partial(columns_kernel, width),
        out_shape=jax.ShapeDtypeStruct((rows, total), F32),
        grid_spec=pltpu.PrefetchScalarGridSpec(
            num_scalar_prefetch=1,
            in_specs=[pl.BlockSpec(memory_space=pltpu.VMEM)] * len(pieces),
            out_specs=pl.BlockSpec(memory_space=pltpu.VMEM),
        ),
    )(jnp.stack(table).astype(jnp.int32), *pieces)


def head_mask(width, head):
    lanes = lax.broadcasted_iota(jnp.int32, (1, width), 1)
    return (lanes >= head * HEAD_DIM) & (lanes < (head + 1) * HEAD_DIM)


def attend_kernel(width, qkv, out, logsum):
    tokens = qkv.shape[1]
    step = min(128, width)
    tile = min(TILE, tokens)
    for start in range(0, width, step):
        keys = qkv[0, :, width + start : width + start + step]
        values = qkv[0, :, 2 * width + start : 2 * width + start + step]
        for row in range(0, tokens, tile):
            queries = qkv[0, row : row + tile, start : start + step] * jnp.asarray(SCALE, BF16)
            total, sums = None, None
            for head in range(step // HEAD_DIM):
                mask = head_mask(step, head)
                scores = dot(jnp.where(mask, queries, jnp.zeros_like(queries)), keys, (1, 1))
                top = jnp.max(scores, axis=1, keepdims=True)
                powers = jnp.exp(scores - top)
                weight = jnp.sum(powers, axis=1, keepdims=True)
                part = dot(powers.astype(BF16), values, (1, 0)) / weight
                level = jnp.broadcast_to(top + jnp.log(weight), part.shape)
                total = part if total is None else jnp.where(mask, part, total)
                sums = level if sums is None else jnp.where(mask, level, sums)
            out[0, row : row + tile, start : start + step] = total.astype(BF16)
            logsum[0, row : row + tile, start : start + step] = sums


def attend(qkv, latent, width):
    _, tokens, _ = qkv.shape
    spec = lambda columns, at: pl.BlockSpec((1, tokens, columns), lambda l: (at, 0, 0))
    return pl.pallas_call(
        partial(attend_kernel, width),
        grid=(1,),
        in_specs=[spec(3 * width, latent)],
        out_specs=[spec(width, 0), spec(width, 0)],
        out_shape=[
            jax.ShapeDtypeStruct((1, tokens, width), BF16),
            jax.ShapeDtypeStruct((1, tokens, width), F32),
        ],
        compiler_params=pltpu.CompilerParams(vmem_limit_bytes=VMEM_LIMIT),
        cost_estimate=pl.CostEstimate(
            flops=tokens * tokens * width,
            bytes_accessed=12 * tokens * width,
            transcendentals=0,
        ),
    )(qkv)


def attend_back_kernel(width, qkv, grads, logsum, out, key_sum, value_sum):
    tokens = qkv.shape[1]
    step = min(128, width)
    tile = min(TILE, tokens)
    for start in range(0, width, step):
        keys = qkv[0, :, width + start : width + start + step]
        values = qkv[0, :, 2 * width + start : 2 * width + start + step]
        key_sum[...] = jnp.zeros_like(key_sum)
        value_sum[...] = jnp.zeros_like(value_sum)
        for row in range(0, tokens, tile):
            queries = qkv[0, row : row + tile, start : start + step] * jnp.asarray(SCALE, BF16)
            grad = grads[0, row : row + tile, start : start + step]
            query_grad = None
            for head in range(step // HEAD_DIM):
                mask = head_mask(step, head)
                own_queries = jnp.where(mask, queries, jnp.zeros_like(queries))
                own_grad = jnp.where(mask, grad, jnp.zeros_like(grad))
                lane = start + head * HEAD_DIM
                level = logsum[0, row : row + tile, lane : lane + 1]
                probs = jnp.exp(dot(own_queries, keys, (1, 1)) - level)
                prob_grad = dot(own_grad, values, (1, 1))
                inner = jnp.sum(probs * prob_grad, axis=1, keepdims=True)
                score_grad = (probs * (prob_grad - inner)).astype(BF16)
                part = dot(score_grad, keys, (1, 0))
                query_grad = part if query_grad is None else jnp.where(mask, part, query_grad)
                key_sum[...] += dot(score_grad, own_queries, (0, 0))
                value_sum[...] += dot(probs.astype(BF16), own_grad, (0, 0))
            out[0, row : row + tile, start : start + step] = (query_grad * SCALE).astype(BF16)
        out[0, :, width + start : width + start + step] = key_sum[...].astype(BF16)
        out[0, :, 2 * width + start : 2 * width + start + step] = value_sum[...].astype(BF16)


def attend_back(qkv, grads, logsum, latent, width):
    _, tokens, _ = qkv.shape
    step = min(128, width)
    spec = lambda columns, at: pl.BlockSpec((1, tokens, columns), lambda l: (at, 0, 0))
    return pl.pallas_call(
        partial(attend_back_kernel, width),
        grid=(1,),
        in_specs=[spec(3 * width, latent), spec(width, 0), spec(width, 0)],
        out_specs=spec(3 * width, 0),
        out_shape=jax.ShapeDtypeStruct((1, tokens, 3 * width), BF16),
        scratch_shapes=[pltpu.VMEM((tokens, step), F32), pltpu.VMEM((tokens, step), F32)],
        compiler_params=pltpu.CompilerParams(vmem_limit_bytes=VMEM_LIMIT),
        cost_estimate=pl.CostEstimate(
            flops=2 * tokens * tokens * width,
            bytes_accessed=18 * tokens * width,
            transcendentals=0,
        ),
    )(qkv, grads, logsum)


def local(
    grid,
    block_in,
    conditioning,
    cotangent,
    ada_weight,
    ada_bias,
    qkv_weight,
    qv_bias,
    out_weight,
    out_bias,
    up_weight,
    up_bias,
    down_weight,
    down_bias,
):
    grid.locate()
    size, at = grid.size, grid.at
    z_n, y_n, c_n, s_n = grid.shape
    _, rows, width = block_in.shape
    hidden = up_weight.shape[1]
    count = grid.count
    groups = c_n * s_n
    head_cols = width // groups
    short = width // count
    long = hidden // count
    block_cols = s_n * long
    half = hidden // 2
    own_group = at["c"] * s_n + at["s"]
    send = grid.send

    cond_own = conditioning[0].astype(F32)
    cond_act = jax.nn.silu(cond_own).astype(BF16)
    shares = jnp.concatenate([qv_bias, out_bias, up_bias, down_bias, cond_act])
    cols = qkv_weight.reshape(short, 3, groups, head_cols)
    blocks = []
    for c_d, s_d in np.ndindex(c_n, s_n):
        target = (at["c"] + c_d) % c_n * s_n + (at["s"] + s_d) % s_n
        part = lax.dynamic_index_in_dim(cols, target, 2, keepdims=False).reshape(short, 3 * head_cols)
        blocks.append(send(part, c=c_d, s=s_d) if c_d + s_d else part)
    x_own = block_in[0]
    shares = after(jnp.broadcast_to(shares[None], (count,) + shares.shape), *blocks)
    qkv_z = grid.gather(jnp.concatenate([block[None] for block in blocks]), "z")
    all_shares = lax.all_to_all(shares, AXES, 0, 0, tiled=True)
    x_all = grid.gather(after(x_own, all_shares), "s")
    cuts = np.cumsum([qv_bias.shape[0], out_bias.shape[0], up_bias.shape[0]])
    bias_cols = shares.shape[1] - width
    b_qv, b_out, b_up, b_down = [
        part.reshape(-1).astype(F32) for part in jnp.split(all_shares[:, :bias_cols], cuts, axis=1)
    ]

    cond_all = all_shares[:, bias_cols:].reshape(count // s_n, s_n, width)[:, 0]
    cond_flat = lax.dynamic_slice_in_dim(cond_all, grid.me * short, short, axis=1)
    bias_row = lax.dynamic_update_slice(
        jnp.zeros((6 * width,), F32), ada_bias.astype(F32), (grid.me * ada_bias.shape[0],)
    )
    terms = (dot(cond_flat, ada_weight, (1, 0)) + bias_row).reshape(count, 6 * width // s_n)
    terms = lax.all_to_all(after(terms, qkv_z), AXES, 0, 0, tiled=True)
    small_z = terms
    parts = grid.arrivals(after(qkv_z, terms), "y")
    terms = grid.gather(jnp.sum(terms, axis=0), "s")
    modulation = jnp.concatenate(
        [lax.dynamic_index_in_dim(terms, (at["s"] - s) % s_n, 0, keepdims=False) for s in range(s_n)]
    )
    shift_attn, scale_attn, gate_attn, shift_mlp, scale_mlp, gate_mlp = jnp.split(modulation, 6)

    jobs, table = [], []
    for i, back in enumerate(grid.steps("y", "z")):
        piece, block = divmod(i, z_n)
        for group, (c_d, s_d) in enumerate(np.ndindex(c_n, s_n)):
            jobs.append((piece, block * groups + group, 0, 0))
            table.append(grid.shard_of({**back, "c": c_d, "s": s_d}))
    w_qkv = place([part.reshape(-1, 1, short, 3 * head_cols) for part in parts], jobs, table)

    wide = half // width
    up_cols = up_weight.reshape(short, z_n * y_n, c_n, block_cols)
    up_own = lax.dynamic_index_in_dim(up_cols, at["c"], 2, keepdims=False).reshape(short, wide, width)
    up_other = lax.dynamic_index_in_dim(up_cols, 1 - at["c"], 2, keepdims=False).reshape(short, wide, width)
    up_other = send(after(up_other, x_all), c=1)
    units = [out_weight] + [rows_of[:, i] for rows_of in (up_own, up_other) for i in range(wide)]
    units = jnp.concatenate([unit[None] for unit in units])
    orders = (("s", "y"), ("y", "s"))
    units_z = grid.arrivals(after(units, small_z), "z")
    up_first = [
        grid.gather(jnp.concatenate([part[None, low:high] for part in units_z]), order[0])
        for low, high, order in ((0, 1 + wide, orders[0]), (1 + wide, 1 + 2 * wide, orders[1]))
    ]
    down_z = grid.arrivals(after(down_weight.reshape(2, long // 2, width), *up_first), "z")
    up_last = [grid.arrivals(after(part, *up_first), order[1]) for part, order in zip(up_first, orders)]
    down_first = [
        grid.gather(jnp.concatenate([part[None, i : i + 1] for part in down_z]), order[0])
        for i, order in enumerate(orders)
    ]

    inputs = x_own.astype(F32)
    normed_all, inverse_all = normalize(x_all.astype(F32))
    modded_all = (normed_all * (1.0 + scale_attn) + shift_attn).astype(BF16).reshape(s_n * rows, width)
    modded_all = jnp.concatenate([modded_all, send(modded_all, c=1)])
    q_bias = lax.dynamic_index_in_dim(b_qv[:width].reshape(groups, head_cols), own_group, 0, keepdims=False)
    v_bias = lax.dynamic_index_in_dim(b_qv[width:].reshape(groups, head_cols), own_group, 0, keepdims=False)
    qkv_bias = jnp.concatenate([q_bias, jnp.zeros_like(q_bias), v_bias])
    qkv = (dot(modded_all, w_qkv, (1, 0)) + qkv_bias).astype(BF16).reshape(c_n, s_n * rows, 3 * head_cols)
    attended_all, logsums = [], []
    for latent in range(c_n):
        qkv = after(qkv, *(attended_all + down_z if latent else up_first))
        part, logsum = attend(qkv, latent, head_cols)
        attended_all.append(part.reshape(s_n, rows, head_cols))
        logsums.append(logsum)
    arrived = []
    for c_d, s_d in np.ndindex(c_n, s_n):
        part = attended_all[c_d][s_d]
        if c_d + s_d:
            part = after(part, *attended_all)
        arrived.append(send(part, c=-c_d, s=-s_d) if c_d + s_d else part)
    up_steps = [grid.steps(order[1], order[0], "z") for order in orders]
    each = count // (c_n * grid.size["y"])
    flat_last = lax.optimization_barrier(tuple(part for parts in up_last for part in parts) + tuple(arrived))
    arrived = flat_last[-len(arrived) :]
    parts = [part.reshape((-1,) + part.shape[2:]) for part in flat_last[: -len(arrived)]]
    jobs, table, out_jobs, out_table = [], [], [], []
    first = 0
    for c_d, (last, steps) in enumerate(zip(up_last, up_steps)):
        per = len(steps) // len(last)
        for i, back in enumerate(steps):
            piece, block = divmod(i, per)
            for part in range(wide):
                jobs.append((first + piece, block, part + 1 - c_d, part))
                table.append(grid.shard_of({**back, "c": c_d}))
        first += len(last)
    out_own = jnp.concatenate([part[:, :1] for part in parts[: len(up_last[0])]])
    for c_d in range(c_n):
        for i, back in enumerate(up_steps[0]):
            out_jobs.append((c_d, i, 0, 0))
            out_table.append(grid.shard_of({**back, "c": c_d}))
    w_out = place([out_own, send(out_own, c=1)], out_jobs, out_table)
    w_up = place(parts, jobs, table)
    arrived = jnp.stack(arrived)
    ordered = []
    for c in range(c_n):
        for s in range(s_n):
            index = (c - at["c"]) % c_n * s_n + (s - at["s"]) % s_n
            ordered.append(lax.dynamic_index_in_dim(arrived, index, 0, keepdims=False))
    attended = jnp.concatenate(ordered, axis=1)
    attn_proj = dot(attended, w_out, (1, 0)) + b_out
    middle = inputs + gate_attn * attn_proj
    normed_mid, inverse_mid = normalize(middle)
    modded_mlp = (normed_mid * (1.0 + scale_mlp) + shift_mlp).astype(BF16)
    mlp_all = jnp.concatenate([modded_mlp, send(modded_mlp, c=1)])
    up_half = lax.dynamic_index_in_dim(b_up.reshape(-1, c_n, block_cols), at["c"], 1, keepdims=False).reshape(half)
    mlp_all = after(mlp_all, *down_first)
    down_last = [grid.arrivals(part, order[1]) for part, order in zip(down_first, orders)]
    pre_act = dot(mlp_all, w_up, (1, 0)) + up_half
    gelu_tanh = partial(jax.nn.gelu, approximate=True)
    activated = gelu_tanh(pre_act).astype(BF16)
    out_cot = cotangent[0].astype(F32)
    mlp_grad = (gate_mlp * out_cot).astype(BF16)
    mlp_grad_all = jnp.concatenate([mlp_grad, send(mlp_grad, c=1)])
    down_terms = dot(activated, mlp_grad_all, (0, 0), BF16).reshape(z_n, y_n, s_n, long, width)
    flat_last = lax.optimization_barrier((down_terms,) + tuple(part for parts in down_last for part in parts))
    down_terms = flat_last[0]
    down_a = grid.shed(down_terms[..., : long // 2, :], 2, "s")
    down_sent = grid.sent
    down_b = grid.shed(down_terms[..., long // 2 :, :], 1, "y")
    down_sent = down_sent + grid.sent
    parts = [part.reshape((-1,) + part.shape[2:]) for part in flat_last[1:]]
    jobs, table = [], []
    first = 0
    for row_half, (last, order) in enumerate(zip(down_last, orders)):
        steps = grid.steps(order[1], order[0], "z")
        per = len(steps) // len(last)
        for i, back in enumerate(steps):
            shard = grid.shard_of(back)
            piece, block = divmod(i, per)
            jobs.append((first + piece, block, 0, 0))
            table.append((shard // (c_n * s_n) * s_n + shard % s_n) * 2 + row_half)
        first += len(last)
    w_down = place(parts, jobs, table)
    proj_terms = dot(activated, w_down, (1, 0))
    mlp_proj = proj_terms[:rows] + send(proj_terms[rows:], c=1) + b_down
    block_out = (middle + gate_mlp * mlp_proj).astype(BF16)

    down_bias_grad = jnp.sum(mlp_grad.astype(F32), axis=0)
    act_grad = dot(after(mlp_grad_all, proj_terms, *down_sent), w_down, (1, 1))
    _, gelu_back = jax.vjp(gelu_tanh, pre_act)
    pre_grad = gelu_back(act_grad)[0].astype(BF16)
    up_bias_grad = jnp.sum(pre_grad.astype(F32), axis=0)
    down_a, down_b = settle(down_a, BF16, pre_grad), settle(down_b, BF16, pre_grad)
    up_terms = dot(after(mlp_all, down_a, down_b), pre_grad, (0, 0), BF16)
    up_terms = up_terms.reshape(z_n, y_n, c_n, s_n, short, half)
    up_a = grid.shed(lax.dynamic_index_in_dim(up_terms, at["c"], 2, keepdims=False), 1, "y")
    up_sent = grid.sent
    up_b = grid.shed(lax.dynamic_index_in_dim(up_terms, 1 - at["c"], 2, keepdims=False), 2, "s")
    up_sent = up_sent + grid.sent
    down_a, down_b = grid.shed(down_a, 1, "y"), grid.shed(down_b, 1, "s")
    mod_terms = dot(after(pre_grad, *up_sent), w_up, (1, 1))
    mlp_mod_grad = mod_terms[:rows] + send(mod_terms[rows:].astype(BF16), c=1).astype(F32)
    middle_part = normalize_back(mlp_mod_grad * (1.0 + scale_mlp), normed_mid, inverse_mid)
    shift_mlp_grad = jnp.sum(mlp_mod_grad, axis=0)
    scale_mlp_grad = jnp.sum(mlp_mod_grad * normed_mid, axis=0)
    middle_grad = out_cot + middle_part
    gate_mlp_grad = jnp.sum(out_cot * mlp_proj, axis=0)
    attn_grad = (gate_attn * middle_grad).astype(BF16)
    down_terms = jnp.concatenate([settle(part, BF16, attn_grad) for part in (down_a, down_b)], axis=1)
    up_a, up_b = settle(up_a, BF16, attn_grad), settle(up_b, BF16, attn_grad)
    attn_grad = after(attn_grad, down_terms, up_a, up_b)
    gate_attn_grad = jnp.sum(middle_grad * attn_proj, axis=0)
    out_bias_grad = jnp.sum(attn_grad.astype(F32), axis=0)
    attended_grad = dot(attn_grad, w_out, (1, 1), BF16)
    arrived = []
    for c_d in range(c_n):
        for s_d in range(s_n):
            target = (at["c"] + c_d) % c_n * s_n + (at["s"] + s_d) % s_n
            part = lax.dynamic_slice_in_dim(attended_grad, target * head_cols, head_cols, axis=1)
            arrived.append(send(part, c=c_d, s=s_d) if c_d + s_d else part)
    up_a, up_b = after(up_a, *arrived), after(up_b, *arrived)
    up_a, up_b = grid.shed(up_a, 1, "s"), grid.shed(up_b, 1, "y")
    down_terms = grid.shed(down_terms, 0, "z")
    out_terms = dot(attended, after(attn_grad, attended_grad), (0, 0), BF16)
    out_terms = out_terms.reshape(z_n, y_n, c_n, s_n, short, width)
    out_terms = grid.reduce(out_terms, 2, "c", BF16)
    up_terms = jnp.concatenate([settle(part, BF16, out_terms) for part in (up_a, up_b)], axis=1)
    out_terms = grid.shed(out_terms, 2, "s")
    out_sent = grid.sent
    up_terms = grid.shed(after(up_terms, *out_sent), 0, "z")
    up_sent = grid.sent
    qkv_grads = []
    for latent in range(c_n):
        grads = jnp.concatenate(arrived[latent * s_n : (latent + 1) * s_n])[None]
        if latent == 0:
            grads = after(grads, *out_sent, *up_sent)
        else:
            down_weight_grad = settle(down_terms, F32, *qkv_grads)
            out_terms = grid.shed(settle(out_terms, BF16, *qkv_grads), 1, "y")
            grads = after(grads, down_weight_grad, *grid.sent)
        qkv_grads.append(attend_back(qkv, grads, logsums[latent], latent, head_cols))
    qkv_grad = jnp.concatenate(qkv_grads).reshape(c_n * s_n * rows, 3 * head_cols)
    up_terms = settle(up_terms, F32, qkv_grad)
    out_terms = grid.shed(settle(out_terms, BF16, qkv_grad), 0, "z")
    qkv_grad = after(qkv_grad, up_terms, *grid.sent)
    mod_terms = dot(qkv_grad, w_qkv, (1, 1)).reshape(c_n, s_n, rows, width)
    mod_sent = mod_terms[1].astype(BF16)
    qkv_terms = dot(modded_all, after(qkv_grad, mod_sent), (0, 0), BF16)
    qkv_terms = qkv_terms.reshape(z_n, y_n, c_n, s_n, short, 3 * head_cols)
    qkv_terms = grid.shed(qkv_terms, 1, "y")
    out_weight_grad = settle(out_terms, F32, *grid.sent)
    mod_terms = after(mod_terms[0], out_weight_grad, *grid.sent)
    mod_sum = mod_terms + send(mod_sent, c=1).astype(F32)
    shift_attn_grad = jnp.sum(mod_sum, axis=(0, 1))
    scale_attn_grad = jnp.sum(mod_sum * normed_all, axis=(0, 1))
    column_sums = jnp.sum(qkv_grad.astype(F32), axis=0)
    arrived = [send(mod_sum[d].astype(BF16), s=-d) for d in range(1, s_n)]

    modulation_grad = jnp.concatenate(
        [shift_attn_grad, scale_attn_grad, gate_attn_grad, shift_mlp_grad, scale_mlp_grad, gate_mlp_grad]
    )
    def spread(value, index, n, axis):
        shape = value.shape[:axis] + (n,) + value.shape[axis:]
        start = tuple(index if i == axis else 0 for i in range(len(shape)))
        return lax.dynamic_update_slice(jnp.zeros(shape, F32), jnp.expand_dims(value, axis), start)

    q_sums = spread(column_sums[:head_cols], own_group, groups, 0).reshape(-1)
    v_sums = spread(column_sums[2 * head_cols :], own_group, groups, 0).reshape(-1)
    up_sums = spread(up_bias_grad.reshape(-1, block_cols), at["c"], c_n, 1).reshape(-1)
    total = jnp.concatenate([modulation_grad, q_sums, v_sums, out_bias_grad, up_sums, down_bias_grad])
    total = grid.sum_over(total, "s")
    total = grid.gather(total, "z")
    qkv_terms = settle(qkv_terms, BF16, total)
    qkv_terms = grid.shed(qkv_terms, 0, "z")
    total = grid.gather(after(total, *grid.sent), "c", "y")
    attn_mod_grad = mod_sum[0]
    for part in arrived:
        attn_mod_grad = attn_mod_grad + after(part, total).astype(F32)
    input_part = normalize_back(attn_mod_grad * (1.0 + scale_attn), normed_all[0], inverse_all[0])
    input_grad = (middle_grad + input_part).astype(BF16)
    z, y, c = ((at[name] - jnp.arange(size[name])) % size[name] for name in ("z", "y", "c"))
    latent = ((z[None, None] * y_n + y[None, :, None]) * c_n + c[:, None, None]).reshape(-1)
    cond_back = jnp.dot(jax.nn.one_hot(latent, count // s_n, dtype=BF16), cond_flat, preferred_element_type=F32)
    mod_grads = total.reshape(-1, total.shape[-1])[:, : 6 * width]
    bias_sums = jnp.sum(total.reshape(-1, total.shape[-1]), axis=0)

    def own_share(start, kept):
        return lax.dynamic_slice_in_dim(bias_sums[start : start + kept * count], grid.me * kept, kept)

    ada_bias_grad = own_share(0, ada_bias.shape[0])
    start = 6 * width
    bias_grads = []
    for bias in (qv_bias, out_bias, up_bias, down_bias):
        bias_grads.append(own_share(start, bias.shape[0]))
        start += bias.shape[0] * count
    qv_bias_grad, out_bias_grad, up_bias_grad, down_bias_grad = bias_grads
    ada_weight_grad = lax.dot_general(
        cond_back, mod_grads, (((0,), (0,)), ((), ())), precision=HIGHEST
    )
    cond_terms = lax.dot_general(
        mod_grads, ada_weight.astype(F32), (((1,), (1,)), ((), ())), precision=HIGHEST
    )
    cond_terms = after(cond_terms, input_grad)
    order = (latent[:, None] == jnp.arange(count // s_n)[None]).astype(F32)
    cond_terms = lax.dot_general(order, cond_terms, (((0,), (0,)), ((), ())), precision=HIGHEST)
    cond_terms = jnp.broadcast_to(cond_terms[:, None], (count // s_n, s_n, short)).reshape(count, short)
    cond_total = lax.all_to_all(cond_terms, AXES, 0, 0, tiled=True).reshape(width)
    qkv_terms = settle(qkv_terms, F32, cond_total)
    _, silu_back = jax.vjp(jax.nn.silu, cond_own)
    cond_grad = silu_back(cond_total)[0].astype(BF16)[None]

    up_first = up_terms[:short].reshape(short, -1, 1, block_cols)
    up_second = up_terms[short:].reshape(short, -1, 1, block_cols)
    up_second = send(up_second, c=1)
    even = at["c"] == 0
    up_weight_grad = jnp.concatenate(
        [jnp.where(even, up_first, up_second), jnp.where(even, up_second, up_first)], axis=2
    ).reshape(short, hidden)
    qkv_terms = qkv_terms.reshape(groups, short, 3 * head_cols)
    arrived, table = [], []
    for c_d, s_d in np.ndindex(c_n, s_n):
        target = (at["c"] + c_d) % c_n * s_n + (at["s"] + s_d) % s_n
        part = lax.dynamic_index_in_dim(qkv_terms, target, 0, keepdims=False)
        arrived.append(send(part, c=c_d, s=s_d) if c_d + s_d else part)
        table.append((at["c"] - c_d) % c_n * s_n + (at["s"] - s_d) % s_n)
    qkv_weight_grad = place_columns(arrived, table, head_cols)
    return (
        block_out[None],
        input_grad[None],
        cond_grad,
        ada_weight_grad,
        ada_bias_grad,
        qkv_weight_grad,
        qv_bias_grad,
        out_weight_grad,
        out_bias_grad,
        up_weight_grad,
        up_bias_grad,
        down_weight_grad,
        down_bias_grad,
    )


def solution(mesh):
    tokens = P("batch", "seq", None)
    vector = P("batch", None)
    matrix, line = P(AXES, None), P(AXES)
    in_specs = (tokens, vector, tokens) + (matrix, line) * 5
    out_specs = (tokens, tokens, vector) + (matrix, line) * 5
    return jax.shard_map(
        partial(local, Grid(mesh)), mesh=mesh, in_specs=in_specs, out_specs=out_specs, check_vma=False
    )
```

time: 716 us -> 534 us (0.75)
  waiting for transfers between devices: 313 us -> 120 us
  other arithmetic: 57.8 us -> 74.5 us
  matrix products: 83.9 us -> 72.9 us
  Pallas kernels: 70.8 us -> 79.1 us
  starting transfers between devices: 96.5 us -> 88.4 us
    ppermute x76 -> x73, waiting for transfers between devices: 313 us -> 109 us  [send(): return lax.ppermute(value, AXES, pairs)]
    ppermute x76 -> x73, starting transfers between devices: 96.5 us -> 73 us  [send(): return lax.ppermute(value, AXES, pairs)]
    all_to_all x0 -> x3, starting transfers between devices: none -> 15.5 us  [the longest x1 7.4 us: local(): terms = lax.all_to_all(after(terms, qkv_z), AXES, 0, 0, tiled=True)]
    dynamic_slice x13 -> x1, local copies, waits for them, and re-layouts: 13.6 us -> 0.15 us  [local(): lax.dynamic_slice_in_dim(attended_grad, target * head_cols, head_cols, ax...]
    dot_general x13, matrix products: 80.3 us -> 69 us  [dot(): lax.dot_general(left, right, ((dims[:1], dims[1:]), ((), ())), preferred_...]
    all_to_all x0 -> x3, waiting for transfers between devices: none -> 10.6 us  [the longest x1 6.56 us: local(): terms = lax.all_to_all(after(terms, qkv_z), AXES, 0, 0, tiled=True)]
    squeeze x10 -> x18, local copies, waits for them, and re-layouts: 4.33 us -> 13.1 us  [the longest x15 9.72 us: shed(): lax.dynamic_index_in_dim(terms, (me + d) % n, axis, keepdims=False)]
    concatenate x7 -> x13, other arithmetic: 6.17 us -> 14.4 us  [the longest x8 7.6 us: gather(): jnp.concatenate([part[None] for part in self.arrivals(value, *names)])]
  transfers between devices with their start and end apart: 76 -> 76, of which waited for: 33 -> 31; matrix products, arithmetic and copies ran while one was open for 22% -> 36% of each run, Pallas kernels for 10% -> 14%
where the time goes in v2:
time: 534 us; the launch traced here: 524 us
  waiting for transfers between devices  120 us (22%)
  starting transfers between devices  88.4 us (17%)
  local copies, waits for them, and re-layouts  85.5 us (16%)
  Pallas kernels  79.1 us (15%)
  other arithmetic  74.5 us (14%)
  matrix products  72.9 us (14%)
    ppermute x73, waiting for transfers between devices, send(): return lax.ppermute(value, AXES, pairs)  109 us
    ppermute x73, starting transfers between devices, send(): return lax.ppermute(value, AXES, pairs)  73 us
    dot_general x13, matrix products, dot(): lax.dot_general(left, right, ((dims[:1], dims[1:]), ((), ())), preferred_...  69 us
    pallas_call x2, Pallas kernels, attend_back(): pl.pallas_call(partial(attend_back_kernel, width), grid=(1,), in_specs=[s...  36.7 us
    unnamed x243, local copies, waits for them, and re-layouts  23.8 us
    pallas_call x2, Pallas kernels, attend(): pl.pallas_call(partial(attend_kernel, width), grid=(1,), in_specs=[spec(3...  21.9 us
    pallas_call x4, Pallas kernels, place(): pl.pallas_call(partial(place_kernel, jobs, flat), out_shape=jax.ShapeDtyp...  18 us
  transfers between devices with their start and end apart: 76, of which 31 were waited for; matrix products, arithmetic and copies ran while one was open for 36% of the time, Pallas kernels for 14%

profile of v2, /device:TPU:0, one launch (start us, length us, event | category | flops | bytes accessed | tf_op | source)
XLA Modules:
  0.0 523.9 jit_solution(10152591457407810410)
XLA Ops:
  14.6 5.3 %all-to-all-start = ((bf16[32,2,640]{2,1,0:T(2,128)(2,1)}), bf16[32,2,640]{2,1,0:T(2,128)(2,1)S(1)}, u32[]{:S(2)}, u32[]{:S(2)}) async-start(bf16[32,2,640]{2,1,0:T(2,128)(2,1)} %reshape.482), calls=%async_computation | async-start | bytes 163840 | tf_op jit(solution)/shard_map/all_to_all | solution.py:316
  30.7 7.9 %collective-permute-done.4 = bf16[4,32,768]{2,1,0:T(8,128)(2,1)S(1)} collective-permute-done((bf16[4,32,768]{2,1,0:T(8,128)(2,1)S(1)}, bf16[4,32,768]{2,1,0:T(8,128)(2,1)S(1)}, u32[]{:S(2)}, u32[]{:S(2)}) %collective-permute-start.4) | collective-permute-done | bytes 196640 | tf_op jit(solution)/shard_map/ppermute | solution.py:70
  41.5 7.4 %all-to-all-start.1 = ((f32[32,1,3072]{2,1,0:T(1,128)}), f32[32,1,3072]{2,1,0:T(1,128)}, u32[]{:S(2)}, u32[]{:S(2)}) async-start(f32[32,1,3072]{2,1,0:T(1,128)} %all_to_all.25), calls=%async_computation.1 | async-start | bytes 786432 | tf_op jit(solution)/shard_map/all_to_all | solution.py:330
  55.1 6.6 %all-to-all-done.1 = f32[32,1,3072]{2,1,0:T(1,128)} async-done(((f32[32,1,3072]{2,1,0:T(1,128)}), f32[32,1,3072]{2,1,0:T(1,128)}, u32[]{:S(2)}, u32[]{:S(2)}) %all-to-all-start.1) | async-done | bytes 393248 | tf_op jit(solution)/shard_map/all_to_all | solution.py:330
  68.8 10.6 %collective-permute-done.6 = f32[3072]{0:T(1024)S(1)} collective-permute-done((f32[3072]{0:T(1024)S(1)}, f32[3072]{0:T(1024)S(1)}, u32[]{:S(2)}, u32[]{:S(2)}) %collective-permute-start.6) | collective-permute-done | bytes 12320 | tf_op jit(solution)/shard_map/ppermute | solution.py:70
  87.6 5.5 %collective-permute-done.10 = bf16[5,32,1024]{2,1,0:T(8,128)(2,1)} collective-permute-done((bf16[5,32,1024]{2,1,0:T(8,128)(2,1)}, bf16[5,32,1024]{2,1,0:T(8,128)(2,1)}, u32[]{:S(2)}, u32[]{:S(2)}) %collective-permute-start.10) | collective-permute-done | bytes 327712 | tf_op jit(solution)/shard_map/ppermute | solution.py:70
  112.3 7.6 %collective-permute-done.12 = bf16[4,3,32,1024]{3,2,1,0:T(8,128)(2,1)} collective-permute-done((bf16[4,3,32,1024]{3,2,1,0:T(8,128)(2,1)}, bf16[4,3,32,1024]{3,2,1,0:T(8,128)(2,1)}, u32[]{:S(2)}, u32[]{:S(2)}) %collective-permute-start.12) | collective-permute-done | bytes 786464 | tf_op jit(solution)/shard_map/ppermute | solution.py:70
  127.3 7.4 %add_convert_fusion = bf16[2048,768]{1,0:T(8,128)(2,1)} fusion(bf16[1024,768]{1,0:T(8,128)(2,1)S(1)} %copy-done.35, f32[768]{0:T(1024)S(1)} %pad_maximum_fusion.29, bf16[1024,1024]{1,0:T(8,128)(2,1)} %collective-permute-done.16, bf16[1024,1024]{1,0:T(8,128)(2,1)} %fusion.10), kind=kOutput, calls=%fused_computation.13 | convolution fusion | flops 3232759808 | bytes 8915968 | tf_op jit(solution)/shard_map/dot_general | solution.py:22
  134.7 10.7 %shard_map.229 = (bf16[1,1024,256]{2,1,0:T(8,128)(2,1)}, f32[1,1024,256]{2,1,0:T(8,128)}) custom-call(bf16[2,1024,768]{2,1,0:T(8,128)(2,1)} %bitcast.403), custom_call_target="tpu_custom_call" | custom-call | flops 268435456 | bytes 3145728 | tf_op jit(solution)/shard_map/pallas_call | solution.py:203
  146.8 11.2 %shard_map.230 = (bf16[1,1024,256]{2,1,0:T(8,128)(2,1)}, f32[1,1024,256]{2,1,0:T(8,128)}) custom-call(bf16[2,1024,768]{2,1,0:T(8,128)(2,1)} %bitcast.404), custom_call_target="tpu_custom_call" | custom-call | flops 268435456 | bytes 3145728 | tf_op jit(solution)/shard_map/pallas_call | solution.py:203
  168.5 5.9 %collective-permute-done.21 = bf16[512,256]{1,0:T(8,128)(2,1)} collective-permute-done((bf16[512,256]{1,0:T(8,128)(2,1)}, bf16[512,256]{1,0:T(8,128)(2,1)}, u32[]{:S(2)}, u32[]{:S(2)}) %collective-permute-start.21) | collective-permute-done | bytes 262176 | tf_op jit(solution)/shard_map/ppermute | solution.py:70
  201.1 5.5 %collective-permute-done.27 = bf16[4,1,64,1024]{3,2,0,1:T(8,128)(2,1)} collective-permute-done((bf16[4,1,64,1024]{3,2,0,1:T(8,128)(2,1)}, bf16[4,1,64,1024]{3,2,0,1:T(8,128)(2,1)}, u32[]{:S(2)}, u32[]{:S(2)}) %collective-permute-start.27) | collective-permute-done | bytes 524320 | tf_op jit(solution)/shard_map/ppermute | solution.py:70
  210.7 5.4 %shard_map.232 = bf16[1024,2048]{1,0:T(8,128)(2,1)} custom-call(s32[64]{0:T(128)} %stack.369.table, bf16[8,3,32,1024]{3,2,1,0:T(8,128)(2,1)} %bitcast.417, bf16[8,3,32,1024]{3,2,1,0:T(8,128)(2,1)} %bitcast.86.refs_1_, bf16[8,2,32,1024]{3,2,1,0:T(8,128)(2,1)} %bitcast.106.refs_2_, bf16[8,2,32,1024]{3,2,1,0:T(8,128)(2,1)} %bitcast.107.refs_3_), custom_call_target="tpu_custom_call" | custom-call | bytes 8388608 | tf_op jit(solution)/shard_map/pallas_call | solution.py:123
  223.4 9.2 %convolution_convert_fusion.1 = bf16[2048,1024]{1,0:T(8,128)(2,1)S(1)} fusion(bf16[512,1024]{1,0:T(8,128)(2,1)} %collective-permute-done.28, bf16[512,1024]{1,0:T(8,128)(2,1)} %get-tuple-element.200, f32[1024,2048]{1,0:T(8,128)S(1)} %fusion.77, f32[2048]{0:T(1024)S(1)} %bitcast.489), kind=kOutput, calls=%fused_computation.27 | convolution fusion | flops 4322230272 | bytes 14688256 | tf_op jit(solution)/shard_map/dot_general | solution.py:22
  241.6 9.2 %fusion.66 = f32[1024,1024]{1,0:T(8,128)S(1)} fusion(bf16[2048,1024]{1,0:T(8,128)(2,1)} %shard_map.233, f32[1024,2048]{1,0:T(8,128)} %copy-done.106, f32[2048]{0:T(1024)S(1)} %bitcast.490), kind=kOutput, calls=%fused_computation.289 | convolution fusion | flops 4315938816 | bytes 16785408 | tf_op jit(solution)/shard_map/dot_general | solution.py:22
  256.5 12.4 %convert_reduce_fusion = (f32[2048]{0:T(1024)}, bf16[1024,2048]{1,0:T(8,128)(2,1)S(1)}) fusion(f32[1024,2048]{1,0:T(8,128)} %copy-done.106, f32[2048]{0:T(1024)S(1)} %bitcast.491, bf16[1024,1024]{1,0:T(8,128)(2,1)S(1)} %copy-done.30, bf16[2048,1024]{1,0:T(8,128)(2,1)S(1)} %copy-done.24), kind=kOutput, calls=%fused_computation.9 | convolution fusion | flops 4343199744 | bytes 18890752 | tf_op jit(solution)/shard_map/dot_general | solution.py:22
  268.8 7.8 %collective-permute-done.33 = bf16[4,2,64,1024]{3,2,1,0:T(8,128)(2,1)S(1)} collective-permute-done((bf16[4,2,64,1024]{3,2,1,0:T(8,128)(2,1)S(1)}, bf16[4,2,64,1024]{3,2,1,0:T(8,128)(2,1)S(1)}, u32[]{:S(2)}, u32[]{:S(2)}) %collective-permute-start.33) | collective-permute-done | bytes 1048608 | tf_op jit(solution)/shard_map/ppermute | solution.py:70
  280.4 5.3 %convolution_convert_fusion = bf16[1024,2048]{1,0:T(8,128)(2,1)S(1)} fusion(bf16[1024,1024]{1,0:T(8,128)(2,1)S(1)} %copy-done.32, bf16[1024,2048]{1,0:T(8,128)(2,1)S(1)} %get-tuple-element.135), kind=kOutput, calls=%fused_computation.26 | convolution fusion | flops 4297064448 | bytes 10485760 | tf_op jit(solution)/shard_map/dot_general | solution.py:22
  321.4 10.8 %collective-permute-done.38 = bf16[4,2,32,2048]{3,2,1,0:T(8,128)(2,1)S(1)} collective-permute-done((bf16[4,2,32,2048]{3,2,1,0:T(8,128)(2,1)}, bf16[4,2,32,2048]{3,2,1,0:T(8,128)(2,1)S(1)}, u32[]{:S(2)}, u32[]{:S(2)}) %collective-permute-start.38) | collective-permute-done | bytes 1048608 | tf_op jit(solution)/shard_map/ppermute | solution.py:70
  359.5 8.9 %collective-permute-done.43 = bf16[4,32,2048]{2,1,0:T(8,128)(2,1)S(1)} collective-permute-done((bf16[4,32,2048]{2,1,0:T(8,128)(2,1)S(1)}, bf16[4,32,2048]{2,1,0:T(8,128)(2,1)S(1)}, u32[]{:S(2)}, u32[]{:S(2)}) %collective-permute-start.43) | collective-permute-done | bytes 524320 | tf_op jit(solution)/shard_map/ppermute | solution.py:70
  371.9 18.2 %shard_map.234 = bf16[1,1024,768]{2,1,0:T(8,128)(2,1)} custom-call(bf16[2,1024,768]{2,1,0:T(8,128)(2,1)} %bitcast.405, bf16[1,1024,256]{2,1,0:T(8,128)(2,1)} %maximum_bitcast_fusion.grads, f32[1,1024,256]{2,1,0:T(8,128)} %get-tuple-element.154.logsum), custom_call_target="tpu_custom_call" | custom-call | flops 536870912 | bytes 4718592 | tf_op jit(solution)/shard_map/pallas_call | solution.py:257
  396.9 18.5 %shard_map.235 = bf16[1,1024,768]{2,1,0:T(8,128)(2,1)} custom-call(bf16[2,1024,768]{2,1,0:T(8,128)(2,1)} %bitcast.406, bf16[1,1024,256]{2,1,0:T(8,128)(2,1)} %maximum_bitcast_fusion.1.grads, f32[1,1024,256]{2,1,0:T(8,128)} %get-tuple-element.162.logsum), custom_call_target="tpu_custom_call" | custom-call | flops 536870912 | bytes 4718592 | tf_op jit(solution)/shard_map/pallas_call | solution.py:257
  436.2 6.1 %fusion.18 = bf16[1024,768]{1,0:T(8,128)(2,1)S(1)} fusion(bf16[2048,768]{1,0:T(8,128)(2,1)S(1)} %bitcast.415, bf16[1024,1024]{1,0:T(8,128)(2,1)} %collective-permute-done.16, bf16[1024,1024]{1,0:T(8,128)(2,1)} %fusion.10), kind=kOutput, calls=%fused_computation.68 | convolution fusion | flops 3230400512 | bytes 8912896 | tf_op jit(solution)/shard_map/dot_general | solution.py:22
  453.7 5.9 %multiply_reduce_fusion = (f32[1024]{0:T(1024)S(1)}, f32[1024]{0:T(1024)S(1)}, f32[2,512,1024]{2,1,0:T(8,128)}, f32[2,512,1024]{2,1,0:T(8,128)}) fusion(f32[2,512]{1,0:T(2,128)} %get-tuple-element.309, f32[2,512]{1,0:T(2,128)} %copy-done.74, bf16[1,512,1024]{2,1,0:T(8,128)(2,1)S(1)} %bitcast.412, bf16[1,512,1024]{2,1,0:T(8,128)(2,1)S(1)} %copy-done.4, ...), kind=kLoop, calls=%fused_computation.21 | loop fusion | flops 9435136 | bytes 16793600 | tf_op jit(solution)/shard_map/reduce_sum | solution.py:521
  (582 shorter events, 310.9 us)
Async XLA Ops:
  4.3 46.1 %collective-permute-start.8 = (bf16[32,2,1024]{2,0,1:T(8,128)(2,1)}, bf16[32,2,1024]{2,0,1:T(8,128)(2,1)}, u32[]{:S(2)}, u32[]{:S(2)}) collective-permute-start(bf16[32,2,1024]{2,0,1:T(8,128)(2,1)} %copy.94), channel_id=1, source_target_pairs={{0,2},{1,3},{2,0},{3,1},{4,6},{5,7},{6,4},{7,5},{8,10},{9,11},{10,... | collective-permute-start | bytes 393224 | tf_op jit(solution)/shard_map/ppermute | solution.py:70
  52.0 29.9 %collective-permute-start.7 = (bf16[512,1024]{1,0:T(8,128)(2,1)S(1)}, bf16[512,1024]{1,0:T(8,128)(2,1)S(1)}, u32[]{:S(2)}, u32[]{:S(2)}) collective-permute-start(bf16[512,1024]{1,0:T(8,128)(2,1)S(1)} %bitcast.408), channel_id=1, source_target_pairs={{0,1},{1,0},{2,3},{3,2},{4,5},{5,4},{6,7},{7,6},{8,9},{9,8},{10,11... | collective-permute-start | bytes 3145736 | tf_op jit(solution)/shard_map/ppermute | solution.py:70
  62.7 30.5 %collective-permute-start.10 = (bf16[5,32,1024]{2,1,0:T(8,128)(2,1)}, bf16[5,32,1024]{2,1,0:T(8,128)(2,1)}, u32[]{:S(2)}, u32[]{:S(2)}) collective-permute-start(bf16[5,32,1024]{2,1,0:T(8,128)(2,1)} %fusion.35), channel_id=1, source_target_pairs={{0,16},{1,17},{2,18},{3,19},{4,20},{5,21},{6,22},{7,23},{8,24},{9,... | collective-permute-start | bytes 983048 | tf_op jit(solution)/shard_map/ppermute | solution.py:70
  63.5 30.6 %collective-permute-start.9 = (bf16[5,32,1024]{2,1,0:T(8,128)(2,1)}, bf16[5,32,1024]{2,1,0:T(8,128)(2,1)}, u32[]{:S(2)}, u32[]{:S(2)}) collective-permute-start(bf16[5,32,1024]{2,1,0:T(8,128)(2,1)} %fusion.35), channel_id=1, source_target_pairs={{0,8},{1,9},{2,10},{3,11},{4,12},{5,13},{6,14},{7,15},{8,16},{9,17... | collective-permute-start | bytes 983048 | tf_op jit(solution)/shard_map/ppermute | solution.py:70
  86.7 39.7 %collective-permute-start.16 = (bf16[1024,1024]{1,0:T(8,128)(2,1)}, bf16[1024,1024]{1,0:T(8,128)(2,1)}, u32[]{:S(2)}, u32[]{:S(2)}) collective-permute-start(bf16[1024,1024]{1,0:T(8,128)(2,1)} %fusion.10), channel_id=1, source_target_pairs={{0,2},{1,3},{2,0},{3,1},{4,6},{5,7},{6,4},{7,5},{8,10},{9,11},{10,... | collective-permute-start | bytes 6291464 | tf_op jit(solution)/shard_map/ppermute | solution.py:70
  125.3 41.2 %collective-permute-start.15 = (bf16[2,4,2,32,1024]{4,3,2,1,0:T(8,128)(2,1)}, bf16[2,4,2,32,1024]{4,3,2,1,0:T(8,128)(2,1)}, u32[]{:S(2)}, u32[]{:S(2)}) collective-permute-start(bf16[2,4,2,32,1024]{4,3,2,1,0:T(8,128)(2,1)} %pad_maximum_fusion.11), channel_id=1, source_target_pairs={{0,1},{1,0},{2,3},{3,2},{4,5},{5,4},{6,7},{7,6},{8,9},{9,8},{10,11... | collective-permute-start | bytes 3145736 | tf_op jit(solution)/shard_map/ppermute | solution.py:70
  126.4 48.0 %collective-permute-start.14 = (bf16[2,4,3,32,1024]{4,3,2,1,0:T(8,128)(2,1)S(1)}, bf16[2,4,3,32,1024]{4,3,2,1,0:T(8,128)(2,1)}, u32[]{:S(2)}, u32[]{:S(2)}) collective-permute-start(bf16[2,4,3,32,1024]{4,3,2,1,0:T(8,128)(2,1)S(1)} %pad_maximum_fusion.10), channel_id=1, source_target_pairs={{0,4},{1,5},{2,6},{3,7},{4,0},{5,1},{6,2},{7,3},{8,12},{9,13},{10,... | collective-permute-start | bytes 4718600 | tf_op jit(solution)/shard_map/ppermute | solution.py:70
  256.1 60.0 %collective-permute-start.31 = (f32[512,1024]{1,0:T(8,128)}, f32[512,1024]{1,0:T(8,128)}, u32[]{:S(2)}, u32[]{:S(2)}) collective-permute-start(f32[512,1024]{1,0:T(8,128)} %slice.262), channel_id=1, source_target_pairs={{0,2},{1,3},{2,0},{3,1},{4,6},{5,7},{6,4},{7,5},{8,10},{9,11},{10,... | collective-permute-start | bytes 6291464 | tf_op jit(solution)/shard_map/ppermute | solution.py:70
  306.0 26.2 %collective-permute-start.38 = (bf16[4,2,32,2048]{3,2,1,0:T(8,128)(2,1)}, bf16[4,2,32,2048]{3,2,1,0:T(8,128)(2,1)S(1)}, u32[]{:S(2)}, u32[]{:S(2)}) collective-permute-start(bf16[4,2,32,2048]{3,2,1,0:T(8,128)(2,1)} %get-tuple-element.211), channel_id=1, source_target_pairs={{0,1},{1,0},{2,3},{3,2},{4,5},{5,4},{6,7},{7,6},{8,9},{9,8},{10,11... | collective-permute-start | bytes 3145736 | tf_op jit(solution)/shard_map/ppermute | solution.py:70
  306.9 26.2 %collective-permute-start.37 = (bf16[4,2,32,2048]{3,2,1,0:T(8,128)(2,1)}, bf16[4,2,32,2048]{3,2,1,0:T(8,128)(2,1)S(1)}, u32[]{:S(2)}, u32[]{:S(2)}) collective-permute-start(bf16[4,2,32,2048]{3,2,1,0:T(8,128)(2,1)} %get-tuple-element.213), channel_id=1, source_target_pairs={{0,4},{1,5},{2,6},{3,7},{4,0},{5,1},{6,2},{7,3},{8,12},{9,13},{10,... | collective-permute-start | bytes 3145736 | tf_op jit(solution)/shard_map/ppermute | solution.py:70
  309.9 33.5 %collective-permute-start.36 = (bf16[4,64,1024]{2,1,0:T(8,128)(2,1)S(1)}, bf16[4,64,1024]{2,1,0:T(8,128)(2,1)S(1)}, u32[]{:S(2)}, u32[]{:S(2)}) collective-permute-start(bf16[4,64,1024]{2,1,0:T(8,128)(2,1)S(1)} %get-tuple-element.243), channel_id=1, source_target_pairs={{0,1},{1,0},{2,3},{3,2},{4,5},{5,4},{6,7},{7,6},{8,9},{9,8},{10,11... | collective-permute-start | bytes 1572872 | tf_op jit(solution)/shard_map/ppermute | solution.py:70
  312.3 31.4 %collective-permute-start.35 = (bf16[4,64,1024]{2,1,0:T(8,128)(2,1)S(1)}, bf16[4,64,1024]{2,1,0:T(8,128)(2,1)S(1)}, u32[]{:S(2)}, u32[]{:S(2)}) collective-permute-start(bf16[4,64,1024]{2,1,0:T(8,128)(2,1)S(1)} %get-tuple-element.245), channel_id=1, source_target_pairs={{0,4},{1,5},{2,6},{3,7},{4,0},{5,1},{6,2},{7,3},{8,12},{9,13},{10,... | collective-permute-start | bytes 1572872 | tf_op jit(solution)/shard_map/ppermute | solution.py:70
  344.1 46.0 %collective-permute-start.45 = (bf16[128,1024]{1,0:T(8,128)(2,1)S(1)}, bf16[128,1024]{1,0:T(8,128)(2,1)S(1)}, u32[]{:S(2)}, u32[]{:S(2)}) collective-permute-start(bf16[128,1024]{1,0:T(8,128)(2,1)S(1)} %get-tuple-element.240), channel_id=1, source_target_pairs={{0,8},{1,9},{2,10},{3,11},{4,12},{5,13},{6,14},{7,15},{8,16},{9,17... | collective-permute-start | bytes 786440 | tf_op jit(solution)/shard_map/ppermute | solution.py:70
  349.1 42.2 %collective-permute-start.46 = (bf16[128,1024]{1,0:T(8,128)(2,1)S(1)}, bf16[128,1024]{1,0:T(8,128)(2,1)S(1)}, u32[]{:S(2)}, u32[]{:S(2)}) collective-permute-start(bf16[128,1024]{1,0:T(8,128)(2,1)S(1)} %get-tuple-element.241), channel_id=1, source_target_pairs={{0,16},{1,17},{2,18},{3,19},{4,20},{5,21},{6,22},{7,23},{8,24},{9,... | collective-permute-start | bytes 786440 | tf_op jit(solution)/shard_map/ppermute | solution.py:70
  358.5 35.8 %collective-permute-start.47 = (bf16[128,1024]{1,0:T(8,128)(2,1)S(1)}, bf16[128,1024]{1,0:T(8,128)(2,1)S(1)}, u32[]{:S(2)}, u32[]{:S(2)}) collective-permute-start(bf16[128,1024]{1,0:T(8,128)(2,1)S(1)} %get-tuple-element.239), channel_id=1, source_target_pairs={{0,24},{1,25},{2,26},{3,27},{4,28},{5,29},{6,30},{7,31},{8,0},{9,1... | collective-permute-start | bytes 786440 | tf_op jit(solution)/shard_map/ppermute | solution.py:70
  369.1 26.1 %collective-permute-start.48 = (bf16[4,2,32,1024]{3,2,1,0:T(8,128)(2,1)S(1)}, bf16[4,2,32,1024]{3,2,1,0:T(8,128)(2,1)S(1)}, u32[]{:S(2)}, u32[]{:S(2)}) collective-permute-start(bf16[4,2,32,1024]{3,2,1,0:T(8,128)(2,1)S(1)} %get-tuple-element.230), channel_id=1, source_target_pairs={{0,1},{1,0},{2,3},{3,2},{4,5},{5,4},{6,7},{7,6},{8,9},{9,8},{10,11... | collective-permute-start | bytes 1572872 | tf_op jit(solution)/shard_map/ppermute | solution.py:70
  370.8 46.3 %collective-permute-start.49 = (bf16[64,2048]{1,0:T(8,128)(2,1)S(1)}, bf16[64,2048]{1,0:T(8,128)(2,1)S(1)}, u32[]{:S(2)}, u32[]{:S(2)}) collective-permute-start(bf16[64,2048]{1,0:T(8,128)(2,1)S(1)} %get-tuple-element.228), channel_id=1, source_target_pairs={{0,8},{1,9},{2,10},{3,11},{4,12},{5,13},{6,14},{7,15},{8,16},{9,17... | collective-permute-start | bytes 786440 | tf_op jit(solution)/shard_map/ppermute | solution.py:70
  390.1 27.0 %collective-permute-start.50 = (bf16[64,2048]{1,0:T(8,128)(2,1)S(1)}, bf16[64,2048]{1,0:T(8,128)(2,1)S(1)}, u32[]{:S(2)}, u32[]{:S(2)}) collective-permute-start(bf16[64,2048]{1,0:T(8,128)(2,1)S(1)} %get-tuple-element.227), channel_id=1, source_target_pairs={{0,16},{1,17},{2,18},{3,19},{4,20},{5,21},{6,22},{7,23},{8,24},{9,... | collective-permute-start | bytes 786440 | tf_op jit(solution)/shard_map/ppermute | solution.py:70
  391.3 25.8 %collective-permute-start.51 = (bf16[64,2048]{1,0:T(8,128)(2,1)S(1)}, bf16[64,2048]{1,0:T(8,128)(2,1)S(1)}, u32[]{:S(2)}, u32[]{:S(2)}) collective-permute-start(bf16[64,2048]{1,0:T(8,128)(2,1)S(1)} %get-tuple-element.226), channel_id=1, source_target_pairs={{0,24},{1,25},{2,26},{3,27},{4,28},{5,29},{6,30},{7,31},{8,0},{9,1... | collective-permute-start | bytes 786440 | tf_op jit(solution)/shard_map/ppermute | solution.py:70
  427.2 26.4 %collective-permute-start.56 = (bf16[2,512,1024]{2,1,0:T(8,128)(2,1)}, bf16[2,512,1024]{2,1,0:T(8,128)(2,1)}, u32[]{:S(2)}, u32[]{:S(2)}) collective-permute-start(bf16[2,512,1024]{2,1,0:T(8,128)(2,1)} %bitcast.190), channel_id=1, source_target_pairs={{0,2},{1,3},{2,0},{3,1},{4,6},{5,7},{6,4},{7,5},{8,10},{9,11},{10,... | collective-permute-start | bytes 6291464 | tf_op jit(solution)/shard_map/ppermute | solution.py:70
  428.3 32.3 %collective-permute-start.72 = (f32[32,8,1,256]{3,2,1,0:T(1,128)}, f32[32,8,1,256]{3,2,1,0:T(1,128)}, u32[]{:S(2)}, u32[]{:S(2)}) collective-permute-start(f32[32,8,1,256]{3,2,1,0:T(1,128)} %reshape.457), channel_id=1, source_target_pairs={{0,2},{1,3},{2,0},{3,1},{4,6},{5,7},{6,4},{7,5},{8,10},{9,11},{10,... | collective-permute-start | bytes 786440 | tf_op jit(solution)/shard_map/ppermute | solution.py:70
  489.0 28.6 %collective-permute-start.69 = (f32[32,768]{1,0:T(8,128)}, f32[32,768]{1,0:T(8,128)}, u32[]{:S(2)}, u32[]{:S(2)}) collective-permute-start(f32[32,768]{1,0:T(8,128)} %get-tuple-element.275), channel_id=1, source_target_pairs={{0,1},{1,0},{2,3},{3,2},{4,5},{5,4},{6,7},{7,6},{8,9},{9,8},{10,11... | collective-permute-start | bytes 294920 | tf_op jit(solution)/shard_map/ppermute | solution.py:70
  490.1 27.5 %collective-permute-start.70 = (f32[32,768]{1,0:T(8,128)}, f32[32,768]{1,0:T(8,128)}, u32[]{:S(2)}, u32[]{:S(2)}) collective-permute-start(f32[32,768]{1,0:T(8,128)} %get-tuple-element.274), channel_id=1, source_target_pairs={{0,2},{1,3},{2,0},{3,1},{4,6},{5,7},{6,4},{7,5},{8,10},{9,11},{10,... | collective-permute-start | bytes 294920 | tf_op jit(solution)/shard_map/ppermute | solution.py:70
  490.4 27.2 %collective-permute-start.71 = (f32[32,768]{1,0:T(8,128)}, f32[32,768]{1,0:T(8,128)}, u32[]{:S(2)}, u32[]{:S(2)}) collective-permute-start(f32[32,768]{1,0:T(8,128)} %get-tuple-element.273), channel_id=1, source_target_pairs={{0,3},{1,2},{2,1},{3,0},{4,7},{5,6},{6,5},{7,4},{8,11},{9,10},{10,... | collective-permute-start | bytes 294920 | tf_op jit(solution)/shard_map/ppermute | solution.py:70
  (161 other events, 1736.6 us)

commit v3 on v2

--- a/solution.py
+++ b/solution.py
@@ -314,7 +314,8 @@
     shares = after(jnp.broadcast_to(shares[None], (count,) + shares.shape), *blocks)
     qkv_z = grid.gather(jnp.concatenate([block[None] for block in blocks]), "z")
     all_shares = lax.all_to_all(shares, AXES, 0, 0, tiled=True)
-    x_all = grid.gather(after(x_own, all_shares), "s")
+    x_all = grid.gather(x_own, "s")
+    all_shares = after(all_shares, x_all)
     cuts = np.cumsum([qv_bias.shape[0], out_bias.shape[0], up_bias.shape[0]])
     bias_cols = shares.shape[1] - width
     b_qv, b_out, b_up, b_down = [
@@ -354,16 +355,9 @@
     orders = (("s", "y"), ("y", "s"))
     units_z = grid.arrivals(after(units, small_z), "z")
     up_first = [
-        grid.gather(jnp.concatenate([part[None, low:high] for part in units_z]), order[0])
+        grid.arrivals(jnp.concatenate([part[None, low:high] for part in units_z]), order[0])
         for low, high, order in ((0, 1 + wide, orders[0]), (1 + wide, 1 + 2 * wide, orders[1]))
     ]
-    down_z = grid.arrivals(after(down_weight.reshape(2, long // 2, width), *up_first), "z")
-    up_last = [grid.arrivals(after(part, *up_first), order[1]) for part, order in zip(up_first, orders)]
-    down_first = [
-        grid.gather(jnp.concatenate([part[None, i : i + 1] for part in down_z]), order[0])
-        for i, order in enumerate(orders)
-    ]
-
     inputs = x_own.astype(F32)
     normed_all, inverse_all = normalize(x_all.astype(F32))
     modded_all = (normed_all * (1.0 + scale_attn) + shift_attn).astype(BF16).reshape(s_n * rows, width)
@@ -372,6 +366,13 @@
     v_bias = lax.dynamic_index_in_dim(b_qv[width:].reshape(groups, head_cols), own_group, 0, keepdims=False)
     qkv_bias = jnp.concatenate([q_bias, jnp.zeros_like(q_bias), v_bias])
     qkv = (dot(modded_all, w_qkv, (1, 0)) + qkv_bias).astype(BF16).reshape(c_n, s_n * rows, 3 * head_cols)
+    up_first = [jnp.concatenate([after(part, qkv)[None] for part in parts]) for parts in up_first]
+    down_z = grid.arrivals(after(down_weight.reshape(2, long // 2, width), *up_first), "z")
+    up_last = [grid.arrivals(after(part, *up_first), order[1]) for part, order in zip(up_first, orders)]
+    down_first = [
+        grid.gather(jnp.concatenate([part[None, i : i + 1] for part in down_z]), order[0])
+        for i, order in enumerate(orders)
+    ]
     attended_all, logsums = [], []
     for latent in range(c_n):
         qkv = after(qkv, *(attended_all + down_z if latent else up_first))
@@ -386,9 +387,8 @@
         arrived.append(send(part, c=-c_d, s=-s_d) if c_d + s_d else part)
     up_steps = [grid.steps(order[1], order[0], "z") for order in orders]
     each = count // (c_n * grid.size["y"])
-    flat_last = lax.optimization_barrier(tuple(part for parts in up_last for part in parts) + tuple(arrived))
-    arrived = flat_last[-len(arrived) :]
-    parts = [part.reshape((-1,) + part.shape[2:]) for part in flat_last[: -len(arrived)]]
+    flat_last = lax.optimization_barrier(tuple(part for parts in up_last for part in parts) + tuple(attended_all))
+    parts = [part.reshape((-1,) + part.shape[2:]) for part in flat_last[: -len(attended_all)]]
     jobs, table, out_jobs, out_table = [], [], [], []
     first = 0
     for c_d, (last, steps) in enumerate(zip(up_last, up_steps)):
@@ -406,21 +406,21 @@
             out_table.append(grid.shard_of({**back, "c": c_d}))
     w_out = place([out_own, send(out_own, c=1)], out_jobs, out_table)
     w_up = place(parts, jobs, table)
-    arrived = jnp.stack(arrived)
+    stacked = jnp.stack(arrived)
     ordered = []
     for c in range(c_n):
         for s in range(s_n):
             index = (c - at["c"]) % c_n * s_n + (s - at["s"]) % s_n
-            ordered.append(lax.dynamic_index_in_dim(arrived, index, 0, keepdims=False))
+            ordered.append(lax.dynamic_index_in_dim(stacked, index, 0, keepdims=False))
     attended = jnp.concatenate(ordered, axis=1)
-    attn_proj = dot(attended, w_out, (1, 0)) + b_out
+    down_last = [grid.arrivals(after(part, *arrived), order[1]) for part, order in zip(down_first, orders)]
+    attn_proj = dot(after(attended, w_up), w_out, (1, 0)) + b_out
+    attn_proj = after(attn_proj, *down_first)
     middle = inputs + gate_attn * attn_proj
     normed_mid, inverse_mid = normalize(middle)
     modded_mlp = (normed_mid * (1.0 + scale_mlp) + shift_mlp).astype(BF16)
     mlp_all = jnp.concatenate([modded_mlp, send(modded_mlp, c=1)])
     up_half = lax.dynamic_index_in_dim(b_up.reshape(-1, c_n, block_cols), at["c"], 1, keepdims=False).reshape(half)
-    mlp_all = after(mlp_all, *down_first)
-    down_last = [grid.arrivals(part, order[1]) for part, order in zip(down_first, orders)]
     pre_act = dot(mlp_all, w_up, (1, 0)) + up_half
     gelu_tanh = partial(jax.nn.gelu, approximate=True)
     activated = gelu_tanh(pre_act).astype(BF16)
@@ -447,7 +447,7 @@
             table.append((shard // (c_n * s_n) * s_n + shard % s_n) * 2 + row_half)
         first += len(last)
     w_down = place(parts, jobs, table)
-    proj_terms = dot(activated, w_down, (1, 0))
+    proj_terms = dot(after(activated, *down_sent), w_down, (1, 0))
     mlp_proj = proj_terms[:rows] + send(proj_terms[rows:], c=1) + b_down
     block_out = (middle + gate_mlp * mlp_proj).astype(BF16)
 
@@ -465,7 +465,9 @@
     up_sent = up_sent + grid.sent
     down_a, down_b = grid.shed(down_a, 1, "y"), grid.shed(down_b, 1, "s")
     mod_terms = dot(after(pre_grad, *up_sent), w_up, (1, 1))
-    mlp_mod_grad = mod_terms[:rows] + send(mod_terms[rows:].astype(BF16), c=1).astype(F32)
+    arrived = send(mod_terms[rows:].astype(BF16), c=1)
+    up_a, up_b = settle(up_a, BF16, mod_terms, arrived), settle(up_b, BF16, mod_terms, arrived)
+    mlp_mod_grad = after(mod_terms[:rows], up_a, up_b) + arrived.astype(F32)
     middle_part = normalize_back(mlp_mod_grad * (1.0 + scale_mlp), normed_mid, inverse_mid)
     shift_mlp_grad = jnp.sum(mlp_mod_grad, axis=0)
     scale_mlp_grad = jnp.sum(mlp_mod_grad * normed_mid, axis=0)
@@ -473,8 +475,7 @@
     gate_mlp_grad = jnp.sum(out_cot * mlp_proj, axis=0)
     attn_grad = (gate_attn * middle_grad).astype(BF16)
     down_terms = jnp.concatenate([settle(part, BF16, attn_grad) for part in (down_a, down_b)], axis=1)
-    up_a, up_b = settle(up_a, BF16, attn_grad), settle(up_b, BF16, attn_grad)
-    attn_grad = after(attn_grad, down_terms, up_a, up_b)
+    attn_grad = after(attn_grad, down_terms)
     gate_attn_grad = jnp.sum(middle_grad * attn_proj, axis=0)
     out_bias_grad = jnp.sum(attn_grad.astype(F32), axis=0)
     attended_grad = dot(attn_grad, w_out, (1, 1), BF16)
@@ -490,32 +491,30 @@
     out_terms = dot(attended, after(attn_grad, attended_grad), (0, 0), BF16)
     out_terms = out_terms.reshape(z_n, y_n, c_n, s_n, short, width)
     out_terms = grid.reduce(out_terms, 2, "c", BF16)
-    up_terms = jnp.concatenate([settle(part, BF16, out_terms) for part in (up_a, up_b)], axis=1)
     out_terms = grid.shed(out_terms, 2, "s")
     out_sent = grid.sent
-    up_terms = grid.shed(after(up_terms, *out_sent), 0, "z")
-    up_sent = grid.sent
     qkv_grads = []
     for latent in range(c_n):
         grads = jnp.concatenate(arrived[latent * s_n : (latent + 1) * s_n])[None]
         if latent == 0:
-            grads = after(grads, *out_sent, *up_sent)
+            grads = after(grads, *out_sent)
         else:
             down_weight_grad = settle(down_terms, F32, *qkv_grads)
-            out_terms = grid.shed(settle(out_terms, BF16, *qkv_grads), 1, "y")
+            up_terms = jnp.concatenate([settle(part, BF16, *qkv_grads) for part in (up_a, up_b)], axis=1)
+            up_terms = grid.shed(up_terms, 0, "z")
             grads = after(grads, down_weight_grad, *grid.sent)
         qkv_grads.append(attend_back(qkv, grads, logsums[latent], latent, head_cols))
     qkv_grad = jnp.concatenate(qkv_grads).reshape(c_n * s_n * rows, 3 * head_cols)
     up_terms = settle(up_terms, F32, qkv_grad)
-    out_terms = grid.shed(settle(out_terms, BF16, qkv_grad), 0, "z")
+    out_terms = grid.shed(settle(out_terms, BF16, qkv_grad), 1, "y")
     qkv_grad = after(qkv_grad, up_terms, *grid.sent)
     mod_terms = dot(qkv_grad, w_qkv, (1, 1)).reshape(c_n, s_n, rows, width)
     mod_sent = mod_terms[1].astype(BF16)
     qkv_terms = dot(modded_all, after(qkv_grad, mod_sent), (0, 0), BF16)
     qkv_terms = qkv_terms.reshape(z_n, y_n, c_n, s_n, short, 3 * head_cols)
     qkv_terms = grid.shed(qkv_terms, 1, "y")
-    out_weight_grad = settle(out_terms, F32, *grid.sent)
-    mod_terms = after(mod_terms[0], out_weight_grad, *grid.sent)
+    out_terms = settle(out_terms, BF16, *grid.sent)
+    mod_terms = after(mod_terms[0], *grid.sent)
     mod_sum = mod_terms + send(mod_sent, c=1).astype(F32)
     shift_attn_grad = jnp.sum(mod_sum, axis=(0, 1))
     scale_attn_grad = jnp.sum(mod_sum * normed_all, axis=(0, 1))
@@ -535,13 +534,18 @@
     up_sums = spread(up_bias_grad.reshape(-1, block_cols), at["c"], c_n, 1).reshape(-1)
     total = jnp.concatenate([modulation_grad, q_sums, v_sums, out_bias_grad, up_sums, down_bias_grad])
     total = grid.sum_over(total, "s")
+    qkv_terms = lax.optimization_barrier(tuple(qkv_terms) + (total,))
+    qkv_terms, total = qkv_terms[:-1], qkv_terms[-1]
     total = grid.gather(total, "z")
     qkv_terms = settle(qkv_terms, BF16, total)
-    qkv_terms = grid.shed(qkv_terms, 0, "z")
-    total = grid.gather(after(total, *grid.sent), "c", "y")
+    total = grid.gather(total, "c", "y")
+    qkv_terms = grid.shed(after(qkv_terms, total), 0, "z")
+    out_terms = grid.shed(after(out_terms, *grid.sent), 0, "z")
+    total = after(total, *grid.sent)
     attn_mod_grad = mod_sum[0]
     for part in arrived:
-        attn_mod_grad = attn_mod_grad + after(part, total).astype(F32)
+        part = after(part, total)
+        attn_mod_grad = attn_mod_grad + part.astype(F32)
     input_part = normalize_back(attn_mod_grad * (1.0 + scale_attn), normed_all[0], inverse_all[0])
     input_grad = (middle_grad + input_part).astype(BF16)
     z, y, c = ((at[name] - jnp.arange(size[name])) % size[name] for name in ("z", "y", "c"))
@@ -566,15 +570,18 @@
     cond_terms = lax.dot_general(
         mod_grads, ada_weight.astype(F32), (((1,), (1,)), ((), ())), precision=HIGHEST
     )
-    cond_terms = after(cond_terms, input_grad)
     order = (latent[:, None] == jnp.arange(count // s_n)[None]).astype(F32)
     cond_terms = lax.dot_general(order, cond_terms, (((0,), (0,)), ((), ())), precision=HIGHEST)
     cond_terms = jnp.broadcast_to(cond_terms[:, None], (count // s_n, s_n, short)).reshape(count, short)
+    cond_terms = after(cond_terms, part)
     cond_total = lax.all_to_all(cond_terms, AXES, 0, 0, tiled=True).reshape(width)
+    cond_total = after(cond_total, input_grad)
     qkv_terms = settle(qkv_terms, F32, cond_total)
+    out_weight_grad = settle(out_terms, F32, cond_total)
     _, silu_back = jax.vjp(jax.nn.silu, cond_own)
     cond_grad = silu_back(cond_total)[0].astype(BF16)[None]
 
+    up_terms = after(up_terms, total)
     up_first = up_terms[:short].reshape(short, -1, 1, block_cols)
     up_second = up_terms[short:].reshape(short, -1, 1, block_cols)
     up_second = send(up_second, c=1)

time: 534 us -> 519 us (0.972)
  waiting for transfers between devices: 120 us -> 106 us
  local copies, waits for them, and re-layouts: 85.5 us -> 74.2 us
  starting transfers between devices: 88.4 us -> 98.5 us
    ppermute x73, waiting for transfers between devices: 109 us -> 85 us  [send(): return lax.ppermute(value, AXES, pairs)]
    ppermute x73, starting transfers between devices: 73 us -> 86.8 us  [send(): return lax.ppermute(value, AXES, pairs)]
    all_to_all x1, waiting for transfers between devices: 2.38 us -> 11.6 us  [local(): all_shares = lax.all_to_all(shares, AXES, 0, 0, tiled=True)]
    broadcast_in_dim x8, local copies, waits for them, and re-layouts: 7.42 us -> 0.1 us  [local(): part[None, low:high]]
    convert_element_type x12, other arithmetic: 6.19 us -> 12.5 us  [settle(): return sum((part.astype(F32) for part in parts)).astype(kind)]
    unnamed x243 -> x241, local copies, waits for them, and re-layouts: 23.8 us -> 20.6 us
  transfers between devices with their start and end apart: 76 -> 76, of which waited for: 31 -> 23; matrix products, arithmetic and copies ran while one was open for 36% -> 32% of each run, Pallas kernels for 14% -> 15%
where the time goes in v3:
time: 519 us; the launch traced here: 511 us
  waiting for transfers between devices  106 us (20%)
  starting transfers between devices  98.5 us (19%)
  Pallas kernels  79.1 us (15%)
  matrix products  77.1 us (15%)
  local copies, waits for them, and re-layouts  74.2 us (14%)
  other arithmetic  72.1 us (14%)
    ppermute x73, starting transfers between devices, send(): return lax.ppermute(value, AXES, pairs)  86.8 us
    ppermute x73, waiting for transfers between devices, send(): return lax.ppermute(value, AXES, pairs)  85 us
    dot_general x13, matrix products, dot(): lax.dot_general(left, right, ((dims[:1], dims[1:]), ((), ())), preferred_...  73.9 us
    pallas_call x2, Pallas kernels, attend_back(): pl.pallas_call(partial(attend_back_kernel, width), grid=(1,), in_specs=[s...  36.7 us
    pallas_call x2, Pallas kernels, attend(): pl.pallas_call(partial(attend_kernel, width), grid=(1,), in_specs=[spec(3...  21.9 us
    unnamed x241, local copies, waits for them, and re-layouts  20.6 us
    pallas_call x4, Pallas kernels, place(): pl.pallas_call(partial(place_kernel, jobs, flat), out_shape=jax.ShapeDtyp...  18 us
    convert_element_type x12, other arithmetic, settle(): return sum((part.astype(F32) for part in parts)).astype(kind)  12.5 us
  transfers between devices with their start and end apart: 76, of which 23 were waited for; matrix products, arithmetic and copies ran while one was open for 32% of the time, Pallas kernels for 15%

profile of v3, /device:TPU:0, one launch (start us, length us, event | category | flops | bytes accessed | tf_op | source)
XLA Modules:
  0.0 510.6 jit_solution(14156987766184516338)
XLA Ops:
  22.5 4.7 all-to-all-start
  27.4 11.6 %all-to-all-done = bf16[32,2,640]{2,1,0:T(2,128)(2,1)S(1)} async-done(((bf16[32,2,640]{2,1,0:T(2,128)(2,1)}), bf16[32,2,640]{2,1,0:T(2,128)(2,1)S(1)}, u32[]{:S(2)}, u32[]{:S(2)}) %all-to-all-start) | async-done | bytes 81952 | tf_op jit(solution)/shard_map/all_to_all | solution.py:316
  49.8 4.2 all-to-all-start.1
  57.6 9.1 %all-to-all-done.1 = f32[32,1,3072]{2,1,0:T(1,128)} async-done(((f32[32,1,3072]{2,1,0:T(1,128)}), f32[32,1,3072]{2,1,0:T(1,128)}, u32[]{:S(2)}, u32[]{:S(2)}) %all-to-all-start.1) | async-done | bytes 393248 | tf_op jit(solution)/shard_map/all_to_all | solution.py:331
  80.1 20.5 %collective-permute-done.12 = bf16[5,32,1024]{2,1,0:T(8,128)(2,1)S(1)} collective-permute-done((bf16[5,32,1024]{2,1,0:T(8,128)(2,1)}, bf16[5,32,1024]{2,1,0:T(8,128)(2,1)S(1)}, u32[]{:S(2)}, u32[]{:S(2)}) %collective-permute-start.12) | collective-permute-done | bytes 327712 | tf_op jit(solution)/shard_map/ppermute | solution.py:70
  107.1 7.2 %add_convert_fusion = bf16[2048,768]{1,0:T(8,128)(2,1)} fusion(bf16[1024,768]{1,0:T(8,128)(2,1)} %shard_map.228, f32[768]{0:T(1024)S(1)} %copy-done.94, bf16[1024,1024]{1,0:T(8,128)(2,1)} %collective-permute-done.8, bf16[1024,1024]{1,0:T(8,128)(2,1)S(1)} %fusion.10), kind=kOutput, calls=%fused_computation.13 | convolution fusion | flops 3232759808 | bytes 8915968 | tf_op jit(solution)/shard_map/dot_general | solution.py:22
  131.7 10.7 %shard_map.229 = (bf16[1,1024,256]{2,1,0:T(8,128)(2,1)}, f32[1,1024,256]{2,1,0:T(8,128)}) custom-call(bf16[2,1024,768]{2,1,0:T(8,128)(2,1)} %bitcast.403), custom_call_target="tpu_custom_call" | custom-call | flops 268435456 | bytes 3145728 | tf_op jit(solution)/shard_map/pallas_call | solution.py:203
  146.4 11.1 %shard_map.230 = (bf16[1,1024,256]{2,1,0:T(8,128)(2,1)}, f32[1,1024,256]{2,1,0:T(8,128)}) custom-call(bf16[2,1024,768]{2,1,0:T(8,128)(2,1)} %bitcast.404), custom_call_target="tpu_custom_call" | custom-call | flops 268435456 | bytes 3145728 | tf_op jit(solution)/shard_map/pallas_call | solution.py:203
  169.8 7.3 %collective-permute-done.26 = bf16[4,1,64,1024]{3,2,0,1:T(8,128)(2,1)S(1)} collective-permute-done((bf16[4,1,64,1024]{3,2,0,1:T(8,128)(2,1)S(1)}, bf16[4,1,64,1024]{3,2,0,1:T(8,128)(2,1)S(1)}, u32[]{:S(2)}, u32[]{:S(2)}) %collective-permute-start.26) | collective-permute-done | bytes 524320 | tf_op jit(solution)/shard_map/ppermute | solution.py:70
  181.8 5.5 %shard_map.231 = bf16[1024,2048]{1,0:T(8,128)(2,1)} custom-call(s32[64]{0:T(128)} %stack.364.table, bf16[8,3,32,1024]{3,2,1,0:T(8,128)(2,1)} %bitcast.417, bf16[8,3,32,1024]{3,2,1,0:T(8,128)(2,1)} %bitcast.83.refs_1_, bf16[8,2,32,1024]{3,2,1,0:T(8,128)(2,1)} %bitcast.424, bf16[8,2,32,1024]{3,2,1,0:T(8,128)(2,1)} %bitcast.433), custom_call_target="tpu_custom_call" | custom-call | bytes 8388608 | tf_op jit(solution)/shard_map/pallas_call | solution.py:123
  207.3 10.0 %multiply_convert_fusion = (bf16[1024,2048]{1,0:T(8,128)(2,1)S(1)}, f32[1024,2048]{1,0:T(8,128)}) fusion(f32[2048]{0:T(1024)S(1)} %bitcast.502, bf16[1024,2048]{1,0:T(8,128)(2,1)S(1)} %copy-done.17, bf16[512,1024]{1,0:T(8,128)(2,1)} %collective-permute-done.27, bf16[512,1024]{1,0:T(8,128)(2,1)} %add_convert_fusion.7), kind=kOutput, calls=%fused_computation.10 | convolution fusion | flops 4320133120 | bytes 18882560 | tf_op jit(solution)/shard_map/dot_general | solution.py:22
  217.4 7.9 %convolution_convert_fusion.1 = bf16[2048,1024]{1,0:T(8,128)(2,1)S(1)} fusion(bf16[1024,2048]{1,0:T(8,128)(2,1)S(1)} %get-tuple-element.139, bf16[512,1024]{1,0:T(8,128)(2,1)} %collective-permute-done.28, bf16[512,1024]{1,0:T(8,128)(2,1)} %get-tuple-element.222), kind=kOutput, calls=%fused_computation.27 | convolution fusion | flops 4301258752 | bytes 10485760 | tf_op jit(solution)/shard_map/dot_general | solution.py:22
  236.2 5.2 %shard_map.233 = bf16[2048,1024]{1,0:T(8,128)(2,1)} custom-call(s32[32]{0:T(128)} %stack.398.table, bf16[8,1,64,1024]{3,2,1,0:T(8,128)(2,1)} %bitcast.423, bf16[8,1,64,1024]{3,2,1,0:T(8,128)(2,1)} %bitcast.435, bf16[8,1,64,1024]{3,2,1,0:T(8,128)(2,1)} %bitcast.422, bf16[8,1,64,1024]{3,2,1,0:T(8,128)(2,1)} %bitcast.434), custom_call_target="tpu_custom_call" | custom-call | bytes 8388608 | tf_op jit(solution)/shard_map/pallas_call | solution.py:123
  241.5 10.1 %fusion.81 = f32[1024,1024]{1,0:T(8,128)} fusion(bf16[1024,2048]{1,0:T(8,128)(2,1)} %copy-done.105, bf16[2048,1024]{1,0:T(8,128)(2,1)} %shard_map.233), kind=kOutput, calls=%fused_computation.306 | convolution fusion | flops 4294967296 | bytes 12582912 | tf_op jit(solution)/shard_map/dot_general | solution.py:22
  251.5 12.8 %convert_reduce_fusion = (f32[2048]{0:T(1024)}, bf16[1024,2048]{1,0:T(8,128)(2,1)S(1)}) fusion(f32[1024,2048]{1,0:T(8,128)} %get-tuple-element.335, f32[2048]{0:T(1024)S(1)} %bitcast.503, bf16[1024,1024]{1,0:T(8,128)(2,1)S(1)} %pad_maximum_fusion.6, bf16[2048,1024]{1,0:T(8,128)(2,1)S(1)} %copy-done.25), kind=kOutput, calls=%fused_computation.9 | convolution fusion | flops 4343199744 | bytes 18890752 | tf_op jit(solution)/shard_map/dot_general | solution.py:22
  271.4 4.8 convolution_convert_fusion
  280.9 4.5 fusion.82
  298.7 16.2 %collective-permute-done.36 = bf16[4,2,32,2048]{3,2,1,0:T(8,128)(2,1)} collective-permute-done((bf16[4,2,32,2048]{3,2,1,0:T(8,128)(2,1)}, bf16[4,2,32,2048]{3,2,1,0:T(8,128)(2,1)}, u32[]{:S(2)}, u32[]{:S(2)}) %collective-permute-start.36) | collective-permute-done | bytes 1048608 | tf_op jit(solution)/shard_map/ppermute | solution.py:70
  335.2 6.2 %collective-permute-start.43 = (bf16[128,1024]{1,0:T(8,128)(2,1)S(1)}, bf16[128,1024]{1,0:T(8,128)(2,1)}, u32[]{:S(2)}, u32[]{:S(2)}) collective-permute-start(bf16[128,1024]{1,0:T(8,128)(2,1)S(1)} %get-tuple-element.262), channel_id=1, source_target_pairs={{0,8},{1,9},{2,10},{3,11},{4,12},{5,13},{6,14},{7,15},{8,16},{9,17... | collective-permute-start | bytes 786440 | tf_op jit(solution)/shard_map/ppermute | solution.py:70
  352.4 18.4 %shard_map.234 = bf16[1,1024,768]{2,1,0:T(8,128)(2,1)} custom-call(bf16[2,1024,768]{2,1,0:T(8,128)(2,1)} %bitcast.405, bf16[1,1024,256]{2,1,0:T(8,128)(2,1)} %maximum_bitcast_fusion.grads, f32[1,1024,256]{2,1,0:T(8,128)} %get-tuple-element.163.logsum), custom_call_target="tpu_custom_call" | custom-call | flops 536870912 | bytes 4718592 | tf_op jit(solution)/shard_map/pallas_call | solution.py:257
  378.6 18.3 %shard_map.235 = bf16[1,1024,768]{2,1,0:T(8,128)(2,1)} custom-call(bf16[2,1024,768]{2,1,0:T(8,128)(2,1)} %bitcast.406, bf16[1,1024,256]{2,1,0:T(8,128)(2,1)} %maximum_bitcast_fusion.1.grads, f32[1,1024,256]{2,1,0:T(8,128)} %get-tuple-element.175.logsum), custom_call_target="tpu_custom_call" | custom-call | flops 536870912 | bytes 4718592 | tf_op jit(solution)/shard_map/pallas_call | solution.py:257
  416.8 5.9 %fusion.18 = bf16[1024,768]{1,0:T(8,128)(2,1)S(1)} fusion(bf16[2048,768]{1,0:T(8,128)(2,1)S(1)} %bitcast.415, bf16[1024,1024]{1,0:T(8,128)(2,1)} %collective-permute-done.8, bf16[1024,1024]{1,0:T(8,128)(2,1)} %copy-done.30), kind=kOutput, calls=%fused_computation.68 | convolution fusion | flops 3230400512 | bytes 8912896 | tf_op jit(solution)/shard_map/dot_general | solution.py:22
  433.1 4.7 multiply_reduce_fusion
  457.6 4.9 collective-permute-done.59
  (579 shorter events, 284.6 us)
Async XLA Ops:
  6.5 34.5 %collective-permute-start.3 = (bf16[512,1024]{1,0:T(8,128)(2,1)}, bf16[512,1024]{1,0:T(8,128)(2,1)S(1)}, u32[]{:S(2)}, u32[]{:S(2)}) collective-permute-start(bf16[512,1024]{1,0:T(8,128)(2,1)} %bitcast.407), channel_id=1, source_target_pairs={{0,1},{1,0},{2,3},{3,2},{4,5},{5,4},{6,7},{7,6},{8,9},{9,8},{10,11... | collective-permute-start | bytes 3145736 | tf_op jit(solution)/shard_map/ppermute | solution.py:70
  71.5 29.0 %collective-permute-start.12 = (bf16[5,32,1024]{2,1,0:T(8,128)(2,1)}, bf16[5,32,1024]{2,1,0:T(8,128)(2,1)S(1)}, u32[]{:S(2)}, u32[]{:S(2)}) collective-permute-start(bf16[5,32,1024]{2,1,0:T(8,128)(2,1)} %fusion.42), channel_id=1, source_target_pairs={{0,16},{1,17},{2,18},{3,19},{4,20},{5,21},{6,22},{7,23},{8,24},{9,... | collective-permute-start | bytes 983048 | tf_op jit(solution)/shard_map/ppermute | solution.py:70
  72.4 28.2 %collective-permute-start.11 = (bf16[5,32,1024]{2,1,0:T(8,128)(2,1)}, bf16[5,32,1024]{2,1,0:T(8,128)(2,1)S(1)}, u32[]{:S(2)}, u32[]{:S(2)}) collective-permute-start(bf16[5,32,1024]{2,1,0:T(8,128)(2,1)} %fusion.42), channel_id=1, source_target_pairs={{0,8},{1,9},{2,10},{3,11},{4,12},{5,13},{6,14},{7,15},{8,16},{9,17... | collective-permute-start | bytes 983048 | tf_op jit(solution)/shard_map/ppermute | solution.py:70
  75.2 31.9 %collective-permute-start.8 = (bf16[1024,1024]{1,0:T(8,128)(2,1)S(1)}, bf16[1024,1024]{1,0:T(8,128)(2,1)}, u32[]{:S(2)}, u32[]{:S(2)}) collective-permute-start(bf16[1024,1024]{1,0:T(8,128)(2,1)S(1)} %fusion.10), channel_id=1, source_target_pairs={{0,2},{1,3},{2,0},{3,1},{4,6},{5,7},{6,4},{7,5},{8,10},{9,11},{10,... | collective-permute-start | bytes 6291464 | tf_op jit(solution)/shard_map/ppermute | solution.py:70
  75.3 27.4 %collective-permute-start.9 = (bf16[4,4,32,768]{3,2,1,0:T(8,128)(2,1)S(1)}, bf16[4,4,32,768]{3,2,1,0:T(8,128)(2,1)S(1)}, u32[]{:S(2)}, u32[]{:S(2)}) collective-permute-start(bf16[4,4,32,768]{3,2,1,0:T(8,128)(2,1)S(1)} %pad_maximum_fusion.18), channel_id=1, source_target_pairs={{0,4},{1,5},{2,6},{3,7},{4,0},{5,1},{6,2},{7,3},{8,12},{9,13},{10,... | collective-permute-start | bytes 2359304 | tf_op jit(solution)/shard_map/ppermute | solution.py:70
  121.5 39.4 %collective-permute-start.22 = (bf16[2,4,3,32,1024]{4,3,2,1,0:T(8,128)(2,1)S(1)}, bf16[2,4,3,32,1024]{4,3,2,1,0:T(8,128)(2,1)}, u32[]{:S(2)}, u32[]{:S(2)}) collective-permute-start(bf16[2,4,3,32,1024]{4,3,2,1,0:T(8,128)(2,1)S(1)} %pad_maximum_fusion.10), channel_id=1, source_target_pairs={{0,4},{1,5},{2,6},{3,7},{4,0},{5,1},{6,2},{7,3},{8,12},{9,13},{10,... | collective-permute-start | bytes 4718600 | tf_op jit(solution)/shard_map/ppermute | solution.py:70
  130.1 30.8 %collective-permute-start.23 = (bf16[2,4,2,32,1024]{4,3,2,1,0:T(8,128)(2,1)S(1)}, bf16[2,4,2,32,1024]{4,3,2,1,0:T(8,128)(2,1)S(1)}, u32[]{:S(2)}, u32[]{:S(2)}) collective-permute-start(bf16[2,4,2,32,1024]{4,3,2,1,0:T(8,128)(2,1)S(1)} %copy-done.21), channel_id=1, source_target_pairs={{0,1},{1,0},{2,3},{3,2},{4,5},{5,4},{6,7},{7,6},{8,9},{9,8},{10,11... | collective-permute-start | bytes 3145736 | tf_op jit(solution)/shard_map/ppermute | solution.py:70
  165.0 37.1 %collective-permute-start.28 = (bf16[512,1024]{1,0:T(8,128)(2,1)}, bf16[512,1024]{1,0:T(8,128)(2,1)}, u32[]{:S(2)}, u32[]{:S(2)}) collective-permute-start(bf16[512,1024]{1,0:T(8,128)(2,1)} %get-tuple-element.222), channel_id=1, source_target_pairs={{0,2},{1,3},{2,0},{3,1},{4,6},{5,7},{6,4},{7,5},{8,10},{9,11},{10,... | collective-permute-start | bytes 3145736 | tf_op jit(solution)/shard_map/ppermute | solution.py:70
  234.2 31.9 %collective-permute-start.33 = (bf16[4,2,64,1024]{3,2,1,0:T(8,128)(2,1)}, bf16[4,2,64,1024]{3,2,1,0:T(8,128)(2,1)}, u32[]{:S(2)}, u32[]{:S(2)}) collective-permute-start(bf16[4,2,64,1024]{3,2,1,0:T(8,128)(2,1)} %get-tuple-element.242), channel_id=1, source_target_pairs={{0,4},{1,5},{2,6},{3,7},{4,0},{5,1},{6,2},{7,3},{8,12},{9,13},{10,... | collective-permute-start | bytes 3145736 | tf_op jit(solution)/shard_map/ppermute | solution.py:70
  235.7 30.4 %collective-permute-start.32 = (bf16[4,2,64,1024]{3,2,1,0:T(8,128)(2,1)}, bf16[4,2,64,1024]{3,2,1,0:T(8,128)(2,1)}, u32[]{:S(2)}, u32[]{:S(2)}) collective-permute-start(bf16[4,2,64,1024]{3,2,1,0:T(8,128)(2,1)} %get-tuple-element.244), channel_id=1, source_target_pairs={{0,1},{1,0},{2,3},{3,2},{4,5},{5,4},{6,7},{7,6},{8,9},{9,8},{10,11... | collective-permute-start | bytes 3145736 | tf_op jit(solution)/shard_map/ppermute | solution.py:70
  288.6 26.3 %collective-permute-start.36 = (bf16[4,2,32,2048]{3,2,1,0:T(8,128)(2,1)}, bf16[4,2,32,2048]{3,2,1,0:T(8,128)(2,1)}, u32[]{:S(2)}, u32[]{:S(2)}) collective-permute-start(bf16[4,2,32,2048]{3,2,1,0:T(8,128)(2,1)} %get-tuple-element.233), channel_id=1, source_target_pairs={{0,1},{1,0},{2,3},{3,2},{4,5},{5,4},{6,7},{7,6},{8,9},{9,8},{10,11... | collective-permute-start | bytes 3145736 | tf_op jit(solution)/shard_map/ppermute | solution.py:70
  290.1 26.3 %collective-permute-start.34 = (bf16[4,2,32,2048]{3,2,1,0:T(8,128)(2,1)}, bf16[4,2,32,2048]{3,2,1,0:T(8,128)(2,1)}, u32[]{:S(2)}, u32[]{:S(2)}) collective-permute-start(bf16[4,2,32,2048]{3,2,1,0:T(8,128)(2,1)} %get-tuple-element.235), channel_id=1, source_target_pairs={{0,4},{1,5},{2,6},{3,7},{4,0},{5,1},{6,2},{7,3},{8,12},{9,13},{10,... | collective-permute-start | bytes 3145736 | tf_op jit(solution)/shard_map/ppermute | solution.py:70
  294.3 28.6 %collective-permute-start.31 = (f32[512,1024]{1,0:T(8,128)S(1)}, f32[512,1024]{1,0:T(8,128)S(1)}, u32[]{:S(2)}, u32[]{:S(2)}) collective-permute-start(f32[512,1024]{1,0:T(8,128)S(1)} %slice.261), channel_id=1, source_target_pairs={{0,2},{1,3},{2,0},{3,1},{4,6},{5,7},{6,4},{7,5},{8,10},{9,11},{10,... | collective-permute-start | bytes 6291464 | tf_op jit(solution)/shard_map/ppermute | solution.py:70
  295.8 38.7 %collective-permute-start.38 = (bf16[4,64,1024]{2,1,0:T(8,128)(2,1)S(1)}, bf16[4,64,1024]{2,1,0:T(8,128)(2,1)S(1)}, u32[]{:S(2)}, u32[]{:S(2)}) collective-permute-start(bf16[4,64,1024]{2,1,0:T(8,128)(2,1)S(1)} %get-tuple-element.265), channel_id=1, source_target_pairs={{0,1},{1,0},{2,3},{3,2},{4,5},{5,4},{6,7},{7,6},{8,9},{9,8},{10,11... | collective-permute-start | bytes 1572872 | tf_op jit(solution)/shard_map/ppermute | solution.py:70
  297.1 37.6 %collective-permute-start.37 = (bf16[4,64,1024]{2,1,0:T(8,128)(2,1)S(1)}, bf16[4,64,1024]{2,1,0:T(8,128)(2,1)S(1)}, u32[]{:S(2)}, u32[]{:S(2)}) collective-permute-start(bf16[4,64,1024]{2,1,0:T(8,128)(2,1)S(1)} %get-tuple-element.267), channel_id=1, source_target_pairs={{0,4},{1,5},{2,6},{3,7},{4,0},{5,1},{6,2},{7,3},{8,12},{9,13},{10,... | collective-permute-start | bytes 1572872 | tf_op jit(solution)/shard_map/ppermute | solution.py:70
  335.2 37.1 %collective-permute-start.43 = (bf16[128,1024]{1,0:T(8,128)(2,1)S(1)}, bf16[128,1024]{1,0:T(8,128)(2,1)}, u32[]{:S(2)}, u32[]{:S(2)}) collective-permute-start(bf16[128,1024]{1,0:T(8,128)(2,1)S(1)} %get-tuple-element.262), channel_id=1, source_target_pairs={{0,8},{1,9},{2,10},{3,11},{4,12},{5,13},{6,14},{7,15},{8,16},{9,17... | collective-permute-start | bytes 786440 | tf_op jit(solution)/shard_map/ppermute | solution.py:70
  341.4 31.0 %collective-permute-start.44 = (bf16[128,1024]{1,0:T(8,128)(2,1)S(1)}, bf16[128,1024]{1,0:T(8,128)(2,1)}, u32[]{:S(2)}, u32[]{:S(2)}) collective-permute-start(bf16[128,1024]{1,0:T(8,128)(2,1)S(1)} %get-tuple-element.263), channel_id=1, source_target_pairs={{0,16},{1,17},{2,18},{3,19},{4,20},{5,21},{6,22},{7,23},{8,24},{9,... | collective-permute-start | bytes 786440 | tf_op jit(solution)/shard_map/ppermute | solution.py:70
  346.0 26.3 %collective-permute-start.46 = (bf16[4,32,2048]{2,1,0:T(8,128)(2,1)S(1)}, bf16[4,32,2048]{2,1,0:T(8,128)(2,1)S(1)}, u32[]{:S(2)}, u32[]{:S(2)}) collective-permute-start(bf16[4,32,2048]{2,1,0:T(8,128)(2,1)S(1)} %get-tuple-element.255), channel_id=1, source_target_pairs={{0,1},{1,0},{2,3},{3,2},{4,5},{5,4},{6,7},{7,6},{8,9},{9,8},{10,11... | collective-permute-start | bytes 1572872 | tf_op jit(solution)/shard_map/ppermute | solution.py:70
  370.8 28.8 %collective-permute-start.51 = (bf16[4,2,32,1024]{3,2,1,0:T(8,128)(2,1)S(1)}, bf16[4,2,32,1024]{3,2,1,0:T(8,128)(2,1)S(1)}, u32[]{:S(2)}, u32[]{:S(2)}) collective-permute-start(bf16[4,2,32,1024]{3,2,1,0:T(8,128)(2,1)S(1)} %get-tuple-element.248), channel_id=1, source_target_pairs={{0,1},{1,0},{2,3},{3,2},{4,5},{5,4},{6,7},{7,6},{8,9},{9,8},{10,11... | collective-permute-start | bytes 1572872 | tf_op jit(solution)/shard_map/ppermute | solution.py:70
  372.7 25.9 %collective-permute-start.48 = (bf16[64,2048]{1,0:T(8,128)(2,1)S(1)}, bf16[64,2048]{1,0:T(8,128)(2,1)S(1)}, u32[]{:S(2)}, u32[]{:S(2)}) collective-permute-start(bf16[64,2048]{1,0:T(8,128)(2,1)S(1)} %get-tuple-element.250), channel_id=1, source_target_pairs={{0,8},{1,9},{2,10},{3,11},{4,12},{5,13},{6,14},{7,15},{8,16},{9,17... | collective-permute-start | bytes 786440 | tf_op jit(solution)/shard_map/ppermute | solution.py:70
  372.8 25.9 %collective-permute-start.49 = (bf16[64,2048]{1,0:T(8,128)(2,1)S(1)}, bf16[64,2048]{1,0:T(8,128)(2,1)S(1)}, u32[]{:S(2)}, u32[]{:S(2)}) collective-permute-start(bf16[64,2048]{1,0:T(8,128)(2,1)S(1)} %get-tuple-element.251), channel_id=1, source_target_pairs={{0,16},{1,17},{2,18},{3,19},{4,20},{5,21},{6,22},{7,23},{8,24},{9,... | collective-permute-start | bytes 786440 | tf_op jit(solution)/shard_map/ppermute | solution.py:70
  452.2 28.3 %collective-permute-start.53 = (bf16[512,1024]{1,0:T(8,128)(2,1)}, bf16[512,1024]{1,0:T(8,128)(2,1)}, u32[]{:S(2)}, u32[]{:S(2)}) collective-permute-start(bf16[512,1024]{1,0:T(8,128)(2,1)} %fusion.20), channel_id=1, source_target_pairs={{0,1},{1,0},{2,3},{3,2},{4,5},{5,4},{6,7},{7,6},{8,9},{9,8},{10,11... | collective-permute-start | bytes 3145736 | tf_op jit(solution)/shard_map/ppermute | solution.py:70
  468.0 29.2 %collective-permute-start.70 = (bf16[32,1024]{1,0:T(8,128)(2,1)}, bf16[32,1024]{1,0:T(8,128)(2,1)}, u32[]{:S(2)}, u32[]{:S(2)}) collective-permute-start(bf16[32,1024]{1,0:T(8,128)(2,1)} %get-tuple-element.298), channel_id=1, source_target_pairs={{0,16},{1,17},{2,18},{3,19},{4,20},{5,21},{6,22},{7,23},{8,24},{9,... | collective-permute-start | bytes 196616 | tf_op jit(solution)/shard_map/ppermute | solution.py:70
  469.1 28.0 %collective-permute-start.71 = (bf16[32,1024]{1,0:T(8,128)(2,1)}, bf16[32,1024]{1,0:T(8,128)(2,1)}, u32[]{:S(2)}, u32[]{:S(2)}) collective-permute-start(bf16[32,1024]{1,0:T(8,128)(2,1)} %get-tuple-element.297), channel_id=1, source_target_pairs={{0,24},{1,25},{2,26},{3,27},{4,28},{5,29},{6,30},{7,31},{8,0},{9,1... | collective-permute-start | bytes 196616 | tf_op jit(solution)/shard_map/ppermute | solution.py:70
  (160 other events, 1647.6 us)

commit v4 on v3

--- a/solution.py
+++ b/solution.py
@@ -513,8 +513,9 @@
     qkv_terms = dot(modded_all, after(qkv_grad, mod_sent), (0, 0), BF16)
     qkv_terms = qkv_terms.reshape(z_n, y_n, c_n, s_n, short, 3 * head_cols)
     qkv_terms = grid.shed(qkv_terms, 1, "y")
-    out_terms = settle(out_terms, BF16, *grid.sent)
-    mod_terms = after(mod_terms[0], *grid.sent)
+    qkv_sent = grid.sent
+    out_terms = grid.shed(settle(out_terms, BF16, *qkv_sent), 0, "z")
+    mod_terms = after(mod_terms[0], *qkv_sent)
     mod_sum = mod_terms + send(mod_sent, c=1).astype(F32)
     shift_attn_grad = jnp.sum(mod_sum, axis=(0, 1))
     scale_attn_grad = jnp.sum(mod_sum * normed_all, axis=(0, 1))
@@ -534,13 +535,13 @@
     up_sums = spread(up_bias_grad.reshape(-1, block_cols), at["c"], c_n, 1).reshape(-1)
     total = jnp.concatenate([modulation_grad, q_sums, v_sums, out_bias_grad, up_sums, down_bias_grad])
     total = grid.sum_over(total, "s")
-    qkv_terms = lax.optimization_barrier(tuple(qkv_terms) + (total,))
+    out_weight_grad = settle(out_terms, F32, total)
+    qkv_terms = lax.optimization_barrier(tuple(qkv_terms) + (after(total, out_weight_grad),))
     qkv_terms, total = qkv_terms[:-1], qkv_terms[-1]
     total = grid.gather(total, "z")
     qkv_terms = settle(qkv_terms, BF16, total)
     total = grid.gather(total, "c", "y")
     qkv_terms = grid.shed(after(qkv_terms, total), 0, "z")
-    out_terms = grid.shed(after(out_terms, *grid.sent), 0, "z")
     total = after(total, *grid.sent)
     attn_mod_grad = mod_sum[0]
     for part in arrived:
@@ -552,6 +553,10 @@
     latent = ((z[None, None] * y_n + y[None, :, None]) * c_n + c[:, None, None]).reshape(-1)
     cond_back = jnp.dot(jax.nn.one_hot(latent, count // s_n, dtype=BF16), cond_flat, preferred_element_type=F32)
     mod_grads = total.reshape(-1, total.shape[-1])[:, : 6 * width]
+    cond_terms = lax.dot_general(
+        mod_grads, ada_weight.astype(F32), (((1,), (1,)), ((), ())), precision=HIGHEST
+    )
+    total, mod_grads = lax.optimization_barrier((total, mod_grads, cond_terms))[:2]
     bias_sums = jnp.sum(total.reshape(-1, total.shape[-1]), axis=0)
 
     def own_share(start, kept):
@@ -567,9 +572,6 @@
     ada_weight_grad = lax.dot_general(
         cond_back, mod_grads, (((0,), (0,)), ((), ())), precision=HIGHEST
     )
-    cond_terms = lax.dot_general(
-        mod_grads, ada_weight.astype(F32), (((1,), (1,)), ((), ())), precision=HIGHEST
-    )
     order = (latent[:, None] == jnp.arange(count // s_n)[None]).astype(F32)
     cond_terms = lax.dot_general(order, cond_terms, (((0,), (0,)), ((), ())), precision=HIGHEST)
     cond_terms = jnp.broadcast_to(cond_terms[:, None], (count // s_n, s_n, short)).reshape(count, short)
@@ -577,7 +579,6 @@
     cond_total = lax.all_to_all(cond_terms, AXES, 0, 0, tiled=True).reshape(width)
     cond_total = after(cond_total, input_grad)
     qkv_terms = settle(qkv_terms, F32, cond_total)
-    out_weight_grad = settle(out_terms, F32, cond_total)
     _, silu_back = jax.vjp(jax.nn.silu, cond_own)
     cond_grad = silu_back(cond_total)[0].astype(BF16)[None]
 

time: 519 us -> 512 us (0.987)
    unnamed x241 -> x233, local copies, waits for them, and re-layouts: 20.6 us -> 21.1 us
  transfers between devices with their start and end apart: 76 -> 76, of which waited for: 23 -> 21; matrix products, arithmetic and copies ran while one was open for 32% -> 32% of each run, Pallas kernels for 15% -> 15%
where the time goes in v4:
time: 512 us; the launch traced here: 504 us
  waiting for transfers between devices  103 us (20%)
  starting transfers between devices  95.6 us (19%)
  Pallas kernels  79.1 us (15%)
  matrix products  76.4 us (15%)
  local copies, waits for them, and re-layouts  73.9 us (14%)
  other arithmetic  71.2 us (14%)
    ppermute x73, starting transfers between devices, send(): return lax.ppermute(value, AXES, pairs)  83.8 us
    ppermute x73, waiting for transfers between devices, send(): return lax.ppermute(value, AXES, pairs)  82.8 us
    dot_general x13, matrix products, dot(): lax.dot_general(left, right, ((dims[:1], dims[1:]), ((), ())), preferred_...  73.9 us
    pallas_call x2, Pallas kernels, attend_back(): pl.pallas_call(partial(attend_back_kernel, width), grid=(1,), in_specs=[s...  36.7 us
    pallas_call x2, Pallas kernels, attend(): pl.pallas_call(partial(attend_kernel, width), grid=(1,), in_specs=[spec(3...  21.9 us
    unnamed x233, local copies, waits for them, and re-layouts  21.1 us
    pallas_call x4, Pallas kernels, place(): pl.pallas_call(partial(place_kernel, jobs, flat), out_shape=jax.ShapeDtyp...  18 us
    convert_element_type x12, other arithmetic, settle(): return sum((part.astype(F32) for part in parts)).astype(kind)  12.4 us
  transfers between devices with their start and end apart: 76, of which 21 were waited for; matrix products, arithmetic and copies ran while one was open for 32% of the time, Pallas kernels for 15%

profile of v4, /device:TPU:0, one launch (start us, length us, event | category | flops | bytes accessed | tf_op | source)
XLA Modules:
  0.0 503.7 jit_solution(14094800423643355889)
XLA Ops:
  22.5 4.7 all-to-all-start
  27.3 11.6 %all-to-all-done = bf16[32,2,640]{2,1,0:T(2,128)(2,1)S(1)} async-done(((bf16[32,2,640]{2,1,0:T(2,128)(2,1)}), bf16[32,2,640]{2,1,0:T(2,128)(2,1)S(1)}, u32[]{:S(2)}, u32[]{:S(2)}) %all-to-all-start) | async-done | bytes 81952 | tf_op jit(solution)/shard_map/all_to_all | solution.py:316
  49.7 4.2 all-to-all-start.1
  57.6 9.1 %all-to-all-done.1 = f32[32,1,3072]{2,1,0:T(1,128)} async-done(((f32[32,1,3072]{2,1,0:T(1,128)}), f32[32,1,3072]{2,1,0:T(1,128)}, u32[]{:S(2)}, u32[]{:S(2)}) %all-to-all-start.1) | async-done | bytes 393248 | tf_op jit(solution)/shard_map/all_to_all | solution.py:331
  80.0 20.5 %collective-permute-done.12 = bf16[5,32,1024]{2,1,0:T(8,128)(2,1)S(1)} collective-permute-done((bf16[5,32,1024]{2,1,0:T(8,128)(2,1)}, bf16[5,32,1024]{2,1,0:T(8,128)(2,1)S(1)}, u32[]{:S(2)}, u32[]{:S(2)}) %collective-permute-start.12) | collective-permute-done | bytes 327712 | tf_op jit(solution)/shard_map/ppermute | solution.py:70
  107.1 7.3 %add_convert_fusion = bf16[2048,768]{1,0:T(8,128)(2,1)} fusion(bf16[1024,768]{1,0:T(8,128)(2,1)} %shard_map.228, f32[768]{0:T(1024)S(1)} %copy-done.90, bf16[1024,1024]{1,0:T(8,128)(2,1)} %collective-permute-done.8, bf16[1024,1024]{1,0:T(8,128)(2,1)S(1)} %fusion.10), kind=kOutput, calls=%fused_computation.13 | convolution fusion | flops 3232759808 | bytes 8915968 | tf_op jit(solution)/shard_map/dot_general | solution.py:22
  131.7 10.7 %shard_map.229 = (bf16[1,1024,256]{2,1,0:T(8,128)(2,1)}, f32[1,1024,256]{2,1,0:T(8,128)}) custom-call(bf16[2,1024,768]{2,1,0:T(8,128)(2,1)} %bitcast.404), custom_call_target="tpu_custom_call" | custom-call | flops 268435456 | bytes 3145728 | tf_op jit(solution)/shard_map/pallas_call | solution.py:203
  146.3 11.1 %shard_map.230 = (bf16[1,1024,256]{2,1,0:T(8,128)(2,1)}, f32[1,1024,256]{2,1,0:T(8,128)}) custom-call(bf16[2,1024,768]{2,1,0:T(8,128)(2,1)} %bitcast.405), custom_call_target="tpu_custom_call" | custom-call | flops 268435456 | bytes 3145728 | tf_op jit(solution)/shard_map/pallas_call | solution.py:203
  169.8 7.3 %collective-permute-done.26 = bf16[4,1,64,1024]{3,2,0,1:T(8,128)(2,1)S(1)} collective-permute-done((bf16[4,1,64,1024]{3,2,0,1:T(8,128)(2,1)S(1)}, bf16[4,1,64,1024]{3,2,0,1:T(8,128)(2,1)S(1)}, u32[]{:S(2)}, u32[]{:S(2)}) %collective-permute-start.26) | collective-permute-done | bytes 524320 | tf_op jit(solution)/shard_map/ppermute | solution.py:70
  181.8 5.5 %shard_map.231 = bf16[1024,2048]{1,0:T(8,128)(2,1)} custom-call(s32[64]{0:T(128)} %stack.364.table, bf16[8,3,32,1024]{3,2,1,0:T(8,128)(2,1)} %bitcast.418, bf16[8,3,32,1024]{3,2,1,0:T(8,128)(2,1)} %bitcast.83.refs_1_, bf16[8,2,32,1024]{3,2,1,0:T(8,128)(2,1)} %bitcast.425, bf16[8,2,32,1024]{3,2,1,0:T(8,128)(2,1)} %bitcast.434), custom_call_target="tpu_custom_call" | custom-call | bytes 8388608 | tf_op jit(solution)/shard_map/pallas_call | solution.py:123
  207.3 10.0 %multiply_convert_fusion = (bf16[1024,2048]{1,0:T(8,128)(2,1)S(1)}, f32[1024,2048]{1,0:T(8,128)}) fusion(f32[2048]{0:T(1024)S(1)} %bitcast.503, bf16[1024,2048]{1,0:T(8,128)(2,1)S(1)} %copy-done.17, bf16[512,1024]{1,0:T(8,128)(2,1)} %collective-permute-done.27, bf16[512,1024]{1,0:T(8,128)(2,1)} %add_convert_fusion.7), kind=kOutput, calls=%fused_computation.10 | convolution fusion | flops 4320133120 | bytes 18882560 | tf_op jit(solution)/shard_map/dot_general | solution.py:22
  217.3 7.9 %convolution_convert_fusion.1 = bf16[2048,1024]{1,0:T(8,128)(2,1)S(1)} fusion(bf16[1024,2048]{1,0:T(8,128)(2,1)S(1)} %get-tuple-element.141, bf16[512,1024]{1,0:T(8,128)(2,1)} %collective-permute-done.28, bf16[512,1024]{1,0:T(8,128)(2,1)} %get-tuple-element.226), kind=kOutput, calls=%fused_computation.27 | convolution fusion | flops 4301258752 | bytes 10485760 | tf_op jit(solution)/shard_map/dot_general | solution.py:22
  236.1 5.2 %shard_map.233 = bf16[2048,1024]{1,0:T(8,128)(2,1)} custom-call(s32[32]{0:T(128)} %stack.398.table, bf16[8,1,64,1024]{3,2,1,0:T(8,128)(2,1)} %bitcast.424, bf16[8,1,64,1024]{3,2,1,0:T(8,128)(2,1)} %bitcast.436, bf16[8,1,64,1024]{3,2,1,0:T(8,128)(2,1)} %bitcast.423, bf16[8,1,64,1024]{3,2,1,0:T(8,128)(2,1)} %bitcast.435), custom_call_target="tpu_custom_call" | custom-call | bytes 8388608 | tf_op jit(solution)/shard_map/pallas_call | solution.py:123
  241.4 10.0 %fusion.79 = f32[1024,1024]{1,0:T(8,128)} fusion(bf16[1024,2048]{1,0:T(8,128)(2,1)} %copy-done.101, bf16[2048,1024]{1,0:T(8,128)(2,1)} %shard_map.233), kind=kOutput, calls=%fused_computation.304 | convolution fusion | flops 4294967296 | bytes 12582912 | tf_op jit(solution)/shard_map/dot_general | solution.py:22
  251.4 12.8 %convert_reduce_fusion = (f32[2048]{0:T(1024)}, bf16[1024,2048]{1,0:T(8,128)(2,1)S(1)}) fusion(f32[1024,2048]{1,0:T(8,128)} %get-tuple-element.339, f32[2048]{0:T(1024)S(1)} %bitcast.504, bf16[1024,1024]{1,0:T(8,128)(2,1)S(1)} %pad_maximum_fusion.6, bf16[2048,1024]{1,0:T(8,128)(2,1)S(1)} %copy-done.25), kind=kOutput, calls=%fused_computation.9 | convolution fusion | flops 4343199744 | bytes 18890752 | tf_op jit(solution)/shard_map/dot_general | solution.py:22
  271.3 4.8 convolution_convert_fusion
  280.8 4.5 fusion.80
  298.6 16.1 %collective-permute-done.36 = bf16[4,2,32,2048]{3,2,1,0:T(8,128)(2,1)} collective-permute-done((bf16[4,2,32,2048]{3,2,1,0:T(8,128)(2,1)}, bf16[4,2,32,2048]{3,2,1,0:T(8,128)(2,1)}, u32[]{:S(2)}, u32[]{:S(2)}) %collective-permute-start.36) | collective-permute-done | bytes 1048608 | tf_op jit(solution)/shard_map/ppermute | solution.py:70
  322.9 4.2 fusion.13
  335.1 6.1 %collective-permute-start.43 = (bf16[128,1024]{1,0:T(8,128)(2,1)S(1)}, bf16[128,1024]{1,0:T(8,128)(2,1)}, u32[]{:S(2)}, u32[]{:S(2)}) collective-permute-start(bf16[128,1024]{1,0:T(8,128)(2,1)S(1)} %get-tuple-element.266), channel_id=1, source_target_pairs={{0,8},{1,9},{2,10},{3,11},{4,12},{5,13},{6,14},{7,15},{8,16},{9,17... | collective-permute-start | bytes 786440 | tf_op jit(solution)/shard_map/ppermute | solution.py:70
  352.3 18.4 %shard_map.234 = bf16[1,1024,768]{2,1,0:T(8,128)(2,1)} custom-call(bf16[2,1024,768]{2,1,0:T(8,128)(2,1)} %bitcast.406, bf16[1,1024,256]{2,1,0:T(8,128)(2,1)} %maximum_bitcast_fusion.grads, f32[1,1024,256]{2,1,0:T(8,128)} %get-tuple-element.165.logsum), custom_call_target="tpu_custom_call" | custom-call | flops 536870912 | bytes 4718592 | tf_op jit(solution)/shard_map/pallas_call | solution.py:257
  378.4 18.3 %shard_map.235 = bf16[1,1024,768]{2,1,0:T(8,128)(2,1)} custom-call(bf16[2,1024,768]{2,1,0:T(8,128)(2,1)} %bitcast.407, bf16[1,1024,256]{2,1,0:T(8,128)(2,1)} %maximum_bitcast_fusion.1.grads, f32[1,1024,256]{2,1,0:T(8,128)} %get-tuple-element.177.logsum), custom_call_target="tpu_custom_call" | custom-call | flops 536870912 | bytes 4718592 | tf_op jit(solution)/shard_map/pallas_call | solution.py:257
  415.9 5.9 %fusion.18 = bf16[1024,768]{1,0:T(8,128)(2,1)S(1)} fusion(bf16[2048,768]{1,0:T(8,128)(2,1)S(1)} %bitcast.416, bf16[1024,1024]{1,0:T(8,128)(2,1)} %collective-permute-done.8, bf16[1024,1024]{1,0:T(8,128)(2,1)} %copy-done.30), kind=kOutput, calls=%fused_computation.68 | convolution fusion | flops 3230400512 | bytes 8912896 | tf_op jit(solution)/shard_map/dot_general | solution.py:22
  438.3 4.7 multiply_reduce_fusion
  (572 shorter events, 278.5 us)
Async XLA Ops:
  6.5 34.5 %collective-permute-start.3 = (bf16[512,1024]{1,0:T(8,128)(2,1)}, bf16[512,1024]{1,0:T(8,128)(2,1)S(1)}, u32[]{:S(2)}, u32[]{:S(2)}) collective-permute-start(bf16[512,1024]{1,0:T(8,128)(2,1)} %bitcast.408), channel_id=1, source_target_pairs={{0,1},{1,0},{2,3},{3,2},{4,5},{5,4},{6,7},{7,6},{8,9},{9,8},{10,11... | collective-permute-start | bytes 3145736 | tf_op jit(solution)/shard_map/ppermute | solution.py:70
  71.5 29.0 %collective-permute-start.12 = (bf16[5,32,1024]{2,1,0:T(8,128)(2,1)}, bf16[5,32,1024]{2,1,0:T(8,128)(2,1)S(1)}, u32[]{:S(2)}, u32[]{:S(2)}) collective-permute-start(bf16[5,32,1024]{2,1,0:T(8,128)(2,1)} %fusion.38), channel_id=1, source_target_pairs={{0,16},{1,17},{2,18},{3,19},{4,20},{5,21},{6,22},{7,23},{8,24},{9,... | collective-permute-start | bytes 983048 | tf_op jit(solution)/shard_map/ppermute | solution.py:70
  72.3 28.2 %collective-permute-start.11 = (bf16[5,32,1024]{2,1,0:T(8,128)(2,1)}, bf16[5,32,1024]{2,1,0:T(8,128)(2,1)S(1)}, u32[]{:S(2)}, u32[]{:S(2)}) collective-permute-start(bf16[5,32,1024]{2,1,0:T(8,128)(2,1)} %fusion.38), channel_id=1, source_target_pairs={{0,8},{1,9},{2,10},{3,11},{4,12},{5,13},{6,14},{7,15},{8,16},{9,17... | collective-permute-start | bytes 983048 | tf_op jit(solution)/shard_map/ppermute | solution.py:70
  75.2 31.9 %collective-permute-start.8 = (bf16[1024,1024]{1,0:T(8,128)(2,1)S(1)}, bf16[1024,1024]{1,0:T(8,128)(2,1)}, u32[]{:S(2)}, u32[]{:S(2)}) collective-permute-start(bf16[1024,1024]{1,0:T(8,128)(2,1)S(1)} %fusion.10), channel_id=1, source_target_pairs={{0,2},{1,3},{2,0},{3,1},{4,6},{5,7},{6,4},{7,5},{8,10},{9,11},{10,... | collective-permute-start | bytes 6291464 | tf_op jit(solution)/shard_map/ppermute | solution.py:70
  75.3 27.4 %collective-permute-start.9 = (bf16[4,4,32,768]{3,2,1,0:T(8,128)(2,1)S(1)}, bf16[4,4,32,768]{3,2,1,0:T(8,128)(2,1)S(1)}, u32[]{:S(2)}, u32[]{:S(2)}) collective-permute-start(bf16[4,4,32,768]{3,2,1,0:T(8,128)(2,1)S(1)} %pad_maximum_fusion.18), channel_id=1, source_target_pairs={{0,4},{1,5},{2,6},{3,7},{4,0},{5,1},{6,2},{7,3},{8,12},{9,13},{10,... | collective-permute-start | bytes 2359304 | tf_op jit(solution)/shard_map/ppermute | solution.py:70
  121.4 39.4 %collective-permute-start.22 = (bf16[2,4,3,32,1024]{4,3,2,1,0:T(8,128)(2,1)S(1)}, bf16[2,4,3,32,1024]{4,3,2,1,0:T(8,128)(2,1)}, u32[]{:S(2)}, u32[]{:S(2)}) collective-permute-start(bf16[2,4,3,32,1024]{4,3,2,1,0:T(8,128)(2,1)S(1)} %pad_maximum_fusion.10), channel_id=1, source_target_pairs={{0,4},{1,5},{2,6},{3,7},{4,0},{5,1},{6,2},{7,3},{8,12},{9,13},{10,... | collective-permute-start | bytes 4718600 | tf_op jit(solution)/shard_map/ppermute | solution.py:70
  130.1 30.7 %collective-permute-start.23 = (bf16[2,4,2,32,1024]{4,3,2,1,0:T(8,128)(2,1)S(1)}, bf16[2,4,2,32,1024]{4,3,2,1,0:T(8,128)(2,1)S(1)}, u32[]{:S(2)}, u32[]{:S(2)}) collective-permute-start(bf16[2,4,2,32,1024]{4,3,2,1,0:T(8,128)(2,1)S(1)} %copy-done.21), channel_id=1, source_target_pairs={{0,1},{1,0},{2,3},{3,2},{4,5},{5,4},{6,7},{7,6},{8,9},{9,8},{10,11... | collective-permute-start | bytes 3145736 | tf_op jit(solution)/shard_map/ppermute | solution.py:70
  165.0 37.0 %collective-permute-start.28 = (bf16[512,1024]{1,0:T(8,128)(2,1)}, bf16[512,1024]{1,0:T(8,128)(2,1)}, u32[]{:S(2)}, u32[]{:S(2)}) collective-permute-start(bf16[512,1024]{1,0:T(8,128)(2,1)} %get-tuple-element.226), channel_id=1, source_target_pairs={{0,2},{1,3},{2,0},{3,1},{4,6},{5,7},{6,4},{7,5},{8,10},{9,11},{10,... | collective-permute-start | bytes 3145736 | tf_op jit(solution)/shard_map/ppermute | solution.py:70
  234.1 31.8 %collective-permute-start.33 = (bf16[4,2,64,1024]{3,2,1,0:T(8,128)(2,1)}, bf16[4,2,64,1024]{3,2,1,0:T(8,128)(2,1)}, u32[]{:S(2)}, u32[]{:S(2)}) collective-permute-start(bf16[4,2,64,1024]{3,2,1,0:T(8,128)(2,1)} %get-tuple-element.246), channel_id=1, source_target_pairs={{0,4},{1,5},{2,6},{3,7},{4,0},{5,1},{6,2},{7,3},{8,12},{9,13},{10,... | collective-permute-start | bytes 3145736 | tf_op jit(solution)/shard_map/ppermute | solution.py:70
  235.6 30.3 %collective-permute-start.32 = (bf16[4,2,64,1024]{3,2,1,0:T(8,128)(2,1)}, bf16[4,2,64,1024]{3,2,1,0:T(8,128)(2,1)}, u32[]{:S(2)}, u32[]{:S(2)}) collective-permute-start(bf16[4,2,64,1024]{3,2,1,0:T(8,128)(2,1)} %get-tuple-element.248), channel_id=1, source_target_pairs={{0,1},{1,0},{2,3},{3,2},{4,5},{5,4},{6,7},{7,6},{8,9},{9,8},{10,11... | collective-permute-start | bytes 3145736 | tf_op jit(solution)/shard_map/ppermute | solution.py:70
  288.5 26.3 %collective-permute-start.36 = (bf16[4,2,32,2048]{3,2,1,0:T(8,128)(2,1)}, bf16[4,2,32,2048]{3,2,1,0:T(8,128)(2,1)}, u32[]{:S(2)}, u32[]{:S(2)}) collective-permute-start(bf16[4,2,32,2048]{3,2,1,0:T(8,128)(2,1)} %get-tuple-element.237), channel_id=1, source_target_pairs={{0,1},{1,0},{2,3},{3,2},{4,5},{5,4},{6,7},{7,6},{8,9},{9,8},{10,11... | collective-permute-start | bytes 3145736 | tf_op jit(solution)/shard_map/ppermute | solution.py:70
  290.0 26.3 %collective-permute-start.34 = (bf16[4,2,32,2048]{3,2,1,0:T(8,128)(2,1)}, bf16[4,2,32,2048]{3,2,1,0:T(8,128)(2,1)}, u32[]{:S(2)}, u32[]{:S(2)}) collective-permute-start(bf16[4,2,32,2048]{3,2,1,0:T(8,128)(2,1)} %get-tuple-element.239), channel_id=1, source_target_pairs={{0,4},{1,5},{2,6},{3,7},{4,0},{5,1},{6,2},{7,3},{8,12},{9,13},{10,... | collective-permute-start | bytes 3145736 | tf_op jit(solution)/shard_map/ppermute | solution.py:70
  294.2 28.6 %collective-permute-start.31 = (f32[512,1024]{1,0:T(8,128)S(1)}, f32[512,1024]{1,0:T(8,128)S(1)}, u32[]{:S(2)}, u32[]{:S(2)}) collective-permute-start(f32[512,1024]{1,0:T(8,128)S(1)} %slice.261), channel_id=1, source_target_pairs={{0,2},{1,3},{2,0},{3,1},{4,6},{5,7},{6,4},{7,5},{8,10},{9,11},{10,... | collective-permute-start | bytes 6291464 | tf_op jit(solution)/shard_map/ppermute | solution.py:70
  295.8 38.8 %collective-permute-start.38 = (bf16[4,64,1024]{2,1,0:T(8,128)(2,1)S(1)}, bf16[4,64,1024]{2,1,0:T(8,128)(2,1)S(1)}, u32[]{:S(2)}, u32[]{:S(2)}) collective-permute-start(bf16[4,64,1024]{2,1,0:T(8,128)(2,1)S(1)} %get-tuple-element.269), channel_id=1, source_target_pairs={{0,1},{1,0},{2,3},{3,2},{4,5},{5,4},{6,7},{7,6},{8,9},{9,8},{10,11... | collective-permute-start | bytes 1572872 | tf_op jit(solution)/shard_map/ppermute | solution.py:70
  297.0 37.6 %collective-permute-start.37 = (bf16[4,64,1024]{2,1,0:T(8,128)(2,1)S(1)}, bf16[4,64,1024]{2,1,0:T(8,128)(2,1)S(1)}, u32[]{:S(2)}, u32[]{:S(2)}) collective-permute-start(bf16[4,64,1024]{2,1,0:T(8,128)(2,1)S(1)} %get-tuple-element.271), channel_id=1, source_target_pairs={{0,4},{1,5},{2,6},{3,7},{4,0},{5,1},{6,2},{7,3},{8,12},{9,13},{10,... | collective-permute-start | bytes 1572872 | tf_op jit(solution)/shard_map/ppermute | solution.py:70
  335.1 37.1 %collective-permute-start.43 = (bf16[128,1024]{1,0:T(8,128)(2,1)S(1)}, bf16[128,1024]{1,0:T(8,128)(2,1)}, u32[]{:S(2)}, u32[]{:S(2)}) collective-permute-start(bf16[128,1024]{1,0:T(8,128)(2,1)S(1)} %get-tuple-element.266), channel_id=1, source_target_pairs={{0,8},{1,9},{2,10},{3,11},{4,12},{5,13},{6,14},{7,15},{8,16},{9,17... | collective-permute-start | bytes 786440 | tf_op jit(solution)/shard_map/ppermute | solution.py:70
  341.3 30.9 %collective-permute-start.44 = (bf16[128,1024]{1,0:T(8,128)(2,1)S(1)}, bf16[128,1024]{1,0:T(8,128)(2,1)}, u32[]{:S(2)}, u32[]{:S(2)}) collective-permute-start(bf16[128,1024]{1,0:T(8,128)(2,1)S(1)} %get-tuple-element.267), channel_id=1, source_target_pairs={{0,16},{1,17},{2,18},{3,19},{4,20},{5,21},{6,22},{7,23},{8,24},{9,... | collective-permute-start | bytes 786440 | tf_op jit(solution)/shard_map/ppermute | solution.py:70
  345.3 25.3 %collective-permute-start.47 = (bf16[4,32,2048]{2,1,0:T(8,128)(2,1)S(1)}, bf16[4,32,2048]{2,1,0:T(8,128)(2,1)S(1)}, u32[]{:S(2)}, u32[]{:S(2)}) collective-permute-start(bf16[4,32,2048]{2,1,0:T(8,128)(2,1)S(1)} %get-tuple-element.257), channel_id=1, source_target_pairs={{0,4},{1,5},{2,6},{3,7},{4,0},{5,1},{6,2},{7,3},{8,12},{9,13},{10,... | collective-permute-start | bytes 1572872 | tf_op jit(solution)/shard_map/ppermute | solution.py:70
  346.0 26.2 %collective-permute-start.46 = (bf16[4,32,2048]{2,1,0:T(8,128)(2,1)S(1)}, bf16[4,32,2048]{2,1,0:T(8,128)(2,1)S(1)}, u32[]{:S(2)}, u32[]{:S(2)}) collective-permute-start(bf16[4,32,2048]{2,1,0:T(8,128)(2,1)S(1)} %get-tuple-element.259), channel_id=1, source_target_pairs={{0,1},{1,0},{2,3},{3,2},{4,5},{5,4},{6,7},{7,6},{8,9},{9,8},{10,11... | collective-permute-start | bytes 1572872 | tf_op jit(solution)/shard_map/ppermute | solution.py:70
  370.7 28.8 %collective-permute-start.51 = (bf16[4,2,32,1024]{3,2,1,0:T(8,128)(2,1)S(1)}, bf16[4,2,32,1024]{3,2,1,0:T(8,128)(2,1)S(1)}, u32[]{:S(2)}, u32[]{:S(2)}) collective-permute-start(bf16[4,2,32,1024]{3,2,1,0:T(8,128)(2,1)S(1)} %get-tuple-element.252), channel_id=1, source_target_pairs={{0,1},{1,0},{2,3},{3,2},{4,5},{5,4},{6,7},{7,6},{8,9},{9,8},{10,11... | collective-permute-start | bytes 1572872 | tf_op jit(solution)/shard_map/ppermute | solution.py:70
  372.6 25.9 %collective-permute-start.48 = (bf16[64,2048]{1,0:T(8,128)(2,1)S(1)}, bf16[64,2048]{1,0:T(8,128)(2,1)S(1)}, u32[]{:S(2)}, u32[]{:S(2)}) collective-permute-start(bf16[64,2048]{1,0:T(8,128)(2,1)S(1)} %get-tuple-element.254), channel_id=1, source_target_pairs={{0,8},{1,9},{2,10},{3,11},{4,12},{5,13},{6,14},{7,15},{8,16},{9,17... | collective-permute-start | bytes 786440 | tf_op jit(solution)/shard_map/ppermute | solution.py:70
  372.6 25.8 %collective-permute-start.49 = (bf16[64,2048]{1,0:T(8,128)(2,1)S(1)}, bf16[64,2048]{1,0:T(8,128)(2,1)S(1)}, u32[]{:S(2)}, u32[]{:S(2)}) collective-permute-start(bf16[64,2048]{1,0:T(8,128)(2,1)S(1)} %get-tuple-element.255), channel_id=1, source_target_pairs={{0,16},{1,17},{2,18},{3,19},{4,20},{5,21},{6,22},{7,23},{8,24},{9,... | collective-permute-start | bytes 786440 | tf_op jit(solution)/shard_map/ppermute | solution.py:70
  409.6 28.6 %collective-permute-start.52 = (bf16[2,512,1024]{2,1,0:T(8,128)(2,1)}, bf16[2,512,1024]{2,1,0:T(8,128)(2,1)}, u32[]{:S(2)}, u32[]{:S(2)}) collective-permute-start(bf16[2,512,1024]{2,1,0:T(8,128)(2,1)} %bitcast.183), channel_id=1, source_target_pairs={{0,2},{1,3},{2,0},{3,1},{4,6},{5,7},{6,4},{7,5},{8,10},{9,11},{10,... | collective-permute-start | bytes 6291464 | tf_op jit(solution)/shard_map/ppermute | solution.py:70
  453.2 26.5 %collective-permute-start.53 = (bf16[512,1024]{1,0:T(8,128)(2,1)}, bf16[512,1024]{1,0:T(8,128)(2,1)}, u32[]{:S(2)}, u32[]{:S(2)}) collective-permute-start(bf16[512,1024]{1,0:T(8,128)(2,1)} %fusion.20), channel_id=1, source_target_pairs={{0,1},{1,0},{2,3},{3,2},{4,5},{5,4},{6,7},{7,6},{8,9},{9,8},{10,11... | collective-permute-start | bytes 3145736 | tf_op jit(solution)/shard_map/ppermute | solution.py:70
  (156 other events, 1588.3 us)

commit v5 on v4

--- a/solution.py
+++ b/solution.py
@@ -370,7 +370,7 @@
     down_z = grid.arrivals(after(down_weight.reshape(2, long // 2, width), *up_first), "z")
     up_last = [grid.arrivals(after(part, *up_first), order[1]) for part, order in zip(up_first, orders)]
     down_first = [
-        grid.gather(jnp.concatenate([part[None, i : i + 1] for part in down_z]), order[0])
+        grid.arrivals(jnp.concatenate([part[None, i : i + 1] for part in down_z]), order[0])
         for i, order in enumerate(orders)
     ]
     attended_all, logsums = [], []
@@ -413,6 +413,9 @@
             index = (c - at["c"]) % c_n * s_n + (s - at["s"]) % s_n
             ordered.append(lax.dynamic_index_in_dim(stacked, index, 0, keepdims=False))
     attended = jnp.concatenate(ordered, axis=1)
+    down_first = [
+        jnp.concatenate([after(part, w_up, w_out)[None] for part in parts]) for parts in down_first
+    ]
     down_last = [grid.arrivals(after(part, *arrived), order[1]) for part, order in zip(down_first, orders)]
     attn_proj = dot(after(attended, w_up), w_out, (1, 0)) + b_out
     attn_proj = after(attn_proj, *down_first)

time: 512 us -> 502 us (0.980)
  waiting for transfers between devices: 103 us -> 96.5 us
    ppermute x73, waiting for transfers between devices: 82.8 us -> 75.2 us  [send(): return lax.ppermute(value, AXES, pairs)]
    unnamed x233 -> x235, local copies, waits for them, and re-layouts: 21.1 us -> 22 us
  transfers between devices with their start and end apart: 76 -> 76, of which waited for: 21 -> 20; matrix products, arithmetic and copies ran while one was open for 32% -> 32% of each run, Pallas kernels for 15% -> 15%
where the time goes in v5:
time: 502 us; the launch traced here: 494 us
  waiting for transfers between devices  96.5 us (19%)
  starting transfers between devices  95.5 us (19%)
  Pallas kernels  79.1 us (16%)
  matrix products  74.9 us (15%)
  local copies, waits for them, and re-layouts  74.2 us (15%)
  other arithmetic  70.4 us (14%)
    ppermute x73, starting transfers between devices, send(): return lax.ppermute(value, AXES, pairs)  84.1 us
    ppermute x73, waiting for transfers between devices, send(): return lax.ppermute(value, AXES, pairs)  75.2 us
    dot_general x13, matrix products, dot(): lax.dot_general(left, right, ((dims[:1], dims[1:]), ((), ())), preferred_...  72.3 us
    pallas_call x2, Pallas kernels, attend_back(): pl.pallas_call(partial(attend_back_kernel, width), grid=(1,), in_specs=[s...  36.7 us
    unnamed x235, local copies, waits for them, and re-layouts  22 us
    pallas_call x2, Pallas kernels, attend(): pl.pallas_call(partial(attend_kernel, width), grid=(1,), in_specs=[spec(3...  21.9 us
    pallas_call x4, Pallas kernels, place(): pl.pallas_call(partial(place_kernel, jobs, flat), out_shape=jax.ShapeDtyp...  18 us
    convert_element_type x12, other arithmetic, settle(): return sum((part.astype(F32) for part in parts)).astype(kind)  12.4 us
  transfers between devices with their start and end apart: 76, of which 20 were waited for; matrix products, arithmetic and copies ran while one was open for 32% of the time, Pallas kernels for 15%

profile of v5, /device:TPU:0, one launch (start us, length us, event | category | flops | bytes accessed | tf_op | source)
XLA Modules:
  0.0 494.2 jit_solution(5504807206624719585)
XLA Ops:
  22.5 4.7 all-to-all-start
  27.3 11.6 %all-to-all-done = bf16[32,2,640]{2,1,0:T(2,128)(2,1)S(1)} async-done(((bf16[32,2,640]{2,1,0:T(2,128)(2,1)}), bf16[32,2,640]{2,1,0:T(2,128)(2,1)S(1)}, u32[]{:S(2)}, u32[]{:S(2)}) %all-to-all-start) | async-done | bytes 81952 | tf_op jit(solution)/shard_map/all_to_all | solution.py:316
  49.7 4.2 all-to-all-start.1
  57.0 9.7 %all-to-all-done.1 = f32[32,1,3072]{2,1,0:T(1,128)} async-done(((f32[32,1,3072]{2,1,0:T(1,128)}), f32[32,1,3072]{2,1,0:T(1,128)}, u32[]{:S(2)}, u32[]{:S(2)}) %all-to-all-start.1) | async-done | bytes 393248 | tf_op jit(solution)/shard_map/all_to_all | solution.py:331
  80.0 20.5 %collective-permute-done.12 = bf16[5,32,1024]{2,1,0:T(8,128)(2,1)S(1)} collective-permute-done((bf16[5,32,1024]{2,1,0:T(8,128)(2,1)}, bf16[5,32,1024]{2,1,0:T(8,128)(2,1)S(1)}, u32[]{:S(2)}, u32[]{:S(2)}) %collective-permute-start.12) | collective-permute-done | bytes 327712 | tf_op jit(solution)/shard_map/ppermute | solution.py:70
  107.1 7.3 %add_convert_fusion = bf16[2048,768]{1,0:T(8,128)(2,1)} fusion(bf16[1024,768]{1,0:T(8,128)(2,1)} %shard_map.228, f32[768]{0:T(1024)S(1)} %pad_maximum_fusion.26, bf16[1024,1024]{1,0:T(8,128)(2,1)} %collective-permute-done.8, bf16[1024,1024]{1,0:T(8,128)(2,1)S(1)} %fusion.10), kind=kOutput, calls=%fused_computation.13 | convolution fusion | flops 3232759808 | bytes 8915968 | tf_op jit(solution)/shard_map/dot_general | solution.py:22
  128.5 10.7 %shard_map.229 = (bf16[1,1024,256]{2,1,0:T(8,128)(2,1)}, f32[1,1024,256]{2,1,0:T(8,128)}) custom-call(bf16[2,1024,768]{2,1,0:T(8,128)(2,1)} %bitcast.404), custom_call_target="tpu_custom_call" | custom-call | flops 268435456 | bytes 3145728 | tf_op jit(solution)/shard_map/pallas_call | solution.py:203
  144.9 11.2 %shard_map.230 = (bf16[1,1024,256]{2,1,0:T(8,128)(2,1)}, f32[1,1024,256]{2,1,0:T(8,128)}) custom-call(bf16[2,1024,768]{2,1,0:T(8,128)(2,1)} %bitcast.405), custom_call_target="tpu_custom_call" | custom-call | flops 268435456 | bytes 3145728 | tf_op jit(solution)/shard_map/pallas_call | solution.py:203
  170.5 5.5 %shard_map.231 = bf16[1024,2048]{1,0:T(8,128)(2,1)} custom-call(s32[64]{0:T(128)} %stack.364.table, bf16[8,3,32,1024]{3,2,1,0:T(8,128)(2,1)} %bitcast.418, bf16[8,3,32,1024]{3,2,1,0:T(8,128)(2,1)} %bitcast.83.refs_1_, bf16[8,2,32,1024]{3,2,1,0:T(8,128)(2,1)} %bitcast.425, bf16[8,2,32,1024]{3,2,1,0:T(8,128)(2,1)} %bitcast.436), custom_call_target="tpu_custom_call" | custom-call | bytes 8388608 | tf_op jit(solution)/shard_map/pallas_call | solution.py:123
  196.2 10.0 %multiply_convert_fusion = (bf16[1024,2048]{1,0:T(8,128)(2,1)S(1)}, f32[1024,2048]{1,0:T(8,128)}) fusion(f32[2048]{0:T(1024)S(1)} %bitcast.504, bf16[1024,2048]{1,0:T(8,128)(2,1)S(1)} %copy-done.17, bf16[512,1024]{1,0:T(8,128)(2,1)} %collective-permute-done.27, bf16[512,1024]{1,0:T(8,128)(2,1)} %add_convert_fusion.7), kind=kOutput, calls=%fused_computation.10 | convolution fusion | flops 4320133120 | bytes 18882560 | tf_op jit(solution)/shard_map/dot_general | solution.py:22
  206.3 7.9 %convolution_convert_fusion.1 = bf16[2048,1024]{1,0:T(8,128)(2,1)S(1)} fusion(bf16[1024,2048]{1,0:T(8,128)(2,1)S(1)} %get-tuple-element.149, bf16[512,1024]{1,0:T(8,128)(2,1)} %collective-permute-done.28, bf16[512,1024]{1,0:T(8,128)(2,1)} %get-tuple-element.234), kind=kOutput, calls=%fused_computation.27 | convolution fusion | flops 4301258752 | bytes 10485760 | tf_op jit(solution)/shard_map/dot_general | solution.py:22
  214.2 5.9 %collective-permute-done.30 = bf16[2,4,1,64,1024]{4,3,1,0,2:T(8,128)(2,1)S(1)} collective-permute-done((bf16[2,4,1,64,1024]{4,3,1,0,2:T(8,128)(2,1)}, bf16[2,4,1,64,1024]{4,3,1,0,2:T(8,128)(2,1)S(1)}, u32[]{:S(2)}, u32[]{:S(2)}) %collective-permute-start.30) | collective-permute-done | bytes 1048608 | tf_op jit(solution)/shard_map/ppermute | solution.py:70
  226.0 5.2 %shard_map.233 = bf16[2048,1024]{1,0:T(8,128)(2,1)} custom-call(s32[32]{0:T(128)} %stack.398.table, bf16[8,1,64,1024]{3,2,1,0:T(8,128)(2,1)} %bitcast.424, bf16[8,1,64,1024]{3,2,1,0:T(8,128)(2,1)} %bitcast.438, bf16[8,1,64,1024]{3,2,1,0:T(8,128)(2,1)} %bitcast.423, bf16[8,1,64,1024]{3,2,1,0:T(8,128)(2,1)} %bitcast.437), custom_call_target="tpu_custom_call" | custom-call | bytes 8388608 | tf_op jit(solution)/shard_map/pallas_call | solution.py:123
  231.2 10.0 %fusion.78 = f32[1024,1024]{1,0:T(8,128)} fusion(bf16[1024,2048]{1,0:T(8,128)(2,1)} %copy-done.102, bf16[2048,1024]{1,0:T(8,128)(2,1)} %shard_map.233), kind=kOutput, calls=%fused_computation.303 | convolution fusion | flops 4294967296 | bytes 12582912 | tf_op jit(solution)/shard_map/dot_general | solution.py:22
  241.3 12.8 %convert_reduce_fusion = (f32[2048]{0:T(1024)}, bf16[1024,2048]{1,0:T(8,128)(2,1)S(1)}) fusion(f32[1024,2048]{1,0:T(8,128)} %get-tuple-element.345, f32[2048]{0:T(1024)S(1)} %bitcast.505, bf16[1024,1024]{1,0:T(8,128)(2,1)S(1)} %pad_maximum_fusion.6, bf16[2048,1024]{1,0:T(8,128)(2,1)S(1)} %copy-done.25), kind=kOutput, calls=%fused_computation.9 | convolution fusion | flops 4343199744 | bytes 18890752 | tf_op jit(solution)/shard_map/dot_general | solution.py:22
  261.2 4.8 convolution_convert_fusion
  270.6 4.5 fusion.79
  288.5 16.1 %collective-permute-done.36 = bf16[4,2,32,2048]{3,2,1,0:T(8,128)(2,1)} collective-permute-done((bf16[4,2,32,2048]{3,2,1,0:T(8,128)(2,1)}, bf16[4,2,32,2048]{3,2,1,0:T(8,128)(2,1)}, u32[]{:S(2)}, u32[]{:S(2)}) %collective-permute-start.36) | collective-permute-done | bytes 1048608 | tf_op jit(solution)/shard_map/ppermute | solution.py:70
  325.0 6.3 %collective-permute-start.43 = (bf16[128,1024]{1,0:T(8,128)(2,1)S(1)}, bf16[128,1024]{1,0:T(8,128)(2,1)}, u32[]{:S(2)}, u32[]{:S(2)}) collective-permute-start(bf16[128,1024]{1,0:T(8,128)(2,1)S(1)} %get-tuple-element.274), channel_id=1, source_target_pairs={{0,8},{1,9},{2,10},{3,11},{4,12},{5,13},{6,14},{7,15},{8,16},{9,17... | collective-permute-start | bytes 786440 | tf_op jit(solution)/shard_map/ppermute | solution.py:70
  343.4 18.4 %shard_map.234 = bf16[1,1024,768]{2,1,0:T(8,128)(2,1)} custom-call(bf16[2,1024,768]{2,1,0:T(8,128)(2,1)} %bitcast.406, bf16[1,1024,256]{2,1,0:T(8,128)(2,1)} %maximum_bitcast_fusion.grads, f32[1,1024,256]{2,1,0:T(8,128)} %get-tuple-element.173.logsum), custom_call_target="tpu_custom_call" | custom-call | flops 536870912 | bytes 4718592 | tf_op jit(solution)/shard_map/pallas_call | solution.py:257
  369.6 18.3 %shard_map.235 = bf16[1,1024,768]{2,1,0:T(8,128)(2,1)} custom-call(bf16[2,1024,768]{2,1,0:T(8,128)(2,1)} %bitcast.407, bf16[1,1024,256]{2,1,0:T(8,128)(2,1)} %maximum_bitcast_fusion.1.grads, f32[1,1024,256]{2,1,0:T(8,128)} %get-tuple-element.185.logsum), custom_call_target="tpu_custom_call" | custom-call | flops 536870912 | bytes 4718592 | tf_op jit(solution)/shard_map/pallas_call | solution.py:257
  405.9 5.9 %fusion.18 = bf16[1024,768]{1,0:T(8,128)(2,1)S(1)} fusion(bf16[2048,768]{1,0:T(8,128)(2,1)S(1)} %bitcast.416, bf16[1024,1024]{1,0:T(8,128)(2,1)} %collective-permute-done.8, bf16[1024,1024]{1,0:T(8,128)(2,1)} %copy-done.30), kind=kOutput, calls=%fused_computation.68 | convolution fusion | flops 3230400512 | bytes 8912896 | tf_op jit(solution)/shard_map/dot_general | solution.py:22
  429.4 4.7 multiply_reduce_fusion
  449.7 4.9 collective-permute-done.63
  (574 shorter events, 269.4 us)
Async XLA Ops:
  6.5 34.5 %collective-permute-start.3 = (bf16[512,1024]{1,0:T(8,128)(2,1)}, bf16[512,1024]{1,0:T(8,128)(2,1)S(1)}, u32[]{:S(2)}, u32[]{:S(2)}) collective-permute-start(bf16[512,1024]{1,0:T(8,128)(2,1)} %bitcast.408), channel_id=1, source_target_pairs={{0,1},{1,0},{2,3},{3,2},{4,5},{5,4},{6,7},{7,6},{8,9},{9,8},{10,11... | collective-permute-start | bytes 3145736 | tf_op jit(solution)/shard_map/ppermute | solution.py:70
  71.5 29.0 %collective-permute-start.12 = (bf16[5,32,1024]{2,1,0:T(8,128)(2,1)}, bf16[5,32,1024]{2,1,0:T(8,128)(2,1)S(1)}, u32[]{:S(2)}, u32[]{:S(2)}) collective-permute-start(bf16[5,32,1024]{2,1,0:T(8,128)(2,1)} %fusion.38), channel_id=1, source_target_pairs={{0,16},{1,17},{2,18},{3,19},{4,20},{5,21},{6,22},{7,23},{8,24},{9,... | collective-permute-start | bytes 983048 | tf_op jit(solution)/shard_map/ppermute | solution.py:70
  72.3 28.2 %collective-permute-start.11 = (bf16[5,32,1024]{2,1,0:T(8,128)(2,1)}, bf16[5,32,1024]{2,1,0:T(8,128)(2,1)S(1)}, u32[]{:S(2)}, u32[]{:S(2)}) collective-permute-start(bf16[5,32,1024]{2,1,0:T(8,128)(2,1)} %fusion.38), channel_id=1, source_target_pairs={{0,8},{1,9},{2,10},{3,11},{4,12},{5,13},{6,14},{7,15},{8,16},{9,17... | collective-permute-start | bytes 983048 | tf_op jit(solution)/shard_map/ppermute | solution.py:70
  75.2 31.9 %collective-permute-start.8 = (bf16[1024,1024]{1,0:T(8,128)(2,1)S(1)}, bf16[1024,1024]{1,0:T(8,128)(2,1)}, u32[]{:S(2)}, u32[]{:S(2)}) collective-permute-start(bf16[1024,1024]{1,0:T(8,128)(2,1)S(1)} %fusion.10), channel_id=1, source_target_pairs={{0,2},{1,3},{2,0},{3,1},{4,6},{5,7},{6,4},{7,5},{8,10},{9,11},{10,... | collective-permute-start | bytes 6291464 | tf_op jit(solution)/shard_map/ppermute | solution.py:70
  75.3 27.3 %collective-permute-start.9 = (bf16[4,4,32,768]{3,2,1,0:T(8,128)(2,1)S(1)}, bf16[4,4,32,768]{3,2,1,0:T(8,128)(2,1)S(1)}, u32[]{:S(2)}, u32[]{:S(2)}) collective-permute-start(bf16[4,4,32,768]{3,2,1,0:T(8,128)(2,1)S(1)} %pad_maximum_fusion.18), channel_id=1, source_target_pairs={{0,4},{1,5},{2,6},{3,7},{4,0},{5,1},{6,2},{7,3},{8,12},{9,13},{10,... | collective-permute-start | bytes 2359304 | tf_op jit(solution)/shard_map/ppermute | solution.py:70
  121.4 37.5 %collective-permute-start.22 = (bf16[2,4,3,32,1024]{4,3,2,1,0:T(8,128)(2,1)S(1)}, bf16[2,4,3,32,1024]{4,3,2,1,0:T(8,128)(2,1)}, u32[]{:S(2)}, u32[]{:S(2)}) collective-permute-start(bf16[2,4,3,32,1024]{4,3,2,1,0:T(8,128)(2,1)S(1)} %pad_maximum_fusion.10), channel_id=1, source_target_pairs={{0,4},{1,5},{2,6},{3,7},{4,0},{5,1},{6,2},{7,3},{8,12},{9,13},{10,... | collective-permute-start | bytes 4718600 | tf_op jit(solution)/shard_map/ppermute | solution.py:70
  126.9 30.9 %collective-permute-start.23 = (bf16[2,4,2,32,1024]{4,3,2,1,0:T(8,128)(2,1)}, bf16[2,4,2,32,1024]{4,3,2,1,0:T(8,128)(2,1)S(1)}, u32[]{:S(2)}, u32[]{:S(2)}) collective-permute-start(bf16[2,4,2,32,1024]{4,3,2,1,0:T(8,128)(2,1)} %pad_maximum_fusion.11), channel_id=1, source_target_pairs={{0,1},{1,0},{2,3},{3,2},{4,5},{5,4},{6,7},{7,6},{8,9},{9,8},{10,11... | collective-permute-start | bytes 3145736 | tf_op jit(solution)/shard_map/ppermute | solution.py:70
  143.3 37.5 %collective-permute-start.26 = (bf16[4,1,64,1024]{3,2,0,1:T(8,128)(2,1)S(1)}, bf16[4,1,64,1024]{3,2,0,1:T(8,128)(2,1)}, u32[]{:S(2)}, u32[]{:S(2)}) collective-permute-start(bf16[4,1,64,1024]{3,2,0,1:T(8,128)(2,1)S(1)} %pad_maximum_fusion.22), channel_id=1, source_target_pairs={{0,4},{1,5},{2,6},{3,7},{4,0},{5,1},{6,2},{7,3},{8,12},{9,13},{10,... | collective-permute-start | bytes 1572872 | tf_op jit(solution)/shard_map/ppermute | solution.py:70
  166.3 26.2 %collective-permute-start.28 = (bf16[512,1024]{1,0:T(8,128)(2,1)}, bf16[512,1024]{1,0:T(8,128)(2,1)}, u32[]{:S(2)}, u32[]{:S(2)}) collective-permute-start(bf16[512,1024]{1,0:T(8,128)(2,1)} %get-tuple-element.234), channel_id=1, source_target_pairs={{0,2},{1,3},{2,0},{3,1},{4,6},{5,7},{6,4},{7,5},{8,10},{9,11},{10,... | collective-permute-start | bytes 3145736 | tf_op jit(solution)/shard_map/ppermute | solution.py:70
  225.3 30.5 %collective-permute-start.33 = (bf16[4,2,64,1024]{3,2,1,0:T(8,128)(2,1)}, bf16[4,2,64,1024]{3,2,1,0:T(8,128)(2,1)}, u32[]{:S(2)}, u32[]{:S(2)}) collective-permute-start(bf16[4,2,64,1024]{3,2,1,0:T(8,128)(2,1)} %get-tuple-element.254), channel_id=1, source_target_pairs={{0,4},{1,5},{2,6},{3,7},{4,0},{5,1},{6,2},{7,3},{8,12},{9,13},{10,... | collective-permute-start | bytes 3145736 | tf_op jit(solution)/shard_map/ppermute | solution.py:70
  225.6 30.2 %collective-permute-start.32 = (bf16[4,2,64,1024]{3,2,1,0:T(8,128)(2,1)}, bf16[4,2,64,1024]{3,2,1,0:T(8,128)(2,1)}, u32[]{:S(2)}, u32[]{:S(2)}) collective-permute-start(bf16[4,2,64,1024]{3,2,1,0:T(8,128)(2,1)} %get-tuple-element.256), channel_id=1, source_target_pairs={{0,1},{1,0},{2,3},{3,2},{4,5},{5,4},{6,7},{7,6},{8,9},{9,8},{10,11... | collective-permute-start | bytes 3145736 | tf_op jit(solution)/shard_map/ppermute | solution.py:70
  278.3 26.3 %collective-permute-start.36 = (bf16[4,2,32,2048]{3,2,1,0:T(8,128)(2,1)}, bf16[4,2,32,2048]{3,2,1,0:T(8,128)(2,1)}, u32[]{:S(2)}, u32[]{:S(2)}) collective-permute-start(bf16[4,2,32,2048]{3,2,1,0:T(8,128)(2,1)} %get-tuple-element.245), channel_id=1, source_target_pairs={{0,1},{1,0},{2,3},{3,2},{4,5},{5,4},{6,7},{7,6},{8,9},{9,8},{10,11... | collective-permute-start | bytes 3145736 | tf_op jit(solution)/shard_map/ppermute | solution.py:70
  279.9 26.3 %collective-permute-start.34 = (bf16[4,2,32,2048]{3,2,1,0:T(8,128)(2,1)}, bf16[4,2,32,2048]{3,2,1,0:T(8,128)(2,1)}, u32[]{:S(2)}, u32[]{:S(2)}) collective-permute-start(bf16[4,2,32,2048]{3,2,1,0:T(8,128)(2,1)} %get-tuple-element.247), channel_id=1, source_target_pairs={{0,4},{1,5},{2,6},{3,7},{4,0},{5,1},{6,2},{7,3},{8,12},{9,13},{10,... | collective-permute-start | bytes 3145736 | tf_op jit(solution)/shard_map/ppermute | solution.py:70
  285.4 27.3 %collective-permute-start.31 = (f32[512,1024]{1,0:T(8,128)S(1)}, f32[512,1024]{1,0:T(8,128)S(1)}, u32[]{:S(2)}, u32[]{:S(2)}) collective-permute-start(f32[512,1024]{1,0:T(8,128)S(1)} %slice.261), channel_id=1, source_target_pairs={{0,2},{1,3},{2,0},{3,1},{4,6},{5,7},{6,4},{7,5},{8,10},{9,11},{10,... | collective-permute-start | bytes 6291464 | tf_op jit(solution)/shard_map/ppermute | solution.py:70
  287.0 37.5 %collective-permute-start.38 = (bf16[4,64,1024]{2,1,0:T(8,128)(2,1)S(1)}, bf16[4,64,1024]{2,1,0:T(8,128)(2,1)S(1)}, u32[]{:S(2)}, u32[]{:S(2)}) collective-permute-start(bf16[4,64,1024]{2,1,0:T(8,128)(2,1)S(1)} %get-tuple-element.277), channel_id=1, source_target_pairs={{0,1},{1,0},{2,3},{3,2},{4,5},{5,4},{6,7},{7,6},{8,9},{9,8},{10,11... | collective-permute-start | bytes 1572872 | tf_op jit(solution)/shard_map/ppermute | solution.py:70
  288.2 36.3 %collective-permute-start.37 = (bf16[4,64,1024]{2,1,0:T(8,128)(2,1)S(1)}, bf16[4,64,1024]{2,1,0:T(8,128)(2,1)S(1)}, u32[]{:S(2)}, u32[]{:S(2)}) collective-permute-start(bf16[4,64,1024]{2,1,0:T(8,128)(2,1)S(1)} %get-tuple-element.279), channel_id=1, source_target_pairs={{0,4},{1,5},{2,6},{3,7},{4,0},{5,1},{6,2},{7,3},{8,12},{9,13},{10,... | collective-permute-start | bytes 1572872 | tf_op jit(solution)/shard_map/ppermute | solution.py:70
  325.0 38.3 %collective-permute-start.43 = (bf16[128,1024]{1,0:T(8,128)(2,1)S(1)}, bf16[128,1024]{1,0:T(8,128)(2,1)}, u32[]{:S(2)}, u32[]{:S(2)}) collective-permute-start(bf16[128,1024]{1,0:T(8,128)(2,1)S(1)} %get-tuple-element.274), channel_id=1, source_target_pairs={{0,8},{1,9},{2,10},{3,11},{4,12},{5,13},{6,14},{7,15},{8,16},{9,17... | collective-permute-start | bytes 786440 | tf_op jit(solution)/shard_map/ppermute | solution.py:70
  331.3 32.0 %collective-permute-start.44 = (bf16[128,1024]{1,0:T(8,128)(2,1)S(1)}, bf16[128,1024]{1,0:T(8,128)(2,1)}, u32[]{:S(2)}, u32[]{:S(2)}) collective-permute-start(bf16[128,1024]{1,0:T(8,128)(2,1)S(1)} %get-tuple-element.275), channel_id=1, source_target_pairs={{0,16},{1,17},{2,18},{3,19},{4,20},{5,21},{6,22},{7,23},{8,24},{9,... | collective-permute-start | bytes 786440 | tf_op jit(solution)/shard_map/ppermute | solution.py:70
  335.2 26.5 %collective-permute-start.47 = (bf16[4,32,2048]{2,1,0:T(8,128)(2,1)S(1)}, bf16[4,32,2048]{2,1,0:T(8,128)(2,1)S(1)}, u32[]{:S(2)}, u32[]{:S(2)}) collective-permute-start(bf16[4,32,2048]{2,1,0:T(8,128)(2,1)S(1)} %get-tuple-element.265), channel_id=1, source_target_pairs={{0,4},{1,5},{2,6},{3,7},{4,0},{5,1},{6,2},{7,3},{8,12},{9,13},{10,... | collective-permute-start | bytes 1572872 | tf_op jit(solution)/shard_map/ppermute | solution.py:70
  336.9 26.4 %collective-permute-start.46 = (bf16[4,32,2048]{2,1,0:T(8,128)(2,1)S(1)}, bf16[4,32,2048]{2,1,0:T(8,128)(2,1)S(1)}, u32[]{:S(2)}, u32[]{:S(2)}) collective-permute-start(bf16[4,32,2048]{2,1,0:T(8,128)(2,1)S(1)} %get-tuple-element.267), channel_id=1, source_target_pairs={{0,1},{1,0},{2,3},{3,2},{4,5},{5,4},{6,7},{7,6},{8,9},{9,8},{10,11... | collective-permute-start | bytes 1572872 | tf_op jit(solution)/shard_map/ppermute | solution.py:70
  361.8 28.8 %collective-permute-start.51 = (bf16[4,2,32,1024]{3,2,1,0:T(8,128)(2,1)S(1)}, bf16[4,2,32,1024]{3,2,1,0:T(8,128)(2,1)S(1)}, u32[]{:S(2)}, u32[]{:S(2)}) collective-permute-start(bf16[4,2,32,1024]{3,2,1,0:T(8,128)(2,1)S(1)} %get-tuple-element.260), channel_id=1, source_target_pairs={{0,1},{1,0},{2,3},{3,2},{4,5},{5,4},{6,7},{7,6},{8,9},{9,8},{10,11... | collective-permute-start | bytes 1572872 | tf_op jit(solution)/shard_map/ppermute | solution.py:70
  363.7 25.9 %collective-permute-start.48 = (bf16[64,2048]{1,0:T(8,128)(2,1)S(1)}, bf16[64,2048]{1,0:T(8,128)(2,1)S(1)}, u32[]{:S(2)}, u32[]{:S(2)}) collective-permute-start(bf16[64,2048]{1,0:T(8,128)(2,1)S(1)} %get-tuple-element.262), channel_id=1, source_target_pairs={{0,8},{1,9},{2,10},{3,11},{4,12},{5,13},{6,14},{7,15},{8,16},{9,17... | collective-permute-start | bytes 786440 | tf_op jit(solution)/shard_map/ppermute | solution.py:70
  400.7 28.6 %collective-permute-start.52 = (bf16[2,512,1024]{2,1,0:T(8,128)(2,1)}, bf16[2,512,1024]{2,1,0:T(8,128)(2,1)}, u32[]{:S(2)}, u32[]{:S(2)}) collective-permute-start(bf16[2,512,1024]{2,1,0:T(8,128)(2,1)} %bitcast.184), channel_id=1, source_target_pairs={{0,2},{1,3},{2,0},{3,1},{4,6},{5,7},{6,4},{7,5},{8,10},{9,11},{10,... | collective-permute-start | bytes 6291464 | tf_op jit(solution)/shard_map/ppermute | solution.py:70
  444.3 26.5 %collective-permute-start.53 = (bf16[512,1024]{1,0:T(8,128)(2,1)}, bf16[512,1024]{1,0:T(8,128)(2,1)}, u32[]{:S(2)}, u32[]{:S(2)}) collective-permute-start(bf16[512,1024]{1,0:T(8,128)(2,1)} %fusion.20), channel_id=1, source_target_pairs={{0,1},{1,0},{2,3},{3,2},{4,5},{5,4},{6,7},{7,6},{8,9},{9,8},{10,11... | collective-permute-start | bytes 3145736 | tf_op jit(solution)/shard_map/ppermute | solution.py:70
  (157 other events, 1513.2 us)
